TPU v7x, 512 devices: a whole 4x8x8 slice. The times are simulated.
512 devices in a mesh: row: 16 (over x_lo, z), col: 32 (over y, x_hi, core).
Axes of the slice: x: 4 (x_hi: 2, x_lo: 2; x = x_hi * 2 + x_lo), y: 8, z: 8, core: 2. Of those that a mesh axis runs over, the one named last changes fastest.
Arguments:
- features: bfloat16 [65536, 256], P(('col', 'row')), may hold values from -6 to 6
- weight: bfloat16 [256, 256], replicated, may hold values from -0.375 to 0.375
- block_values: bfloat16 [16, 32, 96, 128, 128], P('row', 'col'), may hold values from -0.09375 to 0.09375
- block_rows: int32 [16, 32, 96], P('row', 'col'), may hold values from 0 to 31, as said below
- block_cols: int32 [16, 32, 96], P('row', 'col'), may hold values from 0 to 15, as said below
- counts: int32 [16, 32], P('row', 'col'), may hold values from 12 to 96, as said below
- cotangent: bfloat16 [65536, 256], P(('row', 'col')), may hold values from -24 to 24
Outputs:
- activations: bfloat16 [65536, 256], P(('row', 'col'))
- feature_grad: bfloat16 [65536, 256], P(('col', 'row'))
- weight_grad: float32 [256, 256], replicated
Inputs may be any that keep to these rules, and one draw needn't show every extreme that they name: block_rows and block_cols give each slot's block position within its tile; the 96 positions of one tile are all distinct. `block_cols`: see block_rows. `counts`: slots at and past a tile's count are not part of A. Tile (i, j) is full (96 live slots) exactly where j modulo 16 equals i; other tiles hold at most 48.
All inputs are finite; a program needn't handle non-finite values.
Results may differ from a plain program's by a relative error of at most 0.03.
Values may be sent and summed in bfloat16 or wider, within the bound.
No kernel may reach another device: no remote copies, remote signals or barrier semaphores. Data moves between devices by JAX's collectives and lax.ppermute only.
A program may use at most 64 MiB of HBM per device.

v0:
```python
import math

import jax
import jax.numpy as jnp
from jax import lax
from jax.sharding import PartitionSpec as P

group_slots = 8


def gelu_tanh(value):
    return jax.nn.gelu(value, approximate=True)


def tile_product(tiles, source_ids, target_ids, count, panel, flipped, target_blocks):
    block = tiles.shape[-1]
    width = panel.shape[-1]

    def advance(turn, total):
        first = turn * group_slots
        chosen = lax.dynamic_slice_in_dim(tiles, first, group_slots, 0)
        sources = lax.dynamic_slice_in_dim(source_ids, first, group_slots, 0)
        targets = lax.dynamic_slice_in_dim(target_ids, first, group_slots, 0)
        pieces = jnp.take(panel, sources, axis=0)
        if flipped:
            product = jnp.einsum("gba,gbf->gaf", chosen, pieces, preferred_element_type=jnp.float32)
        else:
            product = jnp.einsum("gab,gbf->gaf", chosen, pieces, preferred_element_type=jnp.float32)
        alive_mask = first + jnp.arange(group_slots) < count
        product = jnp.where(alive_mask[:, None, None], product, 0.0)
        return total.at[targets].add(product)

    trips = (count + group_slots - 1) // group_slots
    start_total = jnp.zeros((target_blocks, block, width), jnp.float32)
    total = lax.fori_loop(0, trips, advance, start_total)
    return total.reshape(target_blocks * block, width)


def local(features, weight, block_values, block_rows, block_cols, counts, cotangent):
    rows_dev, width = features.shape
    block = block_values.shape[-1]
    row_count = lax.axis_size("row")
    col_count = lax.axis_size("col")
    node_total = rows_dev * row_count * col_count
    tile_brows = rows_dev * col_count // block
    tile_bcols = rows_dev * row_count // block
    tiles = block_values[0, 0]
    rows_ids = block_rows[0, 0]
    cols_ids = block_cols[0, 0]
    count = counts[0, 0]
    panel = lax.all_gather(features, "row", axis=0, tiled=True)
    partial_value = tile_product(
        tiles, cols_ids, rows_ids, count, panel.reshape(tile_bcols, block, width), False, tile_brows
    ).astype(jnp.bfloat16)
    aggregated = (
        lax.psum_scatter(partial_value, "col", scatter_dimension=0, tiled=True)
        .astype(jnp.float32)
        .astype(jnp.bfloat16)
    )
    preact = jnp.dot(aggregated, weight, preferred_element_type=jnp.float32)
    activations = gelu_tanh(preact).astype(jnp.bfloat16)
    _, pullback = jax.vjp(gelu_tanh, preact)
    grad_pre = pullback(cotangent.astype(jnp.float32))[0].astype(jnp.bfloat16)
    weight_term = lax.dot_general(
        aggregated, grad_pre, (((0,), (0,)), ((), ())), preferred_element_type=jnp.float32
    )
    weight_grad = lax.psum(weight_term, ("row", "col")) * (1.0 / math.sqrt(node_total))
    grad_agg = lax.dot_general(
        grad_pre, weight, (((1,), (1,)), ((), ())), preferred_element_type=jnp.float32
    ).astype(jnp.bfloat16)
    grad_rows = lax.all_gather(grad_agg, "col", axis=0, tiled=True)
    back_partial = tile_product(
        tiles,
        rows_ids,
        cols_ids,
        count,
        grad_rows.reshape(tile_brows, block, width),
        True,
        tile_bcols,
    ).astype(jnp.bfloat16)
    feature_grad = (
        lax.psum_scatter(back_partial, "row", scatter_dimension=0, tiled=True)
        .astype(jnp.float32)
        .astype(jnp.bfloat16)
    )
    return (activations, feature_grad, weight_grad)


def solution(mesh):
    in_specs = (
        P(("col", "row"), None),
        P(),
        P("row", "col", None, None, None),
        P("row", "col", None),
        P("row", "col", None),
        P("row", "col"),
        P(("row", "col"), None),
    )
    out_specs = (P(("row", "col"), None), P(("col", "row"), None), P())
    return jax.shard_map(local, mesh=mesh, in_specs=in_specs, out_specs=out_specs, check_vma=False)
```

profile of v0, /device:TPU:8, one launch (start us, length us, event | category | flops | bytes accessed | tf_op | source)
XLA Modules:
  0.0 728.6 jit_solution(16123546076326498032)
XLA Ops:
  8.6 78.6 %all-gather.3.cloned.1.call-done = bf16[2048,256]{1,0:T(8,128)(2,1)} async-done(((bf16[128,256]{1,0:T(8,128)(2,1)}), bf16[2048,256]{1,0:T(8,128)(2,1)}) %all-gather.3.cloned.1.call-update) | async-done | bytes 1048592 | tf_op jit(solution)/shard_map/all_gather | solution.py:51
  87.3 2.4 broadcast_in_dim.58
  89.7 36.2 %while.20 = (s32[]{:T(128)}, f32[32,128,256]{2,1,0:T(8,128)}, s32[]{:T(128)}, s32[96]{0:T(128)S(1)}, s32[]{:T(128)}, /*index=5*/bf16[96,128,128]{2,1,0:T(8,128)(...) while((s32[]{:T(128)}, f32[32,128,256]{2,1,0:T(8,128)}, ...), condition=%wide.region_2.3_spmd, body=%wide.region_0.2_spmd.sunk | while | flops 67896416 | bytes 6033855 | solution.py:35
  92.5 3.2 scatter_fusion
  98.5 3.3 scatter_fusion
  104.5 3.4 scatter_fusion
  110.6 3.3 scatter_fusion
  116.6 3.3 scatter_fusion
  122.6 3.3 scatter_fusion
  125.9 3.8 convert_element_type.28
  129.9 157.7 %reduce-scatter.3.cloned.1.call-done = bf16[128,256]{1,0:T(8,128)(2,1)} async-done(((bf16[4096,256]{1,0:T(8,128)(2,1)}), bf16[128,256]{1,0:T(8,128)(2,1)}) %reduce-scatter.3.cloned.1.call-update) | async-done | bytes 65552 | tf_op jit(solution)/shard_map/reduce_scatter | solution.py:56
  287.5 1.7 fusion.14
  290.2 2.8 copy.10
  294.0 82.1 %all-gather.5.cloned.1.call-done = bf16[4096,256]{1,0:T(8,128)(2,1)} async-done(((bf16[128,256]{1,0:T(8,128)(2,1)}), bf16[4096,256]{1,0:T(8,128)(2,1)}) %all-gather.5.cloned.1.call-update) | async-done | bytes 2097168 | tf_op jit(solution)/shard_map/all_gather | solution.py:71
  376.0 1.6 broadcast_in_dim.59
  377.6 45.9 %while.21 = (s32[]{:T(128)}, f32[16,128,256]{2,1,0:T(8,128)}, s32[]{:T(128)}, s32[96]{0:T(128)S(1)}, s32[]{:T(128)}, /*index=5*/bf16[96,128,128]{1,2,0:T(8,128)(...) while((s32[]{:T(128)}, f32[16,128,256]{2,1,0:T(8,128)}, ...), condition=%wide.region_6.7_spmd, body=%wide.region_4.6_spmd.sunk | while | flops 67896416 | bytes 6033855 | solution.py:35
  378.4 2.2 gather_fusion.1
  381.9 3.3 scatter_fusion.1
  386.1 2.2 gather_fusion.1
  389.6 3.3 scatter_fusion.1
  393.7 2.2 gather_fusion.1
  397.2 3.3 scatter_fusion.1
  401.3 2.2 gather_fusion.1
  404.9 3.3 scatter_fusion.1
  408.9 2.2 gather_fusion.1
  412.5 3.4 scatter_fusion.1
  416.7 2.2 gather_fusion.1
  420.2 3.4 scatter_fusion.1
  423.5 2.7 convert_element_type.34
  426.2 220.5 %all-reduce.2.cloned.1.call-done = f32[256,256]{1,0:T(8,128)} async-done(((f32[256,256]{1,0:T(8,128)}), f32[256,256]{1,0:T(8,128)}) %all-reduce.2.cloned.1.call-update) | async-done | bytes 262160 | tf_op jit(solution)/shard_map/psum | solution.py:67
  646.8 1.7 broadcast_multiply_fusion
  648.5 73.6 %reduce-scatter.5.cloned.1.call-done = bf16[128,256]{1,0:T(8,128)(2,1)} async-done(((bf16[2048,256]{1,0:T(8,128)(2,1)}), bf16[128,256]{1,0:T(8,128)(2,1)}) %reduce-scatter.5.cloned.1.call-update) | async-done | bytes 65552 | tf_op jit(solution)/shard_map/reduce_scatter | solution.py:82
  (80 shorter events, 31.7 us)
Async XLA Ops:
  7.2 280.4 %copy-start = (bf16[256,256]{1,0:T(8,128)(2,1)S(1)}, bf16[256,256]{1,0:T(8,128)(2,1)}, u32[]{:S(2)}) copy-start(bf16[256,256]{1,0:T(8,128)(2,1)} %param.12) | copy-start | bytes 393220
  7.2 82.6 %copy-start.4 = (s32[1,1,96]{2,1,0:T(1,128)S(1)}, s32[1,1,96]{2,1,0:T(1,128)}, u32[]{:S(2)}) copy-start(s32[1,1,96]{2,1,0:T(1,128)} %param.14) | copy-start | bytes 1156
  7.2 82.5 %copy-start.5 = (s32[1,1,96]{2,1,0:T(1,128)S(1)}, s32[1,1,96]{2,1,0:T(1,128)}, u32[]{:S(2)}) copy-start(s32[1,1,96]{2,1,0:T(1,128)} %param.15) | copy-start | bytes 1156
  7.2 80.1 %all-gather.3.cloned.1.call-start = ((), (), s32[]{:S(2)}) async-start(), calls=%async_computation.2 | async-start | bytes 1114112 | tf_op jit(solution)/shard_map/all_gather | solution.py:51
  7.9 279.6 %reduce-scatter.3.cloned.1.call-start = ((), (), s32[]{:S(2)}) async-start(), calls=%async_computation.3 | async-start | bytes 2162688 | tf_op jit(solution)/shard_map/reduce_scatter | solution.py:56
  87.3 2.4 copy-start.1
  125.9 161.6 %copy-start.6 = (bf16[128,256]{1,0:T(8,128)(2,1)S(1)}, bf16[128,256]{1,0:T(8,128)(2,1)}, u32[]{:S(2)}) copy-start(bf16[128,256]{1,0:T(8,128)(2,1)} %param.17) | copy-start | bytes 196612
  129.8 160.4 %copy-start.2 = (bf16[96,128,128]{2,1,0:T(8,128)(2,1)S(1)}, bf16[96,128,128]{2,1,0:T(8,128)(2,1)}, u32[]{:S(2)}) copy-start(bf16[96,128,128]{2,1,0:T(8,128)(2,1)} %get-tuple-element.331) | copy-start | bytes 9437188
  129.8 246.2 %all-gather.5.cloned.1.call-start = ((), (), s32[]{:S(2)}) async-start(), calls=%async_computation.4 | async-start | bytes 2162688 | tf_op jit(solution)/shard_map/all_gather | solution.py:71
  290.1 356.7 %all-reduce.2.cloned.1.call-start = ((), (), s32[]{:S(2)}) async-start(), calls=%async_computation.6 | async-start | bytes 524288 | tf_op jit(solution)/shard_map/psum | solution.py:67
  290.2 2.8 copy-start.3
  293.9 428.1 %reduce-scatter.5.cloned.1.call-start = ((), (), s32[]{:S(2)}) async-start(), calls=%async_computation.5 | async-start | bytes 1114112 | tf_op jit(solution)/shard_map/reduce_scatter | solution.py:82
Sparse Core Ops, SparseCore 0:
  10.1 77.1 all-gather.2
  129.9 157.5 reduce-scatter.2
  292.0 83.9 all-gather.4
  382.2 264.5 all-reduce.1
  650.0 71.9 reduce-scatter.4
where the time goes:
time: 730 us; the launch traced here: 729 us
  waiting for transfers between devices  613 us (84%)
  other arithmetic  57.7 us (8%)
  local copies, waits for them, and re-layouts  23.4 us (3%)
  matrix products  19.3 us (3%)
  between operations  14.5 us (2%)
    psum x1, waiting for transfers between devices, local(): lax.psum(weight_term, ('row', 'col')) * (1.0 / math.sqrt(node_total))  221 us
    reduce_scatter x1, waiting for transfers between devices, local(): lax.psum_scatter(partial_value, 'col', scatter_dimension=0, tiled=True)  158 us
    all_gather x1, waiting for transfers between devices, local(): grad_rows = lax.all_gather(grad_agg, 'col', axis=0, tiled=True)  82.1 us
    all_gather x1, waiting for transfers between devices, local(): panel = lax.all_gather(features, 'row', axis=0, tiled=True)  78.6 us
    reduce_scatter x1, waiting for transfers between devices, local(): lax.psum_scatter(back_partial, 'row', scatter_dimension=0, tiled=True)  73.6 us
    scatter-add x12, other arithmetic, advance(): return total.at[targets].add(product)  39.8 us
    gather x12, local copies, waits for them, and re-layouts, advance(): pieces = jnp.take(panel, sources, axis=0)  16.5 us
  transfers between devices with their start and end apart: 5, of which 5 were waited for; matrix products, arithmetic and copies ran while one was open for 8% of the time, Pallas kernels for 0%

commit v1 on v0

v1 whole, which is shorter than its diff:
```python
import functools
import math

import jax
import jax.numpy as jnp
from jax import lax
from jax.experimental import pallas as pl
from jax.experimental.pallas import tpu as pltpu
from jax.sharding import PartitionSpec as P

bf16 = jnp.bfloat16
f32 = jnp.float32


def params(mib=48):
    return pltpu.CompilerParams(vmem_limit_bytes=mib * 1024 * 1024)


def forward_kernel(rows_ref, cols_ref, count_ref, core_ref, panel_ref, tiles_ref, keep_ref, send_ref, acc_ref):
    acc_ref[...] = jnp.zeros_like(acc_ref)
    count = count_ref[0]
    core = core_ref[0]

    def one(s):
        return jnp.dot(tiles_ref[s], panel_ref[cols_ref[s]], preferred_element_type=f32)

    def pair(t, carry):
        s = 2 * t
        first = one(s)
        second = one(s + 1)
        acc_ref[rows_ref[s]] += first
        acc_ref[rows_ref[s + 1]] += second
        return carry

    lax.fori_loop(0, count // 2, pair, 0)

    @pl.when(count % 2 == 1)
    def _():
        s = count - 1
        acc_ref[rows_ref[s]] += one(s)

    def flush(t, carry):
        keep_ref[t] = acc_ref[2 * t + core].astype(bf16)
        send_ref[t] = acc_ref[2 * t + 1 - core].astype(bf16)
        return carry

    lax.fori_loop(0, keep_ref.shape[0], flush, 0)


def forward_tiles(rows_ids, cols_ids, count, core, panel, tiles, brows):
    block, width = panel.shape[1:]
    half = jax.ShapeDtypeStruct((brows // 2, block, width), bf16)
    smem = pl.BlockSpec(memory_space=pltpu.SMEM)
    vmem = pl.BlockSpec(memory_space=pltpu.VMEM)
    return pl.pallas_call(
        forward_kernel,
        out_shape=(half, half),
        in_specs=[smem, smem, smem, smem, vmem, vmem],
        out_specs=(vmem, vmem),
        scratch_shapes=[pltpu.VMEM((brows, block, width), f32)],
        compiler_params=params(),
        name="forward_tiles",
    )(rows_ids, cols_ids, count, core, panel, tiles)


def backward_kernel(rows_ref, cols_ref, count_ref, core_ref, mine_ref, other_ref, tiles_ref, out_ref, acc_ref, grads_ref):
    acc_ref[...] = jnp.zeros_like(acc_ref)
    count = count_ref[0]
    core = core_ref[0]

    def place(t, carry):
        grads_ref[2 * t + core] = mine_ref[t]
        grads_ref[2 * t + 1 - core] = other_ref[t]
        return carry

    lax.fori_loop(0, mine_ref.shape[0], place, 0)

    def one(s):
        return lax.dot_general(
            tiles_ref[s], grads_ref[rows_ref[s]], (((0,), (0,)), ((), ())), preferred_element_type=f32
        )

    def pair(t, carry):
        s = 2 * t
        first = one(s)
        second = one(s + 1)
        acc_ref[cols_ref[s]] += first
        acc_ref[cols_ref[s + 1]] += second
        return carry

    lax.fori_loop(0, count // 2, pair, 0)

    @pl.when(count % 2 == 1)
    def _():
        s = count - 1
        acc_ref[cols_ref[s]] += one(s)

    def flush(t, carry):
        out_ref[t] = acc_ref[t].astype(bf16)
        return carry

    lax.fori_loop(0, out_ref.shape[0], flush, 0)


def backward_tiles(rows_ids, cols_ids, count, core, mine, other, tiles, bcols):
    half, block, width = mine.shape
    smem = pl.BlockSpec(memory_space=pltpu.SMEM)
    vmem = pl.BlockSpec(memory_space=pltpu.VMEM)
    return pl.pallas_call(
        backward_kernel,
        out_shape=jax.ShapeDtypeStruct((bcols, block, width), bf16),
        in_specs=[smem, smem, smem, smem, vmem, vmem, vmem],
        out_specs=vmem,
        scratch_shapes=[pltpu.VMEM((bcols, block, width), f32), pltpu.VMEM((2 * half, block, width), bf16)],
        compiler_params=params(),
        name="backward_tiles",
    )(rows_ids, cols_ids, count, core, mine, other, tiles)


def dense_kernel(parts_ref, weight_ref, cotangent_ref, act_ref, grad_agg_ref, weight_term_ref):
    total = parts_ref[0].astype(f32)
    for k in range(1, parts_ref.shape[0]):
        total += parts_ref[k].astype(f32)
    aggregated = total.astype(bf16)
    weight = weight_ref[...]
    preact = jnp.dot(aggregated, weight, preferred_element_type=f32)
    scale = math.sqrt(2 / math.pi)
    square = preact * preact
    tanh = jnp.tanh(scale * (preact + 0.044715 * (square * preact)))
    act_ref[...] = (0.5 * preact * (1.0 + tanh)).astype(bf16)
    slope = 0.5 * (1.0 + tanh) + (0.5 * preact) * (1.0 - tanh * tanh) * (
        scale * (1.0 + (3 * 0.044715) * square)
    )
    grad_pre = (cotangent_ref[...].astype(f32) * slope).astype(bf16)
    weight_term_ref[...] = lax.dot_general(
        aggregated, grad_pre, (((0,), (0,)), ((), ())), preferred_element_type=f32
    )
    grad_agg_ref[...] = lax.dot_general(
        grad_pre, weight, (((1,), (1,)), ((), ())), preferred_element_type=f32
    ).astype(bf16)


def dense(parts, weight, cotangent):
    rows, width = cotangent.shape
    vmem = pl.BlockSpec(memory_space=pltpu.VMEM)
    return pl.pallas_call(
        dense_kernel,
        out_shape=(
            jax.ShapeDtypeStruct((rows, width), bf16),
            jax.ShapeDtypeStruct((rows, width), bf16),
            jax.ShapeDtypeStruct((width, width), f32),
        ),
        in_specs=[vmem] * 3,
        out_specs=(vmem,) * 3,
        compiler_params=params(),
        name="dense",
    )(parts, weight, cotangent)


def spread(shard, axis, groups=None, count=None):
    copies = jnp.broadcast_to(shard[None], (count or lax.axis_size(axis),) + shard.shape)
    return lax.all_to_all(copies, axis, 0, 0, axis_index_groups=groups)


def local(features, weight, block_values, block_rows, block_cols, counts, cotangent):
    rows_dev, width = features.shape
    block = block_values.shape[-1]
    row_count = lax.axis_size("row")
    col_count = lax.axis_size("col")
    node_total = rows_dev * row_count * col_count
    tile_brows = rows_dev * col_count // block
    tile_bcols = rows_dev * row_count // block
    half = col_count // 2
    pairs = [(i, i ^ 1) for i in range(col_count)]
    groups = [[2 * k + c for k in range(half)] for c in range(2)]
    tiles = block_values[0, 0]
    rows_ids = block_rows[0, 0]
    cols_ids = block_cols[0, 0]
    count = counts[0]
    core = jnp.reshape(lax.axis_index("col") % 2, (1,)).astype(jnp.int32)

    panel = spread(features, "row")
    keep, send = forward_tiles(rows_ids, cols_ids, count, core, panel, tiles, tile_brows)
    came = lax.ppermute(send, "col", pairs)
    summed = (keep.astype(f32) + came.astype(f32)).astype(bf16)
    parts = lax.all_to_all(summed, "col", 0, 0, axis_index_groups=groups)
    activations, grad_agg, weight_term = dense(parts, weight, cotangent)

    mine = spread(grad_agg, "col", groups, half)
    other = lax.ppermute(mine, "col", pairs)
    weight_parts = lax.all_to_all(weight_term.reshape(col_count, width // col_count, width), "col", 0, 0)
    weight_rows = jnp.sum(weight_parts, axis=0)
    back = backward_tiles(rows_ids, cols_ids, count, core, mine, other, tiles, tile_bcols)
    weight_rows = jnp.sum(spread(weight_rows, "row"), axis=0) * (1.0 / math.sqrt(node_total))
    back_parts = lax.all_to_all(back, "row", 0, 0)
    feature_grad = jnp.sum(back_parts.astype(f32), axis=0).astype(bf16)
    weight_grad = spread(weight_rows, "col").reshape(width, width)
    return (activations, feature_grad, weight_grad)


def solution(mesh):
    in_specs = (
        P(("col", "row"), None),
        P(),
        P("row", "col", None, None, None),
        P("row", "col", None),
        P("row", "col", None),
        P("row", "col"),
        P(("row", "col"), None),
    )
    out_specs = (P(("row", "col"), None), P(("col", "row"), None), P())
    return jax.shard_map(local, mesh=mesh, in_specs=in_specs, out_specs=out_specs, check_vma=False)
```

time: 730 us -> 212 us (0.29)
  the two profiles are of different devices: /device:TPU:8 before, /device:TPU:20 now
where the time goes in v1:
time: 212 us; the launch traced here: 211 us
  blocking collectives  85.7 us (40%)
  waiting for transfers between devices  67.4 us (32%)
  starting transfers between devices  38.1 us (18%)
  Pallas kernels  13.6 us (6%)
  local copies, waits for them, and re-layouts  3.46 us (2%)
    all_to_all x2, blocking collectives, spread(): return lax.all_to_all(copies, axis, 0, 0, axis_index_groups=groups)  46.4 us
    all_to_all x1, blocking collectives, local(): parts = lax.all_to_all(summed, 'col', 0, 0, axis_index_groups=groups)  39.3 us
    all_to_all x2, waiting for transfers between devices, spread(): return lax.all_to_all(copies, axis, 0, 0, axis_index_groups=groups)  29.3 us
    all_to_all x1, waiting for transfers between devices, local(): back_parts = lax.all_to_all(back, 'row', 0, 0)  27.7 us
    all_to_all x2, starting transfers between devices, spread(): return lax.all_to_all(copies, axis, 0, 0, axis_index_groups=groups)  18.1 us
    all_to_all x1, starting transfers between devices, local(): lax.all_to_all(weight_term.reshape(col_count, width // col_count, width),...  8.06 us
    all_to_all x1, starting transfers between devices, local(): back_parts = lax.all_to_all(back, 'row', 0, 0)  7.92 us
    all_to_all x1, waiting for transfers between devices, local(): lax.all_to_all(weight_term.reshape(col_count, width // col_count, width),...  7.8 us
  transfers between devices with their start and end apart: 6, of which 5 were waited for; matrix products, arithmetic and copies ran while one was open for 0% of the time, Pallas kernels for 3%

profile of v1, /device:TPU:20, one launch (start us, length us, event | category | flops | bytes accessed | tf_op | source)
XLA Modules:
  0.0 210.9 jit_solution(11801319150639928099)
XLA Ops:
  0.6 0.0 copy-start.3
  0.6 0.0 copy-start.2
  0.7 1.9 broadcast_in_dim.8
  2.6 11.1 %all-to-all-start = ((bf16[16,128,256]{2,1,0:T(8,128)(2,1)}), bf16[16,128,256]{2,1,0:T(8,128)(2,1)S(1)}, u32[]{:S(2)}, u32[]{:S(2)}) async-start(bf16[16,128,256]{2,1,0:T(8,128)(2,1)} %broadcast_in_dim.8), calls=%async_computation | async-start | bytes 2097152 | tf_op jit(solution)/shard_map/all_to_all | solution.py:162
  14.3 26.4 %all-to-all-done.panel_ref = bf16[16,128,256]{2,1,0:T(8,128)(2,1)S(1)} async-done(((bf16[16,128,256]{2,1,0:T(8,128)(2,1)}), bf16[16,128,256]{2,1,0:T(8,128)(2,1)S(1)}, u32[]{:S(2)}, u32[]{:S(2)}) %all-to-all-start) | async-done | bytes 1048608 | tf_op jit(solution)/shard_map/all_to_all | solution.py:162
  40.7 0.0 copy-done.3
  40.7 0.0 copy-done.2
  40.7 5.5 %forward_tiles.1 = (bf16[16,128,256]{2,1,0:T(8,128)(2,1)S(1)}, bf16[16,128,256]{2,1,0:T(8,128)(2,1)S(1)}) custom-call(s32[96]{0:T(128)S(1)} %bitcast.9, s32[96]{0:T(128)S(1)} %bitcast.11, s32[1]{0:T(128)} %bitcast.7.count_ref, s32[1]{0:T(128)} %bitcast.3.core_ref, bf16[16,128,256]{2,1,0:T(8,128)(2,1)S(1)} %all-to-all-done.panel_ref, ...), custom_call_target="tpu_custom_call" | custom-call | tf_op jit(solution)/shard_map/forward_tiles/pallas_call | solution.py:55
  46.2 1.9 collective-permute-start
  48.1 2.6 %collective-permute-done = bf16[16,128,256]{2,1,0:T(8,128)(2,1)S(1)} collective-permute-done((bf16[16,128,256]{2,1,0:T(8,128)(2,1)S(1)}, bf16[16,128,256]{2,1,0:T(8,128)(2,1)S(1)}, u32[]{:S(2)}, u32[]{:S(2)}) %collective-permute-start) | collective-permute-done | bytes 1048608 | tf_op jit(solution)/shard_map/ppermute | solution.py:184
  50.7 0.0 copy-start
  50.7 0.0 copy-start.1
  50.7 0.3 add_convert_fusion
  51.1 39.3 %all_to_all.35.parts_ref = bf16[16,128,256]{2,1,0:T(8,128)(2,1)S(1)} all-to-all(bf16[16,128,256]{2,1,0:T(8,128)(2,1)S(1)} %add_convert_fusion), channel_id=1, replica_groups={{0,2,4,6,8,10,12,14,16,18,20,22,24,26,28,30},{1,3,5,7,9,11,13,15,17,19,..., dimensions={0} | all-to-all | bytes 2097152 | tf_op jit(solution)/shard_map/all_to_all | solution.py:186
  90.4 0.0 copy-done
  90.4 0.0 copy-done.1
  90.4 1.2 dense.1
  91.6 0.1 broadcast_in_dim.9
  91.7 33.0 %all_to_all.36.mine_ref = bf16[16,128,256]{2,1,0:T(8,128)(2,1)S(1)} all-to-all(bf16[16,128,256]{2,1,0:T(8,128)(2,1)S(1)} %broadcast_in_dim.9), channel_id=1, replica_groups={{0,2,4,6,8,10,12,14,16,18,20,22,24,26,28,30},{1,3,5,7,9,11,13,15,17,19,..., dimensions={0} | all-to-all | bytes 2097152 | tf_op jit(solution)/shard_map/all_to_all | solution.py:162
  124.7 8.1 %all-to-all-start.4 = ((f32[32,8,256]{2,1,0:T(8,128)}), f32[32,8,256]{2,1,0:T(8,128)S(1)}, u32[]{:S(2)}, u32[]{:S(2)}) async-start(f32[32,8,256]{2,1,0:T(8,128)} %bitcast.5), calls=%async_computation.4 | async-start | bytes 524288 | tf_op jit(solution)/shard_map/all_to_all | solution.py:191
  132.7 2.1 collective-permute-start.1
  134.8 7.8 %all-to-all-done.4 = f32[32,8,256]{2,1,0:T(8,128)S(1)} async-done(((f32[32,8,256]{2,1,0:T(8,128)}), f32[32,8,256]{2,1,0:T(8,128)S(1)}, u32[]{:S(2)}, u32[]{:S(2)}) %all-to-all-start.4) | async-done | bytes 262176 | tf_op jit(solution)/shard_map/all_to_all | solution.py:191
  142.7 13.4 %all_to_all.37 = f32[16,8,256]{2,1,0:T(8,128)S(1)} all-to-all(f32[16,8,256]{2,1,0:T(8,128)S(1)} %broadcast_in_dim.10), channel_id=1, replica_groups=mesh['row'=16,'col'=32] {'row'}, dimensions={0} | all-to-all | bytes 262144 | tf_op jit(solution)/shard_map/all_to_all | solution.py:162
  156.1 0.7 broadcast_in_dim.11
  156.8 7.1 %all-to-all-start.6 = ((f32[32,8,256]{2,1,0:T(8,128)}), f32[32,8,256]{2,1,0:T(8,128)S(1)}, u32[]{:S(2)}, u32[]{:S(2)}) async-start(f32[32,8,256]{2,1,0:T(8,128)} %broadcast_in_dim.11), calls=%async_computation.6 | async-start | bytes 524288 | tf_op jit(solution)/shard_map/all_to_all | solution.py:162
  163.9 0.0 collective-permute-done.1.other_ref
  164.0 6.9 %backward_tiles.1 = bf16[16,128,256]{2,1,0:T(8,128)(2,1)} custom-call(s32[96]{0:T(128)S(1)} %bitcast.10, s32[96]{0:T(128)S(1)} %bitcast.12, s32[1]{0:T(128)} %bitcast.8.count_ref, s32[1]{0:T(128)} %bitcast.3.core_ref, bf16[16,128,256]{2,1,0:T(8,128)(2,1)S(1)} %all_to_all.36.mine_ref, bf16[16,128,256]{2,1,0:T(8,128)(2,1)S(1)} %collective-permute-done.1.other_ref, ...), custom_call_target="tpu_custom_call" | custom-call | tf_op jit(solution)/shard_map/backward_tiles/pallas_call | solution.py:109
  170.9 2.9 %all-to-all-done.6 = f32[32,8,256]{2,1,0:T(8,128)S(1)} async-done(((f32[32,8,256]{2,1,0:T(8,128)}), f32[32,8,256]{2,1,0:T(8,128)S(1)}, u32[]{:S(2)}, u32[]{:S(2)}) %all-to-all-start.6) | async-done | bytes 262176 | tf_op jit(solution)/shard_map/all_to_all | solution.py:162
  173.8 7.9 %all-to-all-start.3 = ((bf16[16,128,256]{2,1,0:T(8,128)(2,1)}), bf16[16,128,256]{2,1,0:T(8,128)(2,1)S(1)}, u32[]{:S(2)}, u32[]{:S(2)}) async-start(bf16[16,128,256]{2,1,0:T(8,128)(2,1)} %backward_tiles.1), calls=%async_computation.3 | async-start | bytes 2097152 | tf_op jit(solution)/shard_map/all_to_all | solution.py:195
  181.7 27.7 %all-to-all-done.3 = bf16[16,128,256]{2,1,0:T(8,128)(2,1)S(1)} async-done(((bf16[16,128,256]{2,1,0:T(8,128)(2,1)}), bf16[16,128,256]{2,1,0:T(8,128)(2,1)S(1)}, u32[]{:S(2)}, u32[]{:S(2)}) %all-to-all-start.3) | async-done | bytes 1048608 | tf_op jit(solution)/shard_map/all_to_all | solution.py:195
  209.4 0.8 reduce_sum.30
  210.2 0.7 copy.12
  (4 shorter events, 0.1 us)
Async XLA Ops:
  0.6 40.1 %copy-start.3 = (s32[1,1,96]{2,1,0:T(1,128)S(1)}, s32[1,1,96]{2,1,0:T(1,128)}, u32[]{:S(2)}) copy-start(s32[1,1,96]{2,1,0:T(1,128)} %param.11) | copy-start | bytes 1156
  0.6 40.1 %copy-start.2 = (s32[1,1,96]{2,1,0:T(1,128)S(1)}, s32[1,1,96]{2,1,0:T(1,128)}, u32[]{:S(2)}) copy-start(s32[1,1,96]{2,1,0:T(1,128)} %param.10) | copy-start | bytes 1156
  2.6 38.1 %all-to-all-start = ((bf16[16,128,256]{2,1,0:T(8,128)(2,1)}), bf16[16,128,256]{2,1,0:T(8,128)(2,1)S(1)}, u32[]{:S(2)}, u32[]{:S(2)}) async-start(bf16[16,128,256]{2,1,0:T(8,128)(2,1)} %broadcast_in_dim.8), calls=%async_computation | async-start | bytes 2097152 | tf_op jit(solution)/shard_map/all_to_all | solution.py:162
  46.2 4.6 %collective-permute-start = (bf16[16,128,256]{2,1,0:T(8,128)(2,1)S(1)}, bf16[16,128,256]{2,1,0:T(8,128)(2,1)S(1)}, u32[]{:S(2)}, u32[]{:S(2)}) collective-permute-start(bf16[16,128,256]{2,1,0:T(8,128)(2,1)S(1)} %get-tuple-element.9), channel_id=1, source_target_pairs={{0,1},{1,0},{2,3},{3,2},{4,5},{5,4},{6,7},{7,6},{8,9},{9,8},{10,11... | collective-permute-start | bytes 3145736 | tf_op jit(solution)/shard_map/ppermute | solution.py:184
  50.7 39.7 %copy-start = (bf16[256,256]{1,0:T(8,128)(2,1)S(1)}, bf16[256,256]{1,0:T(8,128)(2,1)}, u32[]{:S(2)}) copy-start(bf16[256,256]{1,0:T(8,128)(2,1)} %weight_ref.1) | copy-start | bytes 393220
  50.7 39.7 %copy-start.1 = (bf16[128,256]{1,0:T(8,128)(2,1)S(1)}, bf16[128,256]{1,0:T(8,128)(2,1)}, u32[]{:S(2)}) copy-start(bf16[128,256]{1,0:T(8,128)(2,1)} %cotangent_ref.1) | copy-start | bytes 196612
  124.7 17.9 %all-to-all-start.4 = ((f32[32,8,256]{2,1,0:T(8,128)}), f32[32,8,256]{2,1,0:T(8,128)S(1)}, u32[]{:S(2)}, u32[]{:S(2)}) async-start(f32[32,8,256]{2,1,0:T(8,128)} %bitcast.5), calls=%async_computation.4 | async-start | bytes 524288 | tf_op jit(solution)/shard_map/all_to_all | solution.py:191
  132.7 31.2 %collective-permute-start.1 = (bf16[16,128,256]{2,1,0:T(8,128)(2,1)S(1)}, bf16[16,128,256]{2,1,0:T(8,128)(2,1)S(1)}, u32[]{:S(2)}, u32[]{:S(2)}) collective-permute-start(bf16[16,128,256]{2,1,0:T(8,128)(2,1)S(1)} %all_to_all.36.mine_ref), channel_id=1, source_target_pairs={{0,1},{1,0},{2,3},{3,2},{4,5},{5,4},{6,7},{7,6},{8,9},{9,8},{10,11... | collective-permute-start | bytes 3145736 | tf_op jit(solution)/shard_map/ppermute | solution.py:190
  156.8 16.9 %all-to-all-start.6 = ((f32[32,8,256]{2,1,0:T(8,128)}), f32[32,8,256]{2,1,0:T(8,128)S(1)}, u32[]{:S(2)}, u32[]{:S(2)}) async-start(f32[32,8,256]{2,1,0:T(8,128)} %broadcast_in_dim.11), calls=%async_computation.6 | async-start | bytes 524288 | tf_op jit(solution)/shard_map/all_to_all | solution.py:162
  173.8 35.6 %all-to-all-start.3 = ((bf16[16,128,256]{2,1,0:T(8,128)(2,1)}), bf16[16,128,256]{2,1,0:T(8,128)(2,1)S(1)}, u32[]{:S(2)}, u32[]{:S(2)}) async-start(bf16[16,128,256]{2,1,0:T(8,128)(2,1)} %backward_tiles.1), calls=%async_computation.3 | async-start | bytes 2097152 | tf_op jit(solution)/shard_map/all_to_all | solution.py:195

commit v2 on v1

v2 whole, which is shorter than its diff:
```python
import math

import jax
import jax.numpy as jnp
from jax import lax
from jax.experimental import pallas as pl
from jax.experimental.pallas import tpu as pltpu
from jax.sharding import PartitionSpec as P

bf16 = jnp.bfloat16
f32 = jnp.float32
i32 = jnp.int32
smem = pl.BlockSpec(memory_space=pltpu.SMEM)
vmem = pl.BlockSpec(memory_space=pltpu.VMEM)
row_base = 4
col_base = 8
quad = 4


def params(mib=48):
    return pltpu.CompilerParams(vmem_limit_bytes=mib * 1024 * 1024)


def cost(flops, moved):
    return pl.CostEstimate(flops=flops, bytes_accessed=moved, transcendentals=0)


def sort_slots(ids_ref, count, base_ref, extra_ref, extra_ids_ref, total_ref, seen_ref, last_ref, base):
    zero_slot = ids_ref.shape[0]
    targets = base_ref.shape[0] // base

    def clear_base(t, carry):
        base_ref[t] = zero_slot
        return carry

    def clear_extra(t, carry):
        extra_ref[t] = zero_slot
        return carry

    def clear_seen(t, carry):
        seen_ref[t] = 0
        return carry

    lax.fori_loop(0, base_ref.shape[0], clear_base, 0)
    lax.fori_loop(0, extra_ref.shape[0], clear_extra, 0)
    lax.fori_loop(0, targets, clear_seen, 0)
    total_ref[0] = 0

    def place(s, carry):
        target = ids_ref[s]
        seen = seen_ref[target]
        seen_ref[target] = seen + 1

        @pl.when(seen < base)
        def _():
            base_ref[target * base + seen] = s

        @pl.when(seen >= base)
        def _():
            over = (seen - base) % quad

            @pl.when(over == 0)
            def _():
                group = total_ref[0]
                total_ref[0] = group + 1
                last_ref[target] = group
                extra_ids_ref[group] = target

            extra_ref[last_ref[target] * quad + over] = s

        return carry

    lax.fori_loop(0, count, place, 0)


def prepare_kernel(
    rows_ref, cols_ref, count_ref, tiles_ref,
    by_row_ref, more_by_row_ref, more_rows_ref, row_total_ref,
    by_col_ref, more_by_col_ref, more_cols_ref, col_total_ref,
    rows_out_ref, cols_out_ref, plain_ref, flipped_ref,
    seen_ref, last_ref,
):
    slots = tiles_ref.shape[0]
    count = count_ref[0]
    sort_slots(rows_ref, count, by_row_ref, more_by_row_ref, more_rows_ref, row_total_ref, seen_ref, last_ref, row_base)
    sort_slots(cols_ref, count, by_col_ref, more_by_col_ref, more_cols_ref, col_total_ref, seen_ref, last_ref, col_base)

    def copy_ids(s, carry):
        rows_out_ref[s] = rows_ref[s]
        cols_out_ref[s] = cols_ref[s]
        return carry

    lax.fori_loop(0, slots, copy_ids, 0)
    rows_out_ref[slots] = 0
    cols_out_ref[slots] = 0

    def copy_tile(s, carry):
        tile = tiles_ref[s]
        plain_ref[s] = tile
        flipped_ref[s] = tile.T
        return carry

    lax.fori_loop(0, slots, copy_tile, 0)
    plain_ref[slots] = jnp.zeros(plain_ref.shape[1:], bf16)
    flipped_ref[slots] = jnp.zeros(plain_ref.shape[1:], bf16)


def prepare(rows_ids, cols_ids, count, tiles, brows, bcols):
    slots, block, _ = tiles.shape
    ints = lambda size: jax.ShapeDtypeStruct((size,), i32)
    held = jax.ShapeDtypeStruct((slots + 1, block, block), bf16)
    lists = lambda targets, base: (ints(targets * base), ints(slots * quad), ints(slots), ints(1))
    return pl.pallas_call(
        prepare_kernel,
        out_shape=(*lists(brows, row_base), *lists(bcols, col_base), ints(slots + 1), ints(slots + 1), held, held),
        in_specs=[smem, smem, smem, vmem],
        out_specs=(smem,) * 10 + (vmem, vmem),
        scratch_shapes=[pltpu.SMEM((max(brows, bcols),), i32), pltpu.SMEM((max(brows, bcols),), i32)],
        compiler_params=params(),
        cost_estimate=cost(0, 9 * slots * block * block * 2),
        name="prepare",
    )(rows_ids, cols_ids, count, tiles)


def grouped_product(tiles_ref, ids_ref, source, list_ref, first, size):
    slots = [list_ref[first + k] for k in range(size)]
    left = jnp.concatenate([tiles_ref[s] for s in slots], axis=1)
    right = jnp.concatenate([source(ids_ref[s]) for s in slots], axis=0)
    return jnp.dot(left, right, preferred_element_type=f32)


def forward_kernel(
    by_row_ref, more_ref, more_rows_ref, total_ref, cols_ref, core_ref, panel_ref, tiles_ref, keep_ref, send_ref, acc_ref
):
    core = core_ref[0]
    source = lambda c: panel_ref[c]

    def base(t, carry):
        acc_ref[t] = grouped_product(tiles_ref, cols_ref, source, by_row_ref, t * row_base, row_base)
        return carry

    lax.fori_loop(0, acc_ref.shape[0], base, 0, unroll=4)

    def more(t, carry):
        acc_ref[more_rows_ref[t]] += grouped_product(tiles_ref, cols_ref, source, more_ref, t * quad, quad)
        return carry

    lax.fori_loop(0, total_ref[0], more, 0)

    def flush(t, carry):
        keep_ref[t] = acc_ref[2 * t + core].astype(bf16)
        send_ref[t] = acc_ref[2 * t + 1 - core].astype(bf16)
        return carry

    lax.fori_loop(0, keep_ref.shape[0], flush, 0)


def forward_tiles(by_row, more, more_rows, total, cols_ids, core, panel, tiles, brows):
    block, width = panel.shape[1:]
    half = jax.ShapeDtypeStruct((brows // 2, block, width), bf16)
    return pl.pallas_call(
        forward_kernel,
        out_shape=(half, half),
        in_specs=[smem] * 6 + [vmem, vmem],
        out_specs=(vmem, vmem),
        scratch_shapes=[pltpu.VMEM((brows, block, width), f32)],
        compiler_params=params(),
        cost_estimate=cost(2 * brows * row_base * block * block * width, tiles.size * 2),
        name="forward_tiles",
    )(by_row, more, more_rows, total, cols_ids, core, panel, tiles)


def sum_parts(ref):
    total = ref[0].astype(f32)
    for k in range(1, ref.shape[0]):
        total += ref[k].astype(f32)
    return total


def dense_kernel(parts_ref, weight_ref, cotangent_ref, act_ref, message_ref):
    aggregated = sum_parts(parts_ref)
    aggregated_half = aggregated.astype(bf16)
    preact = jnp.dot(aggregated_half, weight_ref[...], preferred_element_type=f32)
    scale = math.sqrt(2 / math.pi)
    square = preact * preact
    tanh = jnp.tanh(scale * (preact + 0.044715 * (square * preact)))
    act_ref[...] = (0.5 * preact * (1.0 + tanh)).astype(bf16)
    slope = 0.5 * (1.0 + tanh) + (0.5 * preact) * (1.0 - tanh * tanh) * (
        scale * (1.0 + (3 * 0.044715) * square)
    )
    grad_pre = (cotangent_ref[...].astype(f32) * slope).astype(bf16)
    turned = aggregated_half.astype(f32).T
    peers = message_ref.shape[0]
    rows = grad_pre.shape[0]
    own = turned.shape[0] // peers
    for k in range(peers):
        message_ref[k, :rows, :] = grad_pre
        low = turned[k * own : k * own + own // 2]
        high = turned[k * own + own // 2 : (k + 1) * own]
        message_ref[k, rows:, :] = jnp.concatenate([low, high], axis=1).astype(bf16)


def dense(parts, weight, cotangent):
    rows, width = cotangent.shape
    peers = parts.shape[0]
    return pl.pallas_call(
        dense_kernel,
        out_shape=(
            jax.ShapeDtypeStruct((rows, width), bf16),
            jax.ShapeDtypeStruct((peers, rows + rows // peers, width), bf16),
        ),
        in_specs=[vmem] * 3,
        out_specs=(vmem,) * 2,
        compiler_params=params(),
        name="dense",
    )(parts, weight, cotangent)


def weight_kernel(message_ref, out_ref):
    peers, _, width = message_ref.shape
    rows = width // 2
    total = None
    for k in range(peers):
        packed = message_ref[k, rows:, :].astype(f32)
        left = jnp.concatenate([packed[:, :rows], packed[:, rows:]], axis=0).astype(bf16)
        term = jnp.dot(left, message_ref[k, :rows, :], preferred_element_type=f32)
        total = term if total is None else total + term
    for k in range(out_ref.shape[0]):
        out_ref[k] = total


def weight_part(message, copies):
    peers, _, width = message.shape
    return pl.pallas_call(
        weight_kernel,
        out_shape=jax.ShapeDtypeStruct((copies, width // peers, width), f32),
        in_specs=[vmem],
        out_specs=vmem,
        compiler_params=params(),
        name="weight_part",
    )(message)


def backward_kernel(by_col_ref, more_ref, more_cols_ref, total_ref, rows_ref, core_ref, mine_ref, other_ref, tiles_ref, out_ref, acc_ref, grads_ref):
    core = core_ref[0]
    block = out_ref.shape[1]

    def place(t, carry):
        grads_ref[2 * t + core] = mine_ref[t, :block, :]
        grads_ref[2 * t + 1 - core] = other_ref[t, :block, :]
        return carry

    lax.fori_loop(0, mine_ref.shape[0], place, 0)
    source = lambda r: grads_ref[r]

    def base(t, carry):
        acc_ref[t] = grouped_product(tiles_ref, rows_ref, source, by_col_ref, t * col_base, col_base)
        return carry

    lax.fori_loop(0, acc_ref.shape[0], base, 0, unroll=2)

    def more(t, carry):
        acc_ref[more_cols_ref[t]] += grouped_product(tiles_ref, rows_ref, source, more_ref, t * quad, quad)
        return carry

    lax.fori_loop(0, total_ref[0], more, 0)

    def flush(t, carry):
        out_ref[t] = acc_ref[t].astype(bf16)
        return carry

    lax.fori_loop(0, out_ref.shape[0], flush, 0)


def backward_tiles(by_col, more, more_cols, total, rows_ids, core, mine, other, tiles, bcols):
    half, _, width = mine.shape
    block = tiles.shape[-1]
    return pl.pallas_call(
        backward_kernel,
        out_shape=jax.ShapeDtypeStruct((bcols, block, width), bf16),
        in_specs=[smem] * 6 + [vmem] * 3,
        out_specs=vmem,
        scratch_shapes=[pltpu.VMEM((bcols, block, width), f32), pltpu.VMEM((2 * half, block, width), bf16)],
        compiler_params=params(),
        cost_estimate=cost(2 * bcols * col_base * block * block * width, tiles.size * 2),
        name="backward_tiles",
    )(by_col, more, more_cols, total, rows_ids, core, mine, other, tiles)


def finish_kernel(parts_ref, weight_ref, out_ref):
    total = sum_parts(parts_ref).astype(bf16)
    out_ref[...] = lax.dot_general(
        total, weight_ref[...], (((1,), (1,)), ((), ())), preferred_element_type=f32
    ).astype(bf16)


def finish(parts, weight):
    return pl.pallas_call(
        finish_kernel,
        out_shape=jax.ShapeDtypeStruct(parts.shape[1:], bf16),
        in_specs=[vmem] * 2,
        out_specs=vmem,
        compiler_params=params(),
        name="finish",
    )(parts, weight)


def gather_over_col(rows, me, size):
    held = rows + lax.ppermute(rows, "col", [(i, i ^ 1) for i in range(size)])
    held = held[None]
    distance = 2
    while distance < size:
        came = lax.ppermute(held, "col", [(i, i ^ distance) for i in range(size)])
        upper = (me // distance) % 2 == 1
        held = jnp.where(upper, jnp.concatenate([came, held]), jnp.concatenate([held, came]))
        distance *= 2
    return held.reshape(-1, rows.shape[-1])


def local(features, weight, block_values, block_rows, block_cols, counts, cotangent):
    rows_dev, width = features.shape
    block = block_values.shape[-1]
    row_count = lax.axis_size("row")
    col_count = lax.axis_size("col")
    node_total = rows_dev * row_count * col_count
    brows = rows_dev * col_count // block
    bcols = rows_dev * row_count // block
    half = col_count // 2
    pairs = [(i, i ^ 1) for i in range(col_count)]
    groups = [[2 * k + c for k in range(half)] for c in range(2)]
    me = lax.axis_index("col")
    core = jnp.reshape(me % 2, (1,)).astype(i32)

    copies = jnp.broadcast_to(features[None], (row_count,) + features.shape)
    panel = lax.all_to_all(copies, "row", 0, 0)
    lists = prepare(block_rows[0, 0], block_cols[0, 0], counts[0], block_values[0, 0], brows, bcols)
    row_lists, col_lists = lists[:4], lists[4:8]
    rows_ids, cols_ids, tiles, flipped = lists[8:]

    keep, send = forward_tiles(*row_lists, cols_ids, core, panel, tiles, brows)
    came = lax.ppermute(send, "col", pairs)
    summed = (keep.astype(f32) + came.astype(f32)).astype(bf16)
    parts = lax.all_to_all(summed, "col", 0, 0, axis_index_groups=groups)
    activations, messages = dense(parts, weight, cotangent)

    mine = lax.all_to_all(messages, "col", 0, 0, axis_index_groups=groups)
    other = lax.ppermute(mine, "col", pairs)
    weight_parts = lax.all_to_all(weight_part(mine, row_count), "row", 0, 0)
    back = backward_tiles(*col_lists, rows_ids, core, mine, other, flipped, bcols)
    back_parts = lax.all_to_all(back, "row", 0, 0)
    weight_rows = jnp.sum(weight_parts, axis=0) * (1.0 / math.sqrt(node_total))
    weight_grad = gather_over_col(weight_rows, me, col_count)
    feature_grad = finish(back_parts, weight)
    return (activations, feature_grad, weight_grad)


def solution(mesh):
    in_specs = (
        P(("col", "row"), None),
        P(),
        P("row", "col", None, None, None),
        P("row", "col", None),
        P("row", "col", None),
        P("row", "col"),
        P(("row", "col"), None),
    )
    out_specs = (P(("row", "col"), None), P(("col", "row"), None), P())
    return jax.shard_map(local, mesh=mesh, in_specs=in_specs, out_specs=out_specs, check_vma=False)
```

time: 212 us -> 187 us (0.88)
  the two profiles are of different devices: /device:TPU:20 before, /device:TPU:2 now
where the time goes in v2:
time: 187 us; the launch traced here: 186 us
  blocking collectives  74.1 us (40%)
  starting transfers between devices  38 us (20%)
  waiting for transfers between devices  34.3 us (18%)
  Pallas kernels  33.2 us (18%)
  local copies, waits for them, and re-layouts  3.83 us (2%)
    all_to_all x1, blocking collectives, local(): parts = lax.all_to_all(summed, 'col', 0, 0, axis_index_groups=groups)  39.2 us
    all_to_all x1, blocking collectives, local(): mine = lax.all_to_all(messages, 'col', 0, 0, axis_index_groups=groups)  34.9 us
    ppermute x4, waiting for transfers between devices, gather_over_col(): came = lax.ppermute(held, 'col', [(i, i ^ distance) for i in range(size)])  22.6 us
    pallas_call x1, Pallas kernels, prepare(): pl.pallas_call(prepare_kernel, out_shape=(*lists(brows, row_base), *lists...  18.6 us
    all_to_all x1, starting transfers between devices, local(): panel = lax.all_to_all(copies, 'row', 0, 0)  11.8 us
    ppermute x4, starting transfers between devices, gather_over_col(): came = lax.ppermute(held, 'col', [(i, i ^ distance) for i in range(size)])  9.35 us
    pallas_call x1, Pallas kernels, backward_tiles(): pl.pallas_call(backward_kernel, out_shape=jax.ShapeDtypeStruct((bcols, bl...  6.45 us
    all_to_all x1, starting transfers between devices, local(): weight_parts = lax.all_to_all(weight_part(mine, row_count), 'row', 0, 0)  5.74 us
  transfers between devices with their start and end apart: 10, of which 8 were waited for; matrix products, arithmetic and copies ran while one was open for 0% of the time, Pallas kernels for 14%

profile of v2, /device:TPU:2, one launch (start us, length us, event | category | flops | bytes accessed | tf_op | source)
XLA Modules:
  0.0 186.2 jit_solution(1133227361474061144)
XLA Ops:
  0.7 1.9 %broadcast_in_dim.4 = bf16[16,128,256]{2,1,0:T(8,128)(2,1)} broadcast(bf16[128,256]{1,0:T(8,128)(2,1)} %param.7), dimensions={1,2} | broadcast | bytes 1114112 | tf_op jit(solution)/shard_map/broadcast_in_dim | solution.py:334
  2.6 11.8 %all-to-all-start = ((bf16[16,128,256]{2,1,0:T(8,128)(2,1)}), bf16[16,128,256]{2,1,0:T(8,128)(2,1)S(1)}, u32[]{:S(2)}, u32[]{:S(2)}) async-start(bf16[16,128,256]{2,1,0:T(8,128)(2,1)} %broadcast_in_dim.4), calls=%async_computation | async-start | bytes 2097152 | tf_op jit(solution)/shard_map/all_to_all | solution.py:335
  15.0 0.0 copy-start
  15.1 1.9 %copy-done = bf16[1,1,96,128,128]{4,3,2,1,0:T(8,128)(2,1)S(1)} copy-done((bf16[1,1,96,128,128]{4,3,2,1,0:T(8,128)(2,1)S(1)}, bf16[1,1,96,128,128]{4,3,2,1,0:T(8,128)(2,1)}, u32[]{:S(2)}) %copy-start) | copy-done | bytes 3145752
  16.9 18.6 %prepare.1 = (s32[128]{0:T(128)S(1)}, s32[384]{0:T(512)S(1)}, s32[96]{0:T(128)S(1)}, s32[1]{0:T(128)}, s32[128]{0:T(128)S(1)}, /*index=5*/s32[384]{0:T(512)S(1)}...) custom-call(s32[96]{0:T(128)S(1)} %bitcast.10, ...), custom_call_target="tpu_custom_call" | custom-call | bytes 28311552 | tf_op jit(solution)/shard_map/prepare/pallas_call | solution.py:113
  35.6 4.6 %all-to-all-done.panel_ref = bf16[16,128,256]{2,1,0:T(8,128)(2,1)S(1)} async-done(((bf16[16,128,256]{2,1,0:T(8,128)(2,1)}), bf16[16,128,256]{2,1,0:T(8,128)(2,1)S(1)}, u32[]{:S(2)}, u32[]{:S(2)}) %all-to-all-start) | async-done | bytes 1048608 | tf_op jit(solution)/shard_map/all_to_all | solution.py:335
  40.1 5.3 %forward_tiles.1 = (bf16[16,128,256]{2,1,0:T(8,128)(2,1)S(1)}, bf16[16,128,256]{2,1,0:T(8,128)(2,1)S(1)}) custom-call(s32[128]{0:T(128)S(1)} %get-tuple-element.19.by_row_ref, s32[384]{0:T(512)S(1)} %get-tuple-element.20.more_ref, s32[96]{0:T(128)S(1)} %get-tuple-element.21.more_rows_ref, s32[1]{0:T(128)} %get-tuple-element.22.total_ref, ...), custom_call_target="tpu_custom_call" | custom-call | flops 1073741824 | bytes 3178496 | tf_op jit(solution)/shard_map/forward_tiles/pallas_call | solution.py:161
  45.5 1.9 %collective-permute-start = (bf16[16,128,256]{2,1,0:T(8,128)(2,1)S(1)}, bf16[16,128,256]{2,1,0:T(8,128)(2,1)S(1)}, u32[]{:S(2)}, u32[]{:S(2)}) collective-permute-start(bf16[16,128,256]{2,1,0:T(8,128)(2,1)S(1)} %get-tuple-element.26), channel_id=1, source_target_pairs={{0,1},{1,0},{2,3},{3,2},{4,5},{5,4},{6,7},{7,6},{8,9},{9,8},{10,11... | collective-permute-start | bytes 3145736 | tf_op jit(solution)/shard_map/ppermute | solution.py:341
  47.4 2.6 %collective-permute-done = bf16[16,128,256]{2,1,0:T(8,128)(2,1)S(1)} collective-permute-done((bf16[16,128,256]{2,1,0:T(8,128)(2,1)S(1)}, bf16[16,128,256]{2,1,0:T(8,128)(2,1)S(1)}, u32[]{:S(2)}, u32[]{:S(2)}) %collective-permute-start) | collective-permute-done | bytes 1048608 | tf_op jit(solution)/shard_map/ppermute | solution.py:341
  50.0 0.4 add_convert_fusion
  50.4 39.2 %all_to_all.25.parts_ref = bf16[16,128,256]{2,1,0:T(8,128)(2,1)S(1)} all-to-all(bf16[16,128,256]{2,1,0:T(8,128)(2,1)S(1)} %add_convert_fusion), channel_id=1, replica_groups={{0,2,4,6,8,10,12,14,16,18,20,22,24,26,28,30},{1,3,5,7,9,11,13,15,17,19,..., dimensions={0} | all-to-all | bytes 2097152 | tf_op jit(solution)/shard_map/all_to_all | solution.py:343
  89.6 0.9 dense.1
  90.5 34.9 %all_to_all.26.mine_ref.message_ref = bf16[16,136,256]{2,1,0:T(8,128)(2,1)S(1)} all-to-all(bf16[16,136,256]{2,1,0:T(8,128)(2,1)S(1)} %get-tuple-element.33), channel_id=1, replica_groups={{0,2,4,6,8,10,12,14,16,18,20,22,24,26,28,30},{1,3,5,7,9,11,13,15,17,19,..., dimensions={0} | all-to-all | bytes 2228224 | tf_op jit(solution)/shard_map/all_to_all | solution.py:346
  125.4 1.9 %collective-permute-start.1 = (bf16[16,136,256]{2,1,0:T(8,128)(2,1)S(1)}, bf16[16,136,256]{2,1,0:T(8,128)(2,1)S(1)}, u32[]{:S(2)}, u32[]{:S(2)}) collective-permute-start(bf16[16,136,256]{2,1,0:T(8,128)(2,1)S(1)} %all_to_all.26.mine_ref.message_ref), channel_id=1, source_target_pairs={{0,1},{1,0},{2,3},{3,2},{4,5},{5,4},{6,7},{7,6},{8,9},{9,8},{10,11... | collective-permute-start | bytes 3342344 | tf_op jit(solution)/shard_map/ppermute | solution.py:347
  127.3 1.0 weight_part.1
  128.3 5.7 %all-to-all-start.4 = ((f32[16,16,256]{2,1,0:T(8,128)}), f32[16,16,256]{2,1,0:T(8,128)S(1)}, u32[]{:S(2)}, u32[]{:S(2)}) async-start(f32[16,16,256]{2,1,0:T(8,128)} %weight_part.1), calls=%async_computation.4 | async-start | bytes 524288 | tf_op jit(solution)/shard_map/all_to_all | solution.py:348
  134.1 6.4 %backward_tiles.1 = bf16[16,128,256]{2,1,0:T(8,128)(2,1)} custom-call(s32[128]{0:T(128)S(1)} %get-tuple-element.28.by_col_ref, s32[384]{0:T(512)S(1)} %get-tuple-element.29.more_ref, s32[96]{0:T(128)S(1)} %get-tuple-element.30.more_cols_ref, s32[1]{0:T(128)} %get-tuple-element.31.total_ref, s32[97]{0:T(128)S(1)} %get-tuple-element.32.rows_ref, ...), custom_call_target="tpu_custom_call" | custom-call | flops 1073741824 | bytes 3178496 | tf_op jit(solution)/shard_map/backward_tiles/pallas_call | solution.py:278
  140.5 3.4 %all-to-all-done.4 = f32[16,16,256]{2,1,0:T(8,128)S(1)} async-done(((f32[16,16,256]{2,1,0:T(8,128)}), f32[16,16,256]{2,1,0:T(8,128)S(1)}, u32[]{:S(2)}, u32[]{:S(2)}) %all-to-all-start.4) | async-done | bytes 262176 | tf_op jit(solution)/shard_map/all_to_all | solution.py:348
  144.0 5.4 %all-to-all-start.3 = ((bf16[16,128,256]{2,1,0:T(8,128)(2,1)}), bf16[16,128,256]{2,1,0:T(8,128)(2,1)S(1)}, u32[]{:S(2)}, u32[]{:S(2)}) async-start(bf16[16,128,256]{2,1,0:T(8,128)(2,1)} %backward_tiles.1), calls=%async_computation.3 | async-start | bytes 2097152 | tf_op jit(solution)/shard_map/all_to_all | solution.py:350
  149.4 1.9 %collective-permute-start.2 = (f32[16,256]{1,0:T(8,128)S(1)}, f32[16,256]{1,0:T(8,128)S(1)}, u32[]{:S(2)}, u32[]{:S(2)}) collective-permute-start(f32[16,256]{1,0:T(8,128)S(1)} %broadcast_multiply_fusion), channel_id=1, source_target_pairs={{0,1},{1,0},{2,3},{3,2},{4,5},{5,4},{6,7},{7,6},{8,9},{9,8},{10,11... | collective-permute-start | bytes 49160 | tf_op jit(solution)/shard_map/ppermute | solution.py:309
  151.3 1.1 collective-permute-done.2
  152.5 2.5 %collective-permute-start.3 = (f32[1,16,256]{2,1,0:T(8,128)S(1)}, f32[1,16,256]{2,1,0:T(8,128)S(1)}, u32[]{:S(2)}, u32[]{:S(2)}) collective-permute-start(f32[1,16,256]{2,1,0:T(8,128)S(1)} %add_bitcast_fusion), channel_id=1, source_target_pairs={{0,2},{1,3},{2,0},{3,1},{4,6},{5,7},{6,4},{7,5},{8,10},{9,11},{10,... | collective-permute-start | bytes 49160 | tf_op jit(solution)/shard_map/ppermute | solution.py:313
  155.0 4.7 %collective-permute-done.3 = f32[1,16,256]{2,1,0:T(8,128)S(1)} collective-permute-done((f32[1,16,256]{2,1,0:T(8,128)S(1)}, f32[1,16,256]{2,1,0:T(8,128)S(1)}, u32[]{:S(2)}, u32[]{:S(2)}) %collective-permute-start.3) | collective-permute-done | bytes 16416 | tf_op jit(solution)/shard_map/ppermute | solution.py:313
  159.7 2.3 %collective-permute-start.4 = (f32[2,16,256]{2,1,0:T(8,128)S(1)}, f32[2,16,256]{2,1,0:T(8,128)S(1)}, u32[]{:S(2)}, u32[]{:S(2)}) collective-permute-start(f32[2,16,256]{2,1,0:T(8,128)S(1)} %maximum_select_fusion.3), channel_id=1, source_target_pairs={{0,4},{1,5},{2,6},{3,7},{4,0},{5,1},{6,2},{7,3},{8,12},{9,13},{10,... | collective-permute-start | bytes 98312 | tf_op jit(solution)/shard_map/ppermute | solution.py:313
  162.1 3.4 %collective-permute-done.4 = f32[2,16,256]{2,1,0:T(8,128)S(1)} collective-permute-done((f32[2,16,256]{2,1,0:T(8,128)S(1)}, f32[2,16,256]{2,1,0:T(8,128)S(1)}, u32[]{:S(2)}, u32[]{:S(2)}) %collective-permute-start.4) | collective-permute-done | bytes 32800 | tf_op jit(solution)/shard_map/ppermute | solution.py:313
  165.5 2.5 %collective-permute-start.5 = (f32[4,16,256]{2,1,0:T(8,128)S(1)}, f32[4,16,256]{2,1,0:T(8,128)S(1)}, u32[]{:S(2)}, u32[]{:S(2)}) collective-permute-start(f32[4,16,256]{2,1,0:T(8,128)S(1)} %maximum_select_fusion.2), channel_id=1, source_target_pairs={{0,8},{1,9},{2,10},{3,11},{4,12},{5,13},{6,14},{7,15},{8,0},{9,1},... | collective-permute-start | bytes 196616 | tf_op jit(solution)/shard_map/ppermute | solution.py:313
  168.1 5.1 %collective-permute-done.5 = f32[4,16,256]{2,1,0:T(8,128)S(1)} collective-permute-done((f32[4,16,256]{2,1,0:T(8,128)S(1)}, f32[4,16,256]{2,1,0:T(8,128)S(1)}, u32[]{:S(2)}, u32[]{:S(2)}) %collective-permute-start.5) | collective-permute-done | bytes 65568 | tf_op jit(solution)/shard_map/ppermute | solution.py:313
  173.1 2.0 %collective-permute-start.6 = (f32[8,16,256]{2,1,0:T(8,128)S(1)}, f32[8,16,256]{2,1,0:T(8,128)S(1)}, u32[]{:S(2)}, u32[]{:S(2)}) collective-permute-start(f32[8,16,256]{2,1,0:T(8,128)S(1)} %maximum_select_fusion.1), channel_id=1, source_target_pairs={{0,16},{1,17},{2,18},{3,19},{4,20},{5,21},{6,22},{7,23},{8,24},{9,... | collective-permute-start | bytes 393224 | tf_op jit(solution)/shard_map/ppermute | solution.py:313
  175.2 9.3 %collective-permute-done.6 = f32[8,16,256]{2,1,0:T(8,128)S(1)} collective-permute-done((f32[8,16,256]{2,1,0:T(8,128)S(1)}, f32[8,16,256]{2,1,0:T(8,128)S(1)}, u32[]{:S(2)}, u32[]{:S(2)}) %collective-permute-start.6) | collective-permute-done | bytes 131104 | tf_op jit(solution)/shard_map/ppermute | solution.py:313
  184.6 0.7 maximum_select_fusion
  185.3 0.0 all-to-all-done.3.parts_ref
  185.3 0.9 finish.1
  (15 shorter events, 0.1 us)
Async XLA Ops:
  0.6 14.4 %copy-start.4 = (s32[1,1,96]{2,1,0:T(1,128)S(1)}, s32[1,1,96]{2,1,0:T(1,128)}, u32[]{:S(2)}) copy-start(s32[1,1,96]{2,1,0:T(1,128)} %param.11) | copy-start | bytes 1156
  0.6 14.4 %copy-start.3 = (s32[1,1,96]{2,1,0:T(1,128)S(1)}, s32[1,1,96]{2,1,0:T(1,128)}, u32[]{:S(2)}) copy-start(s32[1,1,96]{2,1,0:T(1,128)} %param.10) | copy-start | bytes 1156
  2.6 37.5 %all-to-all-start = ((bf16[16,128,256]{2,1,0:T(8,128)(2,1)}), bf16[16,128,256]{2,1,0:T(8,128)(2,1)S(1)}, u32[]{:S(2)}, u32[]{:S(2)}) async-start(bf16[16,128,256]{2,1,0:T(8,128)(2,1)} %broadcast_in_dim.4), calls=%async_computation | async-start | bytes 2097152 | tf_op jit(solution)/shard_map/all_to_all | solution.py:335
  15.0 1.9 %copy-start = (bf16[1,1,96,128,128]{4,3,2,1,0:T(8,128)(2,1)S(1)}, bf16[1,1,96,128,128]{4,3,2,1,0:T(8,128)(2,1)}, u32[]{:S(2)}) copy-start(bf16[1,1,96,128,128]{4,3,2,1,0:T(8,128)(2,1)} %param.9) | copy-start | bytes 9437188
  45.5 4.6 %collective-permute-start = (bf16[16,128,256]{2,1,0:T(8,128)(2,1)S(1)}, bf16[16,128,256]{2,1,0:T(8,128)(2,1)S(1)}, u32[]{:S(2)}, u32[]{:S(2)}) collective-permute-start(bf16[16,128,256]{2,1,0:T(8,128)(2,1)S(1)} %get-tuple-element.26), channel_id=1, source_target_pairs={{0,1},{1,0},{2,3},{3,2},{4,5},{5,4},{6,7},{7,6},{8,9},{9,8},{10,11... | collective-permute-start | bytes 3145736 | tf_op jit(solution)/shard_map/ppermute | solution.py:341
  50.0 39.6 %copy-start.1 = (bf16[256,256]{1,0:T(8,128)(2,1)S(1)}, bf16[256,256]{1,0:T(8,128)(2,1)}, u32[]{:S(2)}) copy-start(bf16[256,256]{1,0:T(8,128)(2,1)} %weight_ref.3) | copy-start | bytes 393220
  50.0 39.6 %copy-start.2 = (bf16[128,256]{1,0:T(8,128)(2,1)S(1)}, bf16[128,256]{1,0:T(8,128)(2,1)}, u32[]{:S(2)}) copy-start(bf16[128,256]{1,0:T(8,128)(2,1)} %cotangent_ref.1) | copy-start | bytes 196612
  125.4 8.6 %collective-permute-start.1 = (bf16[16,136,256]{2,1,0:T(8,128)(2,1)S(1)}, bf16[16,136,256]{2,1,0:T(8,128)(2,1)S(1)}, u32[]{:S(2)}, u32[]{:S(2)}) collective-permute-start(bf16[16,136,256]{2,1,0:T(8,128)(2,1)S(1)} %all_to_all.26.mine_ref.message_ref), channel_id=1, source_target_pairs={{0,1},{1,0},{2,3},{3,2},{4,5},{5,4},{6,7},{7,6},{8,9},{9,8},{10,11... | collective-permute-start | bytes 3342344 | tf_op jit(solution)/shard_map/ppermute | solution.py:347
  128.3 15.6 %all-to-all-start.4 = ((f32[16,16,256]{2,1,0:T(8,128)}), f32[16,16,256]{2,1,0:T(8,128)S(1)}, u32[]{:S(2)}, u32[]{:S(2)}) async-start(f32[16,16,256]{2,1,0:T(8,128)} %weight_part.1), calls=%async_computation.4 | async-start | bytes 524288 | tf_op jit(solution)/shard_map/all_to_all | solution.py:348
  144.0 41.3 %all-to-all-start.3 = ((bf16[16,128,256]{2,1,0:T(8,128)(2,1)}), bf16[16,128,256]{2,1,0:T(8,128)(2,1)S(1)}, u32[]{:S(2)}, u32[]{:S(2)}) async-start(bf16[16,128,256]{2,1,0:T(8,128)(2,1)} %backward_tiles.1), calls=%async_computation.3 | async-start | bytes 2097152 | tf_op jit(solution)/shard_map/all_to_all | solution.py:350
  149.4 3.1 %collective-permute-start.2 = (f32[16,256]{1,0:T(8,128)S(1)}, f32[16,256]{1,0:T(8,128)S(1)}, u32[]{:S(2)}, u32[]{:S(2)}) collective-permute-start(f32[16,256]{1,0:T(8,128)S(1)} %broadcast_multiply_fusion), channel_id=1, source_target_pairs={{0,1},{1,0},{2,3},{3,2},{4,5},{5,4},{6,7},{7,6},{8,9},{9,8},{10,11... | collective-permute-start | bytes 49160 | tf_op jit(solution)/shard_map/ppermute | solution.py:309
  152.5 7.2 %collective-permute-start.3 = (f32[1,16,256]{2,1,0:T(8,128)S(1)}, f32[1,16,256]{2,1,0:T(8,128)S(1)}, u32[]{:S(2)}, u32[]{:S(2)}) collective-permute-start(f32[1,16,256]{2,1,0:T(8,128)S(1)} %add_bitcast_fusion), channel_id=1, source_target_pairs={{0,2},{1,3},{2,0},{3,1},{4,6},{5,7},{6,4},{7,5},{8,10},{9,11},{10,... | collective-permute-start | bytes 49160 | tf_op jit(solution)/shard_map/ppermute | solution.py:313
  159.7 5.8 %collective-permute-start.4 = (f32[2,16,256]{2,1,0:T(8,128)S(1)}, f32[2,16,256]{2,1,0:T(8,128)S(1)}, u32[]{:S(2)}, u32[]{:S(2)}) collective-permute-start(f32[2,16,256]{2,1,0:T(8,128)S(1)} %maximum_select_fusion.3), channel_id=1, source_target_pairs={{0,4},{1,5},{2,6},{3,7},{4,0},{5,1},{6,2},{7,3},{8,12},{9,13},{10,... | collective-permute-start | bytes 98312 | tf_op jit(solution)/shard_map/ppermute | solution.py:313
  165.5 7.6 %collective-permute-start.5 = (f32[4,16,256]{2,1,0:T(8,128)S(1)}, f32[4,16,256]{2,1,0:T(8,128)S(1)}, u32[]{:S(2)}, u32[]{:S(2)}) collective-permute-start(f32[4,16,256]{2,1,0:T(8,128)S(1)} %maximum_select_fusion.2), channel_id=1, source_target_pairs={{0,8},{1,9},{2,10},{3,11},{4,12},{5,13},{6,14},{7,15},{8,0},{9,1},... | collective-permute-start | bytes 196616 | tf_op jit(solution)/shard_map/ppermute | solution.py:313
  173.1 11.4 %collective-permute-start.6 = (f32[8,16,256]{2,1,0:T(8,128)S(1)}, f32[8,16,256]{2,1,0:T(8,128)S(1)}, u32[]{:S(2)}, u32[]{:S(2)}) collective-permute-start(f32[8,16,256]{2,1,0:T(8,128)S(1)} %maximum_select_fusion.1), channel_id=1, source_target_pairs={{0,16},{1,17},{2,18},{3,19},{4,20},{5,21},{6,22},{7,23},{8,24},{9,... | collective-permute-start | bytes 393224 | tf_op jit(solution)/shard_map/ppermute | solution.py:313

commit v3 on v2

v3 whole, which is shorter than its diff:
```python
import functools
import math

import jax
import jax.numpy as jnp
from jax import lax
from jax.experimental import pallas as pl
from jax.experimental.pallas import tpu as pltpu
from jax.sharding import PartitionSpec as P

bf16 = jnp.bfloat16
f32 = jnp.float32
i32 = jnp.int32
smem = pl.BlockSpec(memory_space=pltpu.SMEM)
vmem = pl.BlockSpec(memory_space=pltpu.VMEM)
quad = 4


def params(mib=16):
    return pltpu.CompilerParams(vmem_limit_bytes=mib * 1024 * 1024)


def cost(flops, moved):
    return pl.CostEstimate(flops=flops, bytes_accessed=moved, transcendentals=0)


def sort_slots(target_of, slots, count, base_ref, extra_ref, extra_ids_ref, total_ref, seen_ref, last_ref):
    zero_slot = slots
    size = quad
    targets = base_ref.shape[0] // size

    def clear_base(t, carry):
        base_ref[t] = zero_slot
        return carry

    def clear_extra(t, carry):
        extra_ref[t] = zero_slot
        return carry

    def clear_seen(t, carry):
        seen_ref[t] = 0
        return carry

    lax.fori_loop(0, base_ref.shape[0], clear_base, 0)
    lax.fori_loop(0, extra_ref.shape[0], clear_extra, 0)
    lax.fori_loop(0, targets, clear_seen, 0)
    total_ref[0] = 0

    def place(s, carry):
        target = target_of(s)
        seen = seen_ref[target]
        seen_ref[target] = seen + 1

        @pl.when(seen < size)
        def _():
            base_ref[target * size + seen] = s

        @pl.when(seen >= size)
        def _():
            over = seen % size

            @pl.when(over == 0)
            def _():
                group = total_ref[0]
                total_ref[0] = group + 1
                last_ref[target] = group
                extra_ids_ref[group] = 2 * target + (seen == size).astype(i32)

            extra_ref[last_ref[target] * size + over] = s

        return carry

    lax.fori_loop(0, count, place, 0)


def prepare_kernel(
    rows_ref, cols_ref, count_ref, core_ref, tiles_ref,
    fwd_ref, fwd_more_ref, fwd_more_ids_ref, fwd_total_ref, fwd_source_ref,
    bwd_ref, bwd_more_ref, bwd_more_ids_ref, bwd_total_ref, bwd_source_ref,
    flipped_ref, seen_ref, last_ref,
):
    slots = rows_ref.shape[0]
    count = count_ref[0]
    core = core_ref[0]
    half = fwd_ref.shape[0] // (2 * quad)

    def away(s):
        return (rows_ref[s] % 2 != core).astype(i32)

    def forward_target(s):
        return away(s) * half + rows_ref[s] // 2

    def backward_target(s):
        return away(s) * half + cols_ref[s]

    sort_slots(forward_target, slots, count, fwd_ref, fwd_more_ref, fwd_more_ids_ref, fwd_total_ref, seen_ref, last_ref)
    sort_slots(backward_target, slots, count, bwd_ref, bwd_more_ref, bwd_more_ids_ref, bwd_total_ref, seen_ref, last_ref)

    def sources(s, carry):
        fwd_source_ref[s] = cols_ref[s]
        bwd_source_ref[s] = rows_ref[s] // 2
        return carry

    lax.fori_loop(0, slots, sources, 0)
    fwd_source_ref[slots] = 0
    bwd_source_ref[slots] = 0

    def turn(s, carry):
        flipped_ref[s] = tiles_ref[s].T
        return carry

    lax.fori_loop(0, slots, turn, 0, unroll=4)
    flipped_ref[slots] = jnp.zeros(flipped_ref.shape[1:], bf16)


def prepare(rows_ids, cols_ids, count, core, tiles, targets):
    slots, block, _ = tiles.shape
    ints = lambda size: jax.ShapeDtypeStruct((size,), i32)
    held = jax.ShapeDtypeStruct((slots + 1, block, block), bf16)
    lists = (ints(targets * quad), ints(slots * quad), ints(slots), ints(1), ints(slots + 1))
    return pl.pallas_call(
        prepare_kernel,
        out_shape=(*lists, *lists, held),
        in_specs=[smem] * 4 + [vmem],
        out_specs=(smem,) * 10 + (vmem,),
        scratch_shapes=[pltpu.SMEM((targets,), i32)] * 2,
        compiler_params=params(24),
        cost_estimate=cost(0, 9 * slots * block * block * 2),
        name="prepare",
    )(rows_ids, cols_ids, count, core, tiles)


def grouped_product(tiles_ref, ids_ref, source_ref, list_ref, group):
    slots = [list_ref[group * quad + k] for k in range(quad)]
    block = tiles_ref.shape[1]
    held = tiles_ref.shape[0]
    if held == ids_ref.shape[0]:
        parts = [tiles_ref[s] for s in slots]
    else:
        parts = [tiles_ref[jnp.minimum(s, held - 1)] for s in slots]
        parts = [jnp.where(s < held, part, jnp.zeros_like(part)) for s, part in zip(slots, parts)]
    left = jnp.concatenate(parts, axis=1)
    right = jnp.concatenate([source_ref[ids_ref[s], :block, :] for s in slots], axis=0)
    return jnp.dot(left, right, preferred_element_type=f32)


def further_groups(lists, tiles_ref, source_ref, acc_ref, first, targets, store):
    list_ref, more_ref, more_ids_ref, total_ref, ids_ref = lists

    def more(t, carry):
        code = more_ids_ref[t]
        target = code // 2
        place = target - first

        @pl.when((place >= 0) & (place < targets))
        def _():
            @pl.when(code % 2 == 1)
            def _():
                acc_ref[place] = grouped_product(tiles_ref, ids_ref, source_ref, list_ref, target)

            acc_ref[place] += grouped_product(tiles_ref, ids_ref, source_ref, more_ref, t)
            store(place)

        return carry

    lax.fori_loop(0, total_ref[0], more, 0)


def forward_kernel(part, *refs):
    lists = refs[:5]
    panel_ref, tiles_ref, out_ref, acc_ref = refs[5:]
    half = out_ref.shape[0]

    def base(t, carry):
        product = grouped_product(tiles_ref, lists[4], panel_ref, lists[0], part * half + t)
        out_ref[t] = product.astype(bf16)
        return carry

    lax.fori_loop(0, half, base, 0, unroll=4)

    def store(place):
        out_ref[place] = acc_ref[place].astype(bf16)

    further_groups(lists, tiles_ref, panel_ref, acc_ref, part * half, half, store)


def forward_tiles(part, lists, panel, tiles):
    block, width = panel.shape[1:]
    shape = (lists[0].shape[0] // (2 * quad), block, width)
    return pl.pallas_call(
        functools.partial(forward_kernel, part),
        out_shape=jax.ShapeDtypeStruct(shape, bf16),
        in_specs=[smem] * 5 + [vmem] * 2,
        out_specs=vmem,
        scratch_shapes=[pltpu.VMEM(shape, f32)],
        compiler_params=params(),
        cost_estimate=cost(2 * shape[0] * quad * block * block * width, tiles.size),
        name="forward_tiles_%d" % part,
    )(*lists, panel, tiles)


def spread_kernel(in_ref, out_ref):
    for k in range(out_ref.shape[0]):
        out_ref[k] = in_ref[...]


def spread(shard, copies):
    return pl.pallas_call(
        spread_kernel,
        out_shape=pltpu.VMEM((copies,) + shard.shape, shard.dtype),
        in_specs=[vmem],
        out_specs=vmem,
        compiler_params=params(),
        name="spread",
    )(shard)


def sum_parts(ref):
    total = ref[0].astype(f32)
    for k in range(1, ref.shape[0]):
        total += ref[k].astype(f32)
    return total


def dense_kernel(parts_ref, weight_ref, cotangent_ref, act_ref, message_ref):
    aggregated = sum_parts(parts_ref)
    aggregated_half = aggregated.astype(bf16)
    preact = jnp.dot(aggregated_half, weight_ref[...], preferred_element_type=f32)
    scale = math.sqrt(2 / math.pi)
    square = preact * preact
    tanh = jnp.tanh(scale * (preact + 0.044715 * (square * preact)))
    act_ref[...] = (0.5 * preact * (1.0 + tanh)).astype(bf16)
    slope = 0.5 * (1.0 + tanh) + (0.5 * preact) * (1.0 - tanh * tanh) * (
        scale * (1.0 + (3 * 0.044715) * square)
    )
    grad_pre = (cotangent_ref[...].astype(f32) * slope).astype(bf16)
    turned = aggregated_half.astype(f32).T
    peers = message_ref.shape[0]
    rows = grad_pre.shape[0]
    own = 2 * turned.shape[0] // peers
    for k in range(peers):
        message_ref[k, :rows, :] = grad_pre
        first = (k // 2) * own
        low = turned[first : first + own // 2]
        high = turned[first + own // 2 : first + own]
        message_ref[k, rows:, :] = jnp.concatenate([low, high], axis=1).astype(bf16)


def dense(parts, weight, cotangent):
    rows, width = cotangent.shape
    peers = parts.shape[0]
    return pl.pallas_call(
        dense_kernel,
        out_shape=(
            jax.ShapeDtypeStruct((rows, width), bf16),
            jax.ShapeDtypeStruct((peers, rows + width // peers, width), bf16),
        ),
        in_specs=[vmem] * 3,
        out_specs=(vmem,) * 2,
        compiler_params=params(),
        name="dense",
    )(parts, weight, cotangent)


def weight_kernel(mine_ref, out_ref):
    peers, _, width = mine_ref.shape
    rows = width // 2
    total = None
    for k in range(0, peers, 2):
        left = []
        for p in (k, k + 1):
            packed = mine_ref[p, rows:, :].astype(f32)
            left.append(jnp.concatenate([packed[:, :rows], packed[:, rows:]], axis=0))
        left = jnp.concatenate(left, axis=1).astype(bf16)
        right = jnp.concatenate([mine_ref[k, :rows, :], mine_ref[k + 1, :rows, :]], axis=0)
        term = jnp.dot(left, right, preferred_element_type=f32)
        total = term if total is None else total + term
    rounded = total.astype(bf16)
    for k in range(out_ref.shape[0]):
        out_ref[k] = rounded


def weight_part(mine, copies):
    peers, _, width = mine.shape
    return pl.pallas_call(
        weight_kernel,
        out_shape=jax.ShapeDtypeStruct((copies, 2 * width // peers, width), bf16),
        in_specs=[vmem],
        out_specs=vmem,
        compiler_params=params(),
        cost_estimate=cost(0, mine.size),
        name="weight_part",
    )(mine)


def weight_sum_kernel(scale, parts_ref, out_ref):
    out_ref[...] = sum_parts(parts_ref) * scale


def weight_sum(parts, scale):
    return pl.pallas_call(
        functools.partial(weight_sum_kernel, scale),
        out_shape=jax.ShapeDtypeStruct(parts.shape[1:], f32),
        in_specs=[vmem],
        out_specs=vmem,
        compiler_params=params(),
        cost_estimate=cost(0, parts.size),
        name="weight_sum",
    )(parts)


def gather_over_col(rows, position, size):
    held = (rows + lax.ppermute(rows, "col", [(i, i ^ 1) for i in range(size)]))[None]
    steps = (size // 2, size // 4, size // 8)
    for distance in steps:
        came = lax.ppermute(held, "col", [(i, i ^ distance) for i in range(size)])
        if distance == steps[-1]:
            return held, came
        upper = (position // distance) % 2 == 1
        held = jnp.where(upper, jnp.concatenate([came, held]), jnp.concatenate([held, came]))


def backward_kernel(*refs):
    *refs, held_ref, held_sem = refs
    tiles_copy = pltpu.make_async_copy(refs[7], held_ref, held_sem)
    tiles_copy.start()
    tiles_copy.wait()
    lists = refs[:5]
    list_ref, more_ref, more_ids_ref, total_ref, ids_ref = lists
    mine_ref, other_ref, _, out_ref, acc_ref = refs[5:]
    tiles_ref = held_ref
    targets = out_ref.shape[0]

    def base(t, carry):
        product = grouped_product(tiles_ref, ids_ref, mine_ref, list_ref, t)
        product += grouped_product(tiles_ref, ids_ref, other_ref, list_ref, targets + t)
        acc_ref[t] = product
        out_ref[t] = product.astype(bf16)
        return carry

    lax.fori_loop(0, targets, base, 0, unroll=4)

    def more(t, carry):
        target = more_ids_ref[t] // 2
        place = target % targets

        @pl.when(target < targets)
        def _():
            acc_ref[place] += grouped_product(tiles_ref, ids_ref, mine_ref, more_ref, t)

        @pl.when(target >= targets)
        def _():
            acc_ref[place] += grouped_product(tiles_ref, ids_ref, other_ref, more_ref, t)

        out_ref[place] = acc_ref[place].astype(bf16)
        return carry

    lax.fori_loop(0, total_ref[0], more, 0)


def backward_tiles(lists, mine, other, tiles):
    width = mine.shape[-1]
    block = tiles.shape[-1]
    shape = (lists[0].shape[0] // (2 * quad), block, width)
    return pl.pallas_call(
        backward_kernel,
        out_shape=jax.ShapeDtypeStruct(shape, bf16),
        in_specs=[smem] * 5 + [vmem] * 2 + [pl.BlockSpec(memory_space=pltpu.HBM)],
        out_specs=vmem,
        scratch_shapes=[pltpu.VMEM(shape, f32), pltpu.VMEM(tiles.shape, bf16), pltpu.SemaphoreType.DMA],
        compiler_params=params(),
        cost_estimate=cost(4 * shape[0] * quad * block * block * width, tiles.size),
        name="backward_tiles",
    )(*lists, mine, other, pltpu.with_memory_space_constraint(tiles, pltpu.HBM))


def finish_kernel(upper_ref, parts_ref, weight_ref, held_ref, came_ref, out_ref, weight_out_ref):
    out_ref[...] = lax.dot_general(
        sum_parts(parts_ref).astype(bf16), weight_ref[...], (((1,), (1,)), ((), ())), preferred_element_type=f32
    ).astype(bf16)
    upper = upper_ref[0] == 1
    chunks, own, _ = held_ref.shape
    for k in range(2 * chunks):
        bits = [(k >> b) & 1 for b in range(3)]
        place = bits[1] * 2 + bits[2]
        held, came = held_ref[place], came_ref[place]
        low, high = (held, came) if bits[0] == 0 else (came, held)
        weight_out_ref[k * own : (k + 1) * own, :] = jnp.where(upper, high, low)


def finish(upper, parts, weight, held, came):
    return pl.pallas_call(
        finish_kernel,
        out_shape=(jax.ShapeDtypeStruct(parts.shape[1:], bf16), jax.ShapeDtypeStruct(weight.shape, f32)),
        in_specs=[smem] + [vmem] * 4,
        out_specs=(vmem,) * 2,
        compiler_params=params(),
        name="finish",
    )(upper, parts, weight, held, came)


def local(features, weight, block_values, block_rows, block_cols, counts, cotangent):
    rows_dev, width = features.shape
    row_count = lax.axis_size("row")
    col_count = lax.axis_size("col")
    node_total = rows_dev * row_count * col_count
    half = col_count // 2
    pairs = [(i, i ^ 1) for i in range(col_count)]
    groups = [[2 * k + c for k in range(half)] for c in range(2)]
    position = lax.axis_index("col").astype(i32)
    core = jnp.reshape(position % 2, (1,))
    tiles = block_values[0, 0]

    panel = lax.all_to_all(spread(features, row_count), "row", 0, 0)
    made = prepare(block_rows[0, 0], block_cols[0, 0], counts[0], core, tiles, col_count)
    forward_lists, (*backward_lists, backward_ids), flipped = made[:5], made[5:10], made[10]

    send = forward_tiles(1, forward_lists, panel, tiles)
    came = lax.ppermute(send, "col", pairs)
    keep = forward_tiles(0, forward_lists, panel, tiles)
    summed = (keep.astype(f32) + came.astype(f32)).astype(bf16)
    parts = lax.all_to_all(summed, "col", 0, 0, axis_index_groups=groups)
    activations, messages = dense(parts, weight, cotangent)

    mine = lax.all_to_all(messages, "col", 0, 0, axis_index_groups=groups)
    other = lax.ppermute(mine, "col", pairs)
    weight_rows, backward_ids = lax.optimization_barrier((weight_part(mine, row_count), backward_ids))
    weight_parts = lax.all_to_all(weight_rows, "row", 0, 0)
    back = backward_tiles((*backward_lists, backward_ids), mine, other, flipped)
    back_parts = lax.all_to_all(back, "row", 0, 0)
    weight_rows = weight_sum(weight_parts, 1.0 / math.sqrt(node_total))
    held, came = gather_over_col(weight_rows, position, col_count)
    upper = jnp.reshape((position // (col_count // 8)) % 2, (1,))
    feature_grad, weight_grad = finish(upper, back_parts, weight, held, came)
    return (activations, feature_grad, weight_grad)


def solution(mesh):
    in_specs = (
        P(("col", "row"), None),
        P(),
        P("row", "col", None, None, None),
        P("row", "col", None),
        P("row", "col", None),
        P("row", "col"),
        P(("row", "col"), None),
    )
    out_specs = (P(("row", "col"), None), P(("col", "row"), None), P())
    return jax.shard_map(local, mesh=mesh, in_specs=in_specs, out_specs=out_specs, check_vma=False)
```

time: 187 us -> 180 us (0.963)
  Pallas kernels: 33.2 us -> 27.2 us
  blocking collectives: 74.1 us -> 76.2 us
    all_to_all x2, waiting for transfers between devices: 8.01 us -> 15.5 us  [the longest x1 11.4 us: local(): panel = lax.all_to_all(spread(features, row_count), 'row', 0, 0)]
    pallas_call x5 -> x8, Pallas kernels: 32.3 us -> 26.3 us  [the longest x1 12.1 us: prepare(): pl.pallas_call(prepare_kernel, out_shape=(*lists, *lists, held), in_specs...]
    ppermute x4 -> x3, waiting for transfers between devices: 22.6 us -> 17 us  [gather_over_col(): came = lax.ppermute(held, 'col', [(i, i ^ distance) for i in range(size)])]
    ppermute x1, waiting for transfers between devices: 2.63 us -> 0.01 us  [local(): came = lax.ppermute(send, 'col', pairs)]
    ppermute x4 -> x3, starting transfers between devices: 9.35 us -> 6.92 us  [gather_over_col(): came = lax.ppermute(held, 'col', [(i, i ^ distance) for i in range(size)])]
    broadcast_in_dim x1 -> x0, local copies, waits for them, and re-layouts: 1.93 us -> none  [local(): copies = jnp.broadcast_to(features[None], (row_count,) + features.shape)]
  transfers between devices with their start and end apart: 10 -> 9, of which waited for: 8 -> 6; matrix products, arithmetic and copies ran while one was open for 0% -> 0% of each run, Pallas kernels for 14% -> 12%
where the time goes in v3:
time: 180 us; the launch traced here: 179 us
  blocking collectives  76.2 us (42%)
  starting transfers between devices  36.3 us (20%)
  waiting for transfers between devices  33.7 us (19%)
  Pallas kernels  27.2 us (15%)
  local copies, waits for them, and re-layouts  3.65 us (2%)
    all_to_all x1, blocking collectives, local(): parts = lax.all_to_all(summed, 'col', 0, 0, axis_index_groups=groups)  40.3 us
    all_to_all x1, blocking collectives, local(): mine = lax.all_to_all(messages, 'col', 0, 0, axis_index_groups=groups)  35.9 us
    ppermute x3, waiting for transfers between devices, gather_over_col(): came = lax.ppermute(held, 'col', [(i, i ^ distance) for i in range(size)])  17 us
    pallas_call x1, Pallas kernels, prepare(): pl.pallas_call(prepare_kernel, out_shape=(*lists, *lists, held), in_specs...  12.1 us
    all_to_all x1, starting transfers between devices, local(): panel = lax.all_to_all(spread(features, row_count), 'row', 0, 0)  11.8 us
    all_to_all x1, waiting for transfers between devices, local(): panel = lax.all_to_all(spread(features, row_count), 'row', 0, 0)  11.4 us
    ppermute x3, starting transfers between devices, gather_over_col(): came = lax.ppermute(held, 'col', [(i, i ^ distance) for i in range(size)])  6.92 us
    all_to_all x1, starting transfers between devices, local(): weight_parts = lax.all_to_all(weight_rows, 'row', 0, 0)  6.42 us
  transfers between devices with their start and end apart: 9, of which 6 were waited for; matrix products, arithmetic and copies ran while one was open for 0% of the time, Pallas kernels for 12%

profile of v3, /device:TPU:2, one launch (start us, length us, event | category | flops | bytes accessed | tf_op | source)
XLA Modules:
  0.0 178.9 jit_solution(4418332700564579232)
XLA Ops:
  0.7 1.0 copy-done.4
  1.6 0.1 spread.1
  1.7 1.0 copy-done.1
  2.7 11.8 %all-to-all-start = ((bf16[16,128,256]{2,1,0:T(8,128)(2,1)}), bf16[16,128,256]{2,1,0:T(8,128)(2,1)}, u32[]{:S(2)}, u32[]{:S(2)}) async-start(bf16[16,128,256]{2,1,0:T(8,128)(2,1)} %copy-done.1), calls=%async_computation | async-start | bytes 2097152 | tf_op jit(solution)/shard_map/all_to_all | solution.py:414
  15.2 12.1 %prepare.1 = (s32[128]{0:T(128)S(1)}, s32[384]{0:T(512)S(1)}, s32[96]{0:T(128)S(1)}, s32[1]{0:T(128)}, s32[97]{0:T(128)S(1)}, /*index=5*/s32[128]{0:T(128)S(1)},...) custom-call(s32[96]{0:T(128)S(1)} %bitcast.12, ...), custom_call_target="tpu_custom_call" | custom-call | bytes 28311552 | tf_op jit(solution)/shard_map/prepare/pallas_call | solution.py:121
  27.3 1.6 copy-done.2
  28.9 11.4 %all-to-all-done.refs_5_ = bf16[16,128,256]{2,1,0:T(8,128)(2,1)} async-done(((bf16[16,128,256]{2,1,0:T(8,128)(2,1)}), bf16[16,128,256]{2,1,0:T(8,128)(2,1)}, u32[]{:S(2)}, u32[]{:S(2)}) %all-to-all-start) | async-done | bytes 1048608 | tf_op jit(solution)/shard_map/all_to_all | solution.py:414
  40.4 3.1 %forward_tiles_1.1 = bf16[16,128,256]{2,1,0:T(8,128)(2,1)S(1)} custom-call(s32[128]{0:T(128)S(1)} %get-tuple-element.20.refs_0_, s32[384]{0:T(512)S(1)} %get-tuple-element.21.refs_1_, s32[96]{0:T(128)S(1)} %get-tuple-element.22.refs_2_, s32[1]{0:T(128)} %get-tuple-element.23.refs_3_, s32[97]{0:T(128)S(1)} %get-tuple-element.24.refs_4_, ...), custom_call_target="tpu_custom_call" | custom-call | flops 536870912 | bytes 1572864 | tf_op jit(solution)/shard_map/forward_tiles_1/pallas_call | solution.py:190
  43.5 1.9 %collective-permute-start = (bf16[16,128,256]{2,1,0:T(8,128)(2,1)S(1)}, bf16[16,128,256]{2,1,0:T(8,128)(2,1)S(1)}, u32[]{:S(2)}, u32[]{:S(2)}) collective-permute-start(bf16[16,128,256]{2,1,0:T(8,128)(2,1)S(1)} %forward_tiles_1.1), channel_id=1, source_target_pairs={{0,1},{1,0},{2,3},{3,2},{4,5},{5,4},{6,7},{7,6},{8,9},{9,8},{10,11... | collective-permute-start | bytes 3145736 | tf_op jit(solution)/shard_map/ppermute | solution.py:419
  45.4 3.1 %forward_tiles_0.1 = bf16[16,128,256]{2,1,0:T(8,128)(2,1)S(1)} custom-call(s32[128]{0:T(128)S(1)} %get-tuple-element.20.refs_0_, s32[384]{0:T(512)S(1)} %get-tuple-element.21.refs_1_, s32[96]{0:T(128)S(1)} %get-tuple-element.22.refs_2_, s32[1]{0:T(128)} %get-tuple-element.23.refs_3_, s32[97]{0:T(128)S(1)} %get-tuple-element.24.refs_4_, ...), custom_call_target="tpu_custom_call" | custom-call | flops 536870912 | bytes 1572864 | tf_op jit(solution)/shard_map/forward_tiles_0/pallas_call | solution.py:190
  48.6 0.0 copy-start.3
  48.6 0.0 copy-start.5
  48.6 0.0 collective-permute-done
  48.6 0.3 add_convert_fusion
  49.0 40.3 %all_to_all.25.parts_ref = bf16[16,128,256]{2,1,0:T(8,128)(2,1)S(1)} all-to-all(bf16[16,128,256]{2,1,0:T(8,128)(2,1)S(1)} %add_convert_fusion), channel_id=1, replica_groups={{0,2,4,6,8,10,12,14,16,18,20,22,24,26,28,30},{1,3,5,7,9,11,13,15,17,19,..., dimensions={0} | all-to-all | bytes 2097152 | tf_op jit(solution)/shard_map/all_to_all | solution.py:422
  89.2 0.9 dense.1
  90.2 35.9 %all_to_all.26.mine_ref.refs_5_ = bf16[16,144,256]{2,1,0:T(8,128)(2,1)S(1)} all-to-all(bf16[16,144,256]{2,1,0:T(8,128)(2,1)S(1)} %get-tuple-element.30), channel_id=1, replica_groups={{0,2,4,6,8,10,12,14,16,18,20,22,24,26,28,30},{1,3,5,7,9,11,13,15,17,19,..., dimensions={0} | all-to-all | bytes 2359296 | tf_op jit(solution)/shard_map/all_to_all | solution.py:425
  126.1 1.9 %collective-permute-start.1 = (bf16[16,144,256]{2,1,0:T(8,128)(2,1)S(1)}, bf16[16,144,256]{2,1,0:T(8,128)(2,1)S(1)}, u32[]{:S(2)}, u32[]{:S(2)}) collective-permute-start(bf16[16,144,256]{2,1,0:T(8,128)(2,1)S(1)} %all_to_all.26.mine_ref.refs_5_), channel_id=1, source_target_pairs={{0,1},{1,0},{2,3},{3,2},{4,5},{5,4},{6,7},{7,6},{8,9},{9,8},{10,11... | collective-permute-start | bytes 3538952 | tf_op jit(solution)/shard_map/ppermute | solution.py:426
  128.0 1.0 weight_part.1
  129.0 6.4 %all-to-all-start.4 = ((bf16[16,32,256]{2,1,0:T(8,128)(2,1)}), bf16[16,32,256]{2,1,0:T(8,128)(2,1)S(1)}, u32[]{:S(2)}, u32[]{:S(2)}) async-start(bf16[16,32,256]{2,1,0:T(8,128)(2,1)} %weight_part.1), calls=%async_computation.4 | async-start | bytes 524288 | tf_op jit(solution)/shard_map/all_to_all | solution.py:428
  135.4 5.9 %backward_tiles.1 = bf16[16,128,256]{2,1,0:T(8,128)(2,1)} custom-call(s32[128]{0:T(128)S(1)} %get-tuple-element.26.refs_0_, s32[384]{0:T(512)S(1)} %get-tuple-element.27.refs_1_, s32[96]{0:T(128)S(1)} %get-tuple-element.28.refs_2_, s32[1]{0:T(128)} %get-tuple-element.29.refs_3_, s32[97]{0:T(128)S(1)} %get-tuple-element.32.refs_4_, ...), custom_call_target="tpu_custom_call" | custom-call | flops 1073741824 | bytes 1589248 | tf_op jit(solution)/shard_map/backward_tiles/pallas_call | solution.py:365
  141.3 4.0 %all-to-all-done.4.parts_ref = bf16[16,32,256]{2,1,0:T(8,128)(2,1)S(1)} async-done(((bf16[16,32,256]{2,1,0:T(8,128)(2,1)}), bf16[16,32,256]{2,1,0:T(8,128)(2,1)S(1)}, u32[]{:S(2)}, u32[]{:S(2)}) %all-to-all-start.4) | async-done | bytes 262176 | tf_op jit(solution)/shard_map/all_to_all | solution.py:428
  145.3 5.4 %all-to-all-start.3 = ((bf16[16,128,256]{2,1,0:T(8,128)(2,1)}), bf16[16,128,256]{2,1,0:T(8,128)(2,1)S(1)}, u32[]{:S(2)}, u32[]{:S(2)}) async-start(bf16[16,128,256]{2,1,0:T(8,128)(2,1)} %backward_tiles.1), calls=%async_computation.3 | async-start | bytes 2097152 | tf_op jit(solution)/shard_map/all_to_all | solution.py:430
  150.8 1.9 %collective-permute-start.2 = (f32[32,256]{1,0:T(8,128)S(1)}, f32[32,256]{1,0:T(8,128)S(1)}, u32[]{:S(2)}, u32[]{:S(2)}) collective-permute-start(f32[32,256]{1,0:T(8,128)S(1)} %weight_sum.1), channel_id=1, source_target_pairs={{0,1},{1,0},{2,3},{3,2},{4,5},{5,4},{6,7},{7,6},{8,9},{9,8},{10,11... | collective-permute-start | bytes 98312 | tf_op jit(solution)/shard_map/ppermute | solution.py:313
  152.7 1.2 collective-permute-done.2
  153.9 2.6 %collective-permute-start.3 = (f32[1,32,256]{2,1,0:T(8,128)S(1)}, f32[1,32,256]{2,1,0:T(8,128)S(1)}, u32[]{:S(2)}, u32[]{:S(2)}) collective-permute-start(f32[1,32,256]{2,1,0:T(8,128)S(1)} %add_bitcast_fusion), channel_id=1, source_target_pairs={{0,16},{1,17},{2,18},{3,19},{4,20},{5,21},{6,22},{7,23},{8,24},{9,... | collective-permute-start | bytes 98312 | tf_op jit(solution)/shard_map/ppermute | solution.py:316
  156.5 7.1 %collective-permute-done.3 = f32[1,32,256]{2,1,0:T(8,128)S(1)} collective-permute-done((f32[1,32,256]{2,1,0:T(8,128)S(1)}, f32[1,32,256]{2,1,0:T(8,128)S(1)}, u32[]{:S(2)}, u32[]{:S(2)}) %collective-permute-start.3) | collective-permute-done | bytes 32800 | tf_op jit(solution)/shard_map/ppermute | solution.py:316
  163.7 2.4 %collective-permute-start.4 = (f32[2,32,256]{2,1,0:T(8,128)S(1)}, f32[2,32,256]{2,1,0:T(8,128)S(1)}, u32[]{:S(2)}, u32[]{:S(2)}) collective-permute-start(f32[2,32,256]{2,1,0:T(8,128)S(1)} %maximum_select_fusion.1), channel_id=1, source_target_pairs={{0,8},{1,9},{2,10},{3,11},{4,12},{5,13},{6,14},{7,15},{8,0},{9,1},... | collective-permute-start | bytes 196616 | tf_op jit(solution)/shard_map/ppermute | solution.py:316
  166.1 5.0 %collective-permute-done.4 = f32[2,32,256]{2,1,0:T(8,128)S(1)} collective-permute-done((f32[2,32,256]{2,1,0:T(8,128)S(1)}, f32[2,32,256]{2,1,0:T(8,128)S(1)}, u32[]{:S(2)}, u32[]{:S(2)}) %collective-permute-start.4) | collective-permute-done | bytes 65568 | tf_op jit(solution)/shard_map/ppermute | solution.py:316
  171.1 1.9 %collective-permute-start.5 = (f32[4,32,256]{2,1,0:T(8,128)S(1)}, f32[4,32,256]{2,1,0:T(8,128)S(1)}, u32[]{:S(2)}, u32[]{:S(2)}) collective-permute-start(f32[4,32,256]{2,1,0:T(8,128)S(1)} %maximum_select_fusion.held_ref), channel_id=1, source_target_pairs={{0,4},{1,5},{2,6},{3,7},{4,0},{5,1},{6,2},{7,3},{8,12},{9,13},{10,... | collective-permute-start | bytes 393224 | tf_op jit(solution)/shard_map/ppermute | solution.py:316
  173.0 4.9 %collective-permute-done.5.came_ref = f32[4,32,256]{2,1,0:T(8,128)S(1)} collective-permute-done((f32[4,32,256]{2,1,0:T(8,128)S(1)}, f32[4,32,256]{2,1,0:T(8,128)S(1)}, u32[]{:S(2)}, u32[]{:S(2)}) %collective-permute-start.5) | collective-permute-done | bytes 131104 | tf_op jit(solution)/shard_map/ppermute | solution.py:316
  178.0 0.9 finish.1
  (17 shorter events, 0.1 us)
Async XLA Ops:
  0.6 14.5 %copy-start = (bf16[1,1,96,128,128]{4,3,2,1,0:T(8,128)(2,1)S(1)}, bf16[1,1,96,128,128]{4,3,2,1,0:T(8,128)(2,1)}, u32[]{:S(2)}) copy-start(bf16[1,1,96,128,128]{4,3,2,1,0:T(8,128)(2,1)} %param.9) | copy-start | bytes 9437188
  0.6 1.0 copy-start.4
  1.6 13.5 %copy-start.6 = (s32[1,1,96]{2,1,0:T(1,128)S(1)}, s32[1,1,96]{2,1,0:T(1,128)}, u32[]{:S(2)}) copy-start(s32[1,1,96]{2,1,0:T(1,128)} %param.10) | copy-start | bytes 1156
  1.6 13.6 %copy-start.7 = (s32[1,1,96]{2,1,0:T(1,128)S(1)}, s32[1,1,96]{2,1,0:T(1,128)}, u32[]{:S(2)}) copy-start(s32[1,1,96]{2,1,0:T(1,128)} %param.11) | copy-start | bytes 1156
  1.7 1.0 copy-start.1
  2.7 37.7 %all-to-all-start = ((bf16[16,128,256]{2,1,0:T(8,128)(2,1)}), bf16[16,128,256]{2,1,0:T(8,128)(2,1)}, u32[]{:S(2)}, u32[]{:S(2)}) async-start(bf16[16,128,256]{2,1,0:T(8,128)(2,1)} %copy-done.1), calls=%async_computation | async-start | bytes 2097152 | tf_op jit(solution)/shard_map/all_to_all | solution.py:414
  27.3 1.6 copy-start.2
  43.5 5.1 %collective-permute-start = (bf16[16,128,256]{2,1,0:T(8,128)(2,1)S(1)}, bf16[16,128,256]{2,1,0:T(8,128)(2,1)S(1)}, u32[]{:S(2)}, u32[]{:S(2)}) collective-permute-start(bf16[16,128,256]{2,1,0:T(8,128)(2,1)S(1)} %forward_tiles_1.1), channel_id=1, source_target_pairs={{0,1},{1,0},{2,3},{3,2},{4,5},{5,4},{6,7},{7,6},{8,9},{9,8},{10,11... | collective-permute-start | bytes 3145736 | tf_op jit(solution)/shard_map/ppermute | solution.py:419
  48.6 40.6 %copy-start.3 = (bf16[256,256]{1,0:T(8,128)(2,1)S(1)}, bf16[256,256]{1,0:T(8,128)(2,1)}, u32[]{:S(2)}) copy-start(bf16[256,256]{1,0:T(8,128)(2,1)} %weight_ref.3) | copy-start | bytes 393220
  48.6 40.6 %copy-start.5 = (bf16[128,256]{1,0:T(8,128)(2,1)S(1)}, bf16[128,256]{1,0:T(8,128)(2,1)}, u32[]{:S(2)}) copy-start(bf16[128,256]{1,0:T(8,128)(2,1)} %cotangent_ref.1) | copy-start | bytes 196612
  126.1 9.4 %collective-permute-start.1 = (bf16[16,144,256]{2,1,0:T(8,128)(2,1)S(1)}, bf16[16,144,256]{2,1,0:T(8,128)(2,1)S(1)}, u32[]{:S(2)}, u32[]{:S(2)}) collective-permute-start(bf16[16,144,256]{2,1,0:T(8,128)(2,1)S(1)} %all_to_all.26.mine_ref.refs_5_), channel_id=1, source_target_pairs={{0,1},{1,0},{2,3},{3,2},{4,5},{5,4},{6,7},{7,6},{8,9},{9,8},{10,11... | collective-permute-start | bytes 3538952 | tf_op jit(solution)/shard_map/ppermute | solution.py:426
  129.0 16.3 %all-to-all-start.4 = ((bf16[16,32,256]{2,1,0:T(8,128)(2,1)}), bf16[16,32,256]{2,1,0:T(8,128)(2,1)S(1)}, u32[]{:S(2)}, u32[]{:S(2)}) async-start(bf16[16,32,256]{2,1,0:T(8,128)(2,1)} %weight_part.1), calls=%async_computation.4 | async-start | bytes 524288 | tf_op jit(solution)/shard_map/all_to_all | solution.py:428
  145.3 32.6 %all-to-all-start.3 = ((bf16[16,128,256]{2,1,0:T(8,128)(2,1)}), bf16[16,128,256]{2,1,0:T(8,128)(2,1)S(1)}, u32[]{:S(2)}, u32[]{:S(2)}) async-start(bf16[16,128,256]{2,1,0:T(8,128)(2,1)} %backward_tiles.1), calls=%async_computation.3 | async-start | bytes 2097152 | tf_op jit(solution)/shard_map/all_to_all | solution.py:430
  150.8 3.1 %collective-permute-start.2 = (f32[32,256]{1,0:T(8,128)S(1)}, f32[32,256]{1,0:T(8,128)S(1)}, u32[]{:S(2)}, u32[]{:S(2)}) collective-permute-start(f32[32,256]{1,0:T(8,128)S(1)} %weight_sum.1), channel_id=1, source_target_pairs={{0,1},{1,0},{2,3},{3,2},{4,5},{5,4},{6,7},{7,6},{8,9},{9,8},{10,11... | collective-permute-start | bytes 98312 | tf_op jit(solution)/shard_map/ppermute | solution.py:313
  153.9 9.8 %collective-permute-start.3 = (f32[1,32,256]{2,1,0:T(8,128)S(1)}, f32[1,32,256]{2,1,0:T(8,128)S(1)}, u32[]{:S(2)}, u32[]{:S(2)}) collective-permute-start(f32[1,32,256]{2,1,0:T(8,128)S(1)} %add_bitcast_fusion), channel_id=1, source_target_pairs={{0,16},{1,17},{2,18},{3,19},{4,20},{5,21},{6,22},{7,23},{8,24},{9,... | collective-permute-start | bytes 98312 | tf_op jit(solution)/shard_map/ppermute | solution.py:316
  163.7 7.4 %collective-permute-start.4 = (f32[2,32,256]{2,1,0:T(8,128)S(1)}, f32[2,32,256]{2,1,0:T(8,128)S(1)}, u32[]{:S(2)}, u32[]{:S(2)}) collective-permute-start(f32[2,32,256]{2,1,0:T(8,128)S(1)} %maximum_select_fusion.1), channel_id=1, source_target_pairs={{0,8},{1,9},{2,10},{3,11},{4,12},{5,13},{6,14},{7,15},{8,0},{9,1},... | collective-permute-start | bytes 196616 | tf_op jit(solution)/shard_map/ppermute | solution.py:316
  171.1 6.9 %collective-permute-start.5 = (f32[4,32,256]{2,1,0:T(8,128)S(1)}, f32[4,32,256]{2,1,0:T(8,128)S(1)}, u32[]{:S(2)}, u32[]{:S(2)}) collective-permute-start(f32[4,32,256]{2,1,0:T(8,128)S(1)} %maximum_select_fusion.held_ref), channel_id=1, source_target_pairs={{0,4},{1,5},{2,6},{3,7},{4,0},{5,1},{6,2},{7,3},{8,12},{9,13},{10,... | collective-permute-start | bytes 393224 | tf_op jit(solution)/shard_map/ppermute | solution.py:316

commit v4 on v3

--- a/solution.py
+++ b/solution.py
@@ -64,7 +64,7 @@
                 group = total_ref[0]
                 total_ref[0] = group + 1
                 last_ref[target] = group
-                extra_ids_ref[group] = 2 * target + (seen == size).astype(i32)
+                extra_ids_ref[group] = target
 
             extra_ref[last_ref[target] * size + over] = s
 
@@ -144,44 +144,32 @@
     return jnp.dot(left, right, preferred_element_type=f32)
 
 
-def further_groups(lists, tiles_ref, source_ref, acc_ref, first, targets, store):
-    list_ref, more_ref, more_ids_ref, total_ref, ids_ref = lists
-
-    def more(t, carry):
-        code = more_ids_ref[t]
-        target = code // 2
-        place = target - first
-
-        @pl.when((place >= 0) & (place < targets))
-        def _():
-            @pl.when(code % 2 == 1)
-            def _():
-                acc_ref[place] = grouped_product(tiles_ref, ids_ref, source_ref, list_ref, target)
-
-            acc_ref[place] += grouped_product(tiles_ref, ids_ref, source_ref, more_ref, t)
-            store(place)
-
-        return carry
-
-    lax.fori_loop(0, total_ref[0], more, 0)
-
-
 def forward_kernel(part, *refs):
     lists = refs[:5]
+    list_ref, more_ref, more_ids_ref, total_ref, ids_ref = lists
     panel_ref, tiles_ref, out_ref, acc_ref = refs[5:]
     half = out_ref.shape[0]
 
     def base(t, carry):
-        product = grouped_product(tiles_ref, lists[4], panel_ref, lists[0], part * half + t)
+        product = grouped_product(tiles_ref, ids_ref, panel_ref, list_ref, part * half + t)
+        acc_ref[t] = product
         out_ref[t] = product.astype(bf16)
         return carry
 
-    lax.fori_loop(0, half, base, 0, unroll=4)
-
-    def store(place):
-        out_ref[place] = acc_ref[place].astype(bf16)
-
-    further_groups(lists, tiles_ref, panel_ref, acc_ref, part * half, half, store)
+    lax.fori_loop(0, half, base, 0, unroll=half)
+
+    def more(t, carry):
+        place = more_ids_ref[t] - part * half
+
+        @pl.when((place >= 0) & (place < half))
+        def _():
+            total = acc_ref[place] + grouped_product(tiles_ref, ids_ref, panel_ref, more_ref, t)
+            acc_ref[place] = total
+            out_ref[place] = total.astype(bf16)
+
+        return carry
+
+    lax.fori_loop(0, total_ref[0], more, 0)
 
 
 def forward_tiles(part, lists, panel, tiles):
@@ -338,10 +326,10 @@
         out_ref[t] = product.astype(bf16)
         return carry
 
-    lax.fori_loop(0, targets, base, 0, unroll=4)
+    lax.fori_loop(0, targets, base, 0, unroll=targets)
 
     def more(t, carry):
-        target = more_ids_ref[t] // 2
+        target = more_ids_ref[t]
         place = target % targets
 
         @pl.when(target < targets)

time: 180 us -> 178 us (0.989)
  no operation moved by 1% of the time
where the time goes in v4:
time: 178 us; the launch traced here: 177 us
  blocking collectives  75.8 us (43%)
  starting transfers between devices  36.2 us (20%)
  waiting for transfers between devices  33.4 us (19%)
  Pallas kernels  26.5 us (15%)
  local copies, waits for them, and re-layouts  3.65 us (2%)
    all_to_all x1, blocking collectives, local(): parts = lax.all_to_all(summed, 'col', 0, 0, axis_index_groups=groups)  39.9 us
    all_to_all x1, blocking collectives, local(): mine = lax.all_to_all(messages, 'col', 0, 0, axis_index_groups=groups)  35.9 us
    ppermute x3, waiting for transfers between devices, gather_over_col(): came = lax.ppermute(held, 'col', [(i, i ^ distance) for i in range(size)])  17 us
    pallas_call x1, Pallas kernels, prepare(): pl.pallas_call(prepare_kernel, out_shape=(*lists, *lists, held), in_specs...  12.8 us
    all_to_all x1, starting transfers between devices, local(): panel = lax.all_to_all(spread(features, row_count), 'row', 0, 0)  11.8 us
    all_to_all x1, waiting for transfers between devices, local(): panel = lax.all_to_all(spread(features, row_count), 'row', 0, 0)  10.8 us
    ppermute x3, starting transfers between devices, gather_over_col(): came = lax.ppermute(held, 'col', [(i, i ^ distance) for i in range(size)])  7.05 us
    all_to_all x1, starting transfers between devices, local(): weight_parts = lax.all_to_all(weight_rows, 'row', 0, 0)  6.18 us
  transfers between devices with their start and end apart: 9, of which 6 were waited for; matrix products, arithmetic and copies ran while one was open for 0% of the time, Pallas kernels for 12%

profile of v4, /device:TPU:2, one launch (start us, length us, event | category | flops | bytes accessed | tf_op | source)
XLA Modules:
  0.0 177.4 jit_solution(15118155676570139572)
XLA Ops:
  0.7 1.0 copy-done.4
  1.6 0.1 spread.1
  1.7 1.0 copy-done.1
  2.7 11.8 %all-to-all-start = ((bf16[16,128,256]{2,1,0:T(8,128)(2,1)}), bf16[16,128,256]{2,1,0:T(8,128)(2,1)}, u32[]{:S(2)}, u32[]{:S(2)}) async-start(bf16[16,128,256]{2,1,0:T(8,128)(2,1)} %copy-done.1), calls=%async_computation | async-start | bytes 2097152 | tf_op jit(solution)/shard_map/all_to_all | solution.py:402
  15.2 12.8 %prepare.1 = (s32[128]{0:T(128)S(1)}, s32[384]{0:T(512)S(1)}, s32[96]{0:T(128)S(1)}, s32[1]{0:T(128)}, s32[97]{0:T(128)S(1)}, /*index=5*/s32[128]{0:T(128)S(1)},...) custom-call(s32[96]{0:T(128)S(1)} %bitcast.12, ...), custom_call_target="tpu_custom_call" | custom-call | bytes 28311552 | tf_op jit(solution)/shard_map/prepare/pallas_call | solution.py:121
  28.0 1.6 copy-done.2
  29.6 10.8 %all-to-all-done.refs_5_ = bf16[16,128,256]{2,1,0:T(8,128)(2,1)} async-done(((bf16[16,128,256]{2,1,0:T(8,128)(2,1)}), bf16[16,128,256]{2,1,0:T(8,128)(2,1)}, u32[]{:S(2)}, u32[]{:S(2)}) %all-to-all-start) | async-done | bytes 1048608 | tf_op jit(solution)/shard_map/all_to_all | solution.py:402
  40.4 2.7 %forward_tiles_1.1 = bf16[16,128,256]{2,1,0:T(8,128)(2,1)S(1)} custom-call(s32[128]{0:T(128)S(1)} %get-tuple-element.20.refs_0_, s32[384]{0:T(512)S(1)} %get-tuple-element.21.refs_1_, s32[96]{0:T(128)S(1)} %get-tuple-element.22.refs_2_, s32[1]{0:T(128)} %get-tuple-element.23.refs_3_, s32[97]{0:T(128)S(1)} %get-tuple-element.24.refs_4_, ...), custom_call_target="tpu_custom_call" | custom-call | flops 536870912 | bytes 1572864 | tf_op jit(solution)/shard_map/forward_tiles_1/pallas_call | solution.py:178
  43.1 1.9 %collective-permute-start = (bf16[16,128,256]{2,1,0:T(8,128)(2,1)S(1)}, bf16[16,128,256]{2,1,0:T(8,128)(2,1)S(1)}, u32[]{:S(2)}, u32[]{:S(2)}) collective-permute-start(bf16[16,128,256]{2,1,0:T(8,128)(2,1)S(1)} %forward_tiles_1.1), channel_id=1, source_target_pairs={{0,1},{1,0},{2,3},{3,2},{4,5},{5,4},{6,7},{7,6},{8,9},{9,8},{10,11... | collective-permute-start | bytes 3145736 | tf_op jit(solution)/shard_map/ppermute | solution.py:407
  45.0 2.7 %forward_tiles_0.1 = bf16[16,128,256]{2,1,0:T(8,128)(2,1)S(1)} custom-call(s32[128]{0:T(128)S(1)} %get-tuple-element.20.refs_0_, s32[384]{0:T(512)S(1)} %get-tuple-element.21.refs_1_, s32[96]{0:T(128)S(1)} %get-tuple-element.22.refs_2_, s32[1]{0:T(128)} %get-tuple-element.23.refs_3_, s32[97]{0:T(128)S(1)} %get-tuple-element.24.refs_4_, ...), custom_call_target="tpu_custom_call" | custom-call | flops 536870912 | bytes 1572864 | tf_op jit(solution)/shard_map/forward_tiles_0/pallas_call | solution.py:178
  47.7 0.0 copy-start.3
  47.7 0.0 copy-start.5
  47.7 0.3 add_convert_fusion
  48.0 39.9 %all_to_all.25.parts_ref = bf16[16,128,256]{2,1,0:T(8,128)(2,1)S(1)} all-to-all(bf16[16,128,256]{2,1,0:T(8,128)(2,1)S(1)} %add_convert_fusion), channel_id=1, replica_groups={{0,2,4,6,8,10,12,14,16,18,20,22,24,26,28,30},{1,3,5,7,9,11,13,15,17,19,..., dimensions={0} | all-to-all | bytes 2097152 | tf_op jit(solution)/shard_map/all_to_all | solution.py:410
  87.9 0.9 dense.1
  88.8 35.9 %all_to_all.26.mine_ref.refs_5_ = bf16[16,144,256]{2,1,0:T(8,128)(2,1)S(1)} all-to-all(bf16[16,144,256]{2,1,0:T(8,128)(2,1)S(1)} %get-tuple-element.30), channel_id=1, replica_groups={{0,2,4,6,8,10,12,14,16,18,20,22,24,26,28,30},{1,3,5,7,9,11,13,15,17,19,..., dimensions={0} | all-to-all | bytes 2359296 | tf_op jit(solution)/shard_map/all_to_all | solution.py:413
  124.7 1.9 %collective-permute-start.1 = (bf16[16,144,256]{2,1,0:T(8,128)(2,1)S(1)}, bf16[16,144,256]{2,1,0:T(8,128)(2,1)S(1)}, u32[]{:S(2)}, u32[]{:S(2)}) collective-permute-start(bf16[16,144,256]{2,1,0:T(8,128)(2,1)S(1)} %all_to_all.26.mine_ref.refs_5_), channel_id=1, source_target_pairs={{0,1},{1,0},{2,3},{3,2},{4,5},{5,4},{6,7},{7,6},{8,9},{9,8},{10,11... | collective-permute-start | bytes 3538952 | tf_op jit(solution)/shard_map/ppermute | solution.py:414
  126.6 1.0 weight_part.1
  127.7 6.2 %all-to-all-start.4 = ((bf16[16,32,256]{2,1,0:T(8,128)(2,1)}), bf16[16,32,256]{2,1,0:T(8,128)(2,1)S(1)}, u32[]{:S(2)}, u32[]{:S(2)}) async-start(bf16[16,32,256]{2,1,0:T(8,128)(2,1)} %weight_part.1), calls=%async_computation.4 | async-start | bytes 524288 | tf_op jit(solution)/shard_map/all_to_all | solution.py:416
  133.8 0.0 collective-permute-done.1.refs_6_
  133.8 5.4 %backward_tiles.1 = bf16[16,128,256]{2,1,0:T(8,128)(2,1)} custom-call(s32[128]{0:T(128)S(1)} %get-tuple-element.26.refs_0_, s32[384]{0:T(512)S(1)} %get-tuple-element.27.refs_1_, s32[96]{0:T(128)S(1)} %get-tuple-element.28.refs_2_, s32[1]{0:T(128)} %get-tuple-element.29.refs_3_, s32[97]{0:T(128)S(1)} %get-tuple-element.32.refs_4_, ...), custom_call_target="tpu_custom_call" | custom-call | flops 1073741824 | bytes 1589248 | tf_op jit(solution)/shard_map/backward_tiles/pallas_call | solution.py:353
  139.2 4.5 %all-to-all-done.4.parts_ref = bf16[16,32,256]{2,1,0:T(8,128)(2,1)S(1)} async-done(((bf16[16,32,256]{2,1,0:T(8,128)(2,1)}), bf16[16,32,256]{2,1,0:T(8,128)(2,1)S(1)}, u32[]{:S(2)}, u32[]{:S(2)}) %all-to-all-start.4) | async-done | bytes 262176 | tf_op jit(solution)/shard_map/all_to_all | solution.py:416
  143.7 5.4 %all-to-all-start.3 = ((bf16[16,128,256]{2,1,0:T(8,128)(2,1)}), bf16[16,128,256]{2,1,0:T(8,128)(2,1)S(1)}, u32[]{:S(2)}, u32[]{:S(2)}) async-start(bf16[16,128,256]{2,1,0:T(8,128)(2,1)} %backward_tiles.1), calls=%async_computation.3 | async-start | bytes 2097152 | tf_op jit(solution)/shard_map/all_to_all | solution.py:418
  149.2 1.9 %collective-permute-start.2 = (f32[32,256]{1,0:T(8,128)S(1)}, f32[32,256]{1,0:T(8,128)S(1)}, u32[]{:S(2)}, u32[]{:S(2)}) collective-permute-start(f32[32,256]{1,0:T(8,128)S(1)} %weight_sum.1), channel_id=1, source_target_pairs={{0,1},{1,0},{2,3},{3,2},{4,5},{5,4},{6,7},{7,6},{8,9},{9,8},{10,11... | collective-permute-start | bytes 98312 | tf_op jit(solution)/shard_map/ppermute | solution.py:301
  151.1 1.2 collective-permute-done.2
  152.3 2.7 %collective-permute-start.3 = (f32[1,32,256]{2,1,0:T(8,128)S(1)}, f32[1,32,256]{2,1,0:T(8,128)S(1)}, u32[]{:S(2)}, u32[]{:S(2)}) collective-permute-start(f32[1,32,256]{2,1,0:T(8,128)S(1)} %add_bitcast_fusion), channel_id=1, source_target_pairs={{0,16},{1,17},{2,18},{3,19},{4,20},{5,21},{6,22},{7,23},{8,24},{9,... | collective-permute-start | bytes 98312 | tf_op jit(solution)/shard_map/ppermute | solution.py:304
  155.1 7.1 %collective-permute-done.3 = f32[1,32,256]{2,1,0:T(8,128)S(1)} collective-permute-done((f32[1,32,256]{2,1,0:T(8,128)S(1)}, f32[1,32,256]{2,1,0:T(8,128)S(1)}, u32[]{:S(2)}, u32[]{:S(2)}) %collective-permute-start.3) | collective-permute-done | bytes 32800 | tf_op jit(solution)/shard_map/ppermute | solution.py:304
  162.2 2.4 %collective-permute-start.4 = (f32[2,32,256]{2,1,0:T(8,128)S(1)}, f32[2,32,256]{2,1,0:T(8,128)S(1)}, u32[]{:S(2)}, u32[]{:S(2)}) collective-permute-start(f32[2,32,256]{2,1,0:T(8,128)S(1)} %maximum_select_fusion.1), channel_id=1, source_target_pairs={{0,8},{1,9},{2,10},{3,11},{4,12},{5,13},{6,14},{7,15},{8,0},{9,1},... | collective-permute-start | bytes 196616 | tf_op jit(solution)/shard_map/ppermute | solution.py:304
  164.6 5.0 %collective-permute-done.4 = f32[2,32,256]{2,1,0:T(8,128)S(1)} collective-permute-done((f32[2,32,256]{2,1,0:T(8,128)S(1)}, f32[2,32,256]{2,1,0:T(8,128)S(1)}, u32[]{:S(2)}, u32[]{:S(2)}) %collective-permute-start.4) | collective-permute-done | bytes 65568 | tf_op jit(solution)/shard_map/ppermute | solution.py:304
  169.6 1.9 %collective-permute-start.5 = (f32[4,32,256]{2,1,0:T(8,128)S(1)}, f32[4,32,256]{2,1,0:T(8,128)S(1)}, u32[]{:S(2)}, u32[]{:S(2)}) collective-permute-start(f32[4,32,256]{2,1,0:T(8,128)S(1)} %maximum_select_fusion.held_ref), channel_id=1, source_target_pairs={{0,4},{1,5},{2,6},{3,7},{4,0},{5,1},{6,2},{7,3},{8,12},{9,13},{10,... | collective-permute-start | bytes 393224 | tf_op jit(solution)/shard_map/ppermute | solution.py:304
  171.6 4.9 %collective-permute-done.5.came_ref = f32[4,32,256]{2,1,0:T(8,128)S(1)} collective-permute-done((f32[4,32,256]{2,1,0:T(8,128)S(1)}, f32[4,32,256]{2,1,0:T(8,128)S(1)}, u32[]{:S(2)}, u32[]{:S(2)}) %collective-permute-start.5) | collective-permute-done | bytes 131104 | tf_op jit(solution)/shard_map/ppermute | solution.py:304
  176.5 0.9 finish.1
  (17 shorter events, 0.1 us)
Async XLA Ops:
  0.6 14.5 %copy-start = (bf16[1,1,96,128,128]{4,3,2,1,0:T(8,128)(2,1)S(1)}, bf16[1,1,96,128,128]{4,3,2,1,0:T(8,128)(2,1)}, u32[]{:S(2)}) copy-start(bf16[1,1,96,128,128]{4,3,2,1,0:T(8,128)(2,1)} %param.9) | copy-start | bytes 9437188
  0.6 1.0 copy-start.4
  1.6 13.5 %copy-start.6 = (s32[1,1,96]{2,1,0:T(1,128)S(1)}, s32[1,1,96]{2,1,0:T(1,128)}, u32[]{:S(2)}) copy-start(s32[1,1,96]{2,1,0:T(1,128)} %param.10) | copy-start | bytes 1156
  1.6 13.6 %copy-start.7 = (s32[1,1,96]{2,1,0:T(1,128)S(1)}, s32[1,1,96]{2,1,0:T(1,128)}, u32[]{:S(2)}) copy-start(s32[1,1,96]{2,1,0:T(1,128)} %param.11) | copy-start | bytes 1156
  1.7 1.0 copy-start.1
  2.7 37.7 %all-to-all-start = ((bf16[16,128,256]{2,1,0:T(8,128)(2,1)}), bf16[16,128,256]{2,1,0:T(8,128)(2,1)}, u32[]{:S(2)}, u32[]{:S(2)}) async-start(bf16[16,128,256]{2,1,0:T(8,128)(2,1)} %copy-done.1), calls=%async_computation | async-start | bytes 2097152 | tf_op jit(solution)/shard_map/all_to_all | solution.py:402
  28.0 1.6 copy-start.2
  43.1 4.6 %collective-permute-start = (bf16[16,128,256]{2,1,0:T(8,128)(2,1)S(1)}, bf16[16,128,256]{2,1,0:T(8,128)(2,1)S(1)}, u32[]{:S(2)}, u32[]{:S(2)}) collective-permute-start(bf16[16,128,256]{2,1,0:T(8,128)(2,1)S(1)} %forward_tiles_1.1), channel_id=1, source_target_pairs={{0,1},{1,0},{2,3},{3,2},{4,5},{5,4},{6,7},{7,6},{8,9},{9,8},{10,11... | collective-permute-start | bytes 3145736 | tf_op jit(solution)/shard_map/ppermute | solution.py:407
  47.7 40.2 %copy-start.3 = (bf16[256,256]{1,0:T(8,128)(2,1)S(1)}, bf16[256,256]{1,0:T(8,128)(2,1)}, u32[]{:S(2)}) copy-start(bf16[256,256]{1,0:T(8,128)(2,1)} %weight_ref.3) | copy-start | bytes 393220
  47.7 40.2 %copy-start.5 = (bf16[128,256]{1,0:T(8,128)(2,1)S(1)}, bf16[128,256]{1,0:T(8,128)(2,1)}, u32[]{:S(2)}) copy-start(bf16[128,256]{1,0:T(8,128)(2,1)} %cotangent_ref.1) | copy-start | bytes 196612
  124.7 9.1 %collective-permute-start.1 = (bf16[16,144,256]{2,1,0:T(8,128)(2,1)S(1)}, bf16[16,144,256]{2,1,0:T(8,128)(2,1)S(1)}, u32[]{:S(2)}, u32[]{:S(2)}) collective-permute-start(bf16[16,144,256]{2,1,0:T(8,128)(2,1)S(1)} %all_to_all.26.mine_ref.refs_5_), channel_id=1, source_target_pairs={{0,1},{1,0},{2,3},{3,2},{4,5},{5,4},{6,7},{7,6},{8,9},{9,8},{10,11... | collective-permute-start | bytes 3538952 | tf_op jit(solution)/shard_map/ppermute | solution.py:414
  127.7 16.1 %all-to-all-start.4 = ((bf16[16,32,256]{2,1,0:T(8,128)(2,1)}), bf16[16,32,256]{2,1,0:T(8,128)(2,1)S(1)}, u32[]{:S(2)}, u32[]{:S(2)}) async-start(bf16[16,32,256]{2,1,0:T(8,128)(2,1)} %weight_part.1), calls=%async_computation.4 | async-start | bytes 524288 | tf_op jit(solution)/shard_map/all_to_all | solution.py:416
  143.7 32.7 %all-to-all-start.3 = ((bf16[16,128,256]{2,1,0:T(8,128)(2,1)}), bf16[16,128,256]{2,1,0:T(8,128)(2,1)S(1)}, u32[]{:S(2)}, u32[]{:S(2)}) async-start(bf16[16,128,256]{2,1,0:T(8,128)(2,1)} %backward_tiles.1), calls=%async_computation.3 | async-start | bytes 2097152 | tf_op jit(solution)/shard_map/all_to_all | solution.py:418
  149.2 3.1 %collective-permute-start.2 = (f32[32,256]{1,0:T(8,128)S(1)}, f32[32,256]{1,0:T(8,128)S(1)}, u32[]{:S(2)}, u32[]{:S(2)}) collective-permute-start(f32[32,256]{1,0:T(8,128)S(1)} %weight_sum.1), channel_id=1, source_target_pairs={{0,1},{1,0},{2,3},{3,2},{4,5},{5,4},{6,7},{7,6},{8,9},{9,8},{10,11... | collective-permute-start | bytes 98312 | tf_op jit(solution)/shard_map/ppermute | solution.py:301
  152.3 9.9 %collective-permute-start.3 = (f32[1,32,256]{2,1,0:T(8,128)S(1)}, f32[1,32,256]{2,1,0:T(8,128)S(1)}, u32[]{:S(2)}, u32[]{:S(2)}) collective-permute-start(f32[1,32,256]{2,1,0:T(8,128)S(1)} %add_bitcast_fusion), channel_id=1, source_target_pairs={{0,16},{1,17},{2,18},{3,19},{4,20},{5,21},{6,22},{7,23},{8,24},{9,... | collective-permute-start | bytes 98312 | tf_op jit(solution)/shard_map/ppermute | solution.py:304
  162.2 7.4 %collective-permute-start.4 = (f32[2,32,256]{2,1,0:T(8,128)S(1)}, f32[2,32,256]{2,1,0:T(8,128)S(1)}, u32[]{:S(2)}, u32[]{:S(2)}) collective-permute-start(f32[2,32,256]{2,1,0:T(8,128)S(1)} %maximum_select_fusion.1), channel_id=1, source_target_pairs={{0,8},{1,9},{2,10},{3,11},{4,12},{5,13},{6,14},{7,15},{8,0},{9,1},... | collective-permute-start | bytes 196616 | tf_op jit(solution)/shard_map/ppermute | solution.py:304
  169.6 6.9 %collective-permute-start.5 = (f32[4,32,256]{2,1,0:T(8,128)S(1)}, f32[4,32,256]{2,1,0:T(8,128)S(1)}, u32[]{:S(2)}, u32[]{:S(2)}) collective-permute-start(f32[4,32,256]{2,1,0:T(8,128)S(1)} %maximum_select_fusion.held_ref), channel_id=1, source_target_pairs={{0,4},{1,5},{2,6},{3,7},{4,0},{5,1},{6,2},{7,3},{8,12},{9,13},{10,... | collective-permute-start | bytes 393224 | tf_op jit(solution)/shard_map/ppermute | solution.py:304

commit v5 on v4

--- a/solution.py
+++ b/solution.py
@@ -87,8 +87,11 @@
     def away(s):
         return (rows_ref[s] % 2 != core).astype(i32)
 
+    def place(s):
+        return (rows_ref[s] // 2 % 2) * (half // 2) + rows_ref[s] // 4
+
     def forward_target(s):
-        return away(s) * half + rows_ref[s] // 2
+        return away(s) * half + place(s)
 
     def backward_target(s):
         return away(s) * half + cols_ref[s]
@@ -98,7 +101,7 @@
 
     def sources(s, carry):
         fwd_source_ref[s] = cols_ref[s]
-        bwd_source_ref[s] = rows_ref[s] // 2
+        bwd_source_ref[s] = place(s)
         return carry
 
     lax.fori_loop(0, slots, sources, 0)
@@ -228,7 +231,7 @@
     own = 2 * turned.shape[0] // peers
     for k in range(peers):
         message_ref[k, :rows, :] = grad_pre
-        first = (k // 2) * own
+        first = (k % (peers // 2)) * own
         low = turned[first : first + own // 2]
         high = turned[first + own // 2 : first + own]
         message_ref[k, rows:, :] = jnp.concatenate([low, high], axis=1).astype(bf16)
@@ -394,7 +397,7 @@
     node_total = rows_dev * row_count * col_count
     half = col_count // 2
     pairs = [(i, i ^ 1) for i in range(col_count)]
-    groups = [[2 * k + c for k in range(half)] for c in range(2)]
+    groups = [[4 * y + 2 * x + c for x in range(2) for y in range(half // 2)] for c in range(2)]
     position = lax.axis_index("col").astype(i32)
     core = jnp.reshape(position % 2, (1,))
     tiles = block_values[0, 0]

time: 178 us -> 177 us (level)
  waiting for transfers between devices: 33.4 us -> 28.6 us
  starting transfers between devices: 36.2 us -> 39.9 us
    ppermute x3, waiting for transfers between devices: 17 us -> 13.2 us  [gather_over_col(): came = lax.ppermute(held, 'col', [(i, i ^ distance) for i in range(size)])]
    ppermute x3, starting transfers between devices: 7.05 us -> 10.5 us  [gather_over_col(): came = lax.ppermute(held, 'col', [(i, i ^ distance) for i in range(size)])]
    all_to_all x1, blocking collectives: 39.9 us -> 37.4 us  [local(): parts = lax.all_to_all(summed, 'col', 0, 0, axis_index_groups=groups)]
  transfers between devices with their start and end apart: 9 -> 9, of which waited for: 6 -> 6; matrix products, arithmetic and copies ran while one was open for 0% -> 0% of each run, Pallas kernels for 12% -> 13%
where the time goes in v5:
time: 177 us; the launch traced here: 176 us
  blocking collectives  74.7 us (42%)
  starting transfers between devices  39.9 us (23%)
  waiting for transfers between devices  28.6 us (16%)
  Pallas kernels  27.5 us (16%)
  local copies, waits for them, and re-layouts  3.65 us (2%)
    all_to_all x1, blocking collectives, local(): parts = lax.all_to_all(summed, 'col', 0, 0, axis_index_groups=groups)  37.4 us
    all_to_all x1, blocking collectives, local(): mine = lax.all_to_all(messages, 'col', 0, 0, axis_index_groups=groups)  37.3 us
    pallas_call x1, Pallas kernels, prepare(): pl.pallas_call(prepare_kernel, out_shape=(*lists, *lists, held), in_specs...  13.8 us
    ppermute x3, waiting for transfers between devices, gather_over_col(): came = lax.ppermute(held, 'col', [(i, i ^ distance) for i in range(size)])  13.2 us
    all_to_all x1, starting transfers between devices, local(): panel = lax.all_to_all(spread(features, row_count), 'row', 0, 0)  11.8 us
    ppermute x3, starting transfers between devices, gather_over_col(): came = lax.ppermute(held, 'col', [(i, i ^ distance) for i in range(size)])  10.5 us
    all_to_all x1, waiting for transfers between devices, local(): panel = lax.all_to_all(spread(features, row_count), 'row', 0, 0)  9.73 us
    all_to_all x1, starting transfers between devices, local(): weight_parts = lax.all_to_all(weight_rows, 'row', 0, 0)  6.39 us
  transfers between devices with their start and end apart: 9, of which 6 were waited for; matrix products, arithmetic and copies ran while one was open for 0% of the time, Pallas kernels for 13%

profile of v5, /device:TPU:2, one launch (start us, length us, event | category | flops | bytes accessed | tf_op | source)
XLA Modules:
  0.0 176.2 jit_solution(14538155374377961508)
XLA Ops:
  0.7 1.0 copy-done.4
  1.6 0.1 spread.1
  1.7 1.0 copy-done.1
  2.7 11.8 %all-to-all-start = ((bf16[16,128,256]{2,1,0:T(8,128)(2,1)}), bf16[16,128,256]{2,1,0:T(8,128)(2,1)}, u32[]{:S(2)}, u32[]{:S(2)}) async-start(bf16[16,128,256]{2,1,0:T(8,128)(2,1)} %copy-done.1), calls=%async_computation | async-start | bytes 2097152 | tf_op jit(solution)/shard_map/all_to_all | solution.py:405
  15.2 13.8 %prepare.1 = (s32[128]{0:T(128)S(1)}, s32[384]{0:T(512)S(1)}, s32[96]{0:T(128)S(1)}, s32[1]{0:T(128)}, s32[97]{0:T(128)S(1)}, /*index=5*/s32[128]{0:T(128)S(1)},...) custom-call(s32[96]{0:T(128)S(1)} %bitcast.12, ...), custom_call_target="tpu_custom_call" | custom-call | bytes 28311552 | tf_op jit(solution)/shard_map/prepare/pallas_call | solution.py:124
  29.0 1.6 copy-done.2
  30.6 9.7 %all-to-all-done.refs_5_ = bf16[16,128,256]{2,1,0:T(8,128)(2,1)} async-done(((bf16[16,128,256]{2,1,0:T(8,128)(2,1)}), bf16[16,128,256]{2,1,0:T(8,128)(2,1)}, u32[]{:S(2)}, u32[]{:S(2)}) %all-to-all-start) | async-done | bytes 1048608 | tf_op jit(solution)/shard_map/all_to_all | solution.py:405
  40.4 2.7 %forward_tiles_1.1 = bf16[16,128,256]{2,1,0:T(8,128)(2,1)S(1)} custom-call(s32[128]{0:T(128)S(1)} %get-tuple-element.20.refs_0_, s32[384]{0:T(512)S(1)} %get-tuple-element.21.refs_1_, s32[96]{0:T(128)S(1)} %get-tuple-element.22.refs_2_, s32[1]{0:T(128)} %get-tuple-element.23.refs_3_, s32[97]{0:T(128)S(1)} %get-tuple-element.24.refs_4_, ...), custom_call_target="tpu_custom_call" | custom-call | flops 536870912 | bytes 1572864 | tf_op jit(solution)/shard_map/forward_tiles_1/pallas_call | solution.py:181
  43.1 1.9 %collective-permute-start = (bf16[16,128,256]{2,1,0:T(8,128)(2,1)S(1)}, bf16[16,128,256]{2,1,0:T(8,128)(2,1)S(1)}, u32[]{:S(2)}, u32[]{:S(2)}) collective-permute-start(bf16[16,128,256]{2,1,0:T(8,128)(2,1)S(1)} %forward_tiles_1.1), channel_id=1, source_target_pairs={{0,1},{1,0},{2,3},{3,2},{4,5},{5,4},{6,7},{7,6},{8,9},{9,8},{10,11... | collective-permute-start | bytes 3145736 | tf_op jit(solution)/shard_map/ppermute | solution.py:410
  45.0 2.7 %forward_tiles_0.1 = bf16[16,128,256]{2,1,0:T(8,128)(2,1)S(1)} custom-call(s32[128]{0:T(128)S(1)} %get-tuple-element.20.refs_0_, s32[384]{0:T(512)S(1)} %get-tuple-element.21.refs_1_, s32[96]{0:T(128)S(1)} %get-tuple-element.22.refs_2_, s32[1]{0:T(128)} %get-tuple-element.23.refs_3_, s32[97]{0:T(128)S(1)} %get-tuple-element.24.refs_4_, ...), custom_call_target="tpu_custom_call" | custom-call | flops 536870912 | bytes 1572864 | tf_op jit(solution)/shard_map/forward_tiles_0/pallas_call | solution.py:181
  47.7 0.0 copy-start.3
  47.7 0.0 copy-start.5
  47.7 0.0 collective-permute-done
  47.7 0.3 add_convert_fusion
  48.0 37.4 %all_to_all.25.parts_ref = bf16[16,128,256]{2,1,0:T(8,128)(2,1)S(1)} all-to-all(bf16[16,128,256]{2,1,0:T(8,128)(2,1)S(1)} %add_convert_fusion), channel_id=1, replica_groups={{0,4,8,12,16,20,24,28,2,6,10,14,18,22,26,30},{1,5,9,13,17,21,25,29,3,7,..., dimensions={0} | all-to-all | bytes 2097152 | tf_op jit(solution)/shard_map/all_to_all | solution.py:413
  85.5 0.9 dense.1
  86.4 37.3 %all_to_all.26.mine_ref.refs_5_ = bf16[16,144,256]{2,1,0:T(8,128)(2,1)S(1)} all-to-all(bf16[16,144,256]{2,1,0:T(8,128)(2,1)S(1)} %get-tuple-element.30), channel_id=1, replica_groups={{0,4,8,12,16,20,24,28,2,6,10,14,18,22,26,30},{1,5,9,13,17,21,25,29,3,7,..., dimensions={0} | all-to-all | bytes 2359296 | tf_op jit(solution)/shard_map/all_to_all | solution.py:416
  123.7 1.9 %collective-permute-start.1 = (bf16[16,144,256]{2,1,0:T(8,128)(2,1)S(1)}, bf16[16,144,256]{2,1,0:T(8,128)(2,1)S(1)}, u32[]{:S(2)}, u32[]{:S(2)}) collective-permute-start(bf16[16,144,256]{2,1,0:T(8,128)(2,1)S(1)} %all_to_all.26.mine_ref.refs_5_), channel_id=1, source_target_pairs={{0,1},{1,0},{2,3},{3,2},{4,5},{5,4},{6,7},{7,6},{8,9},{9,8},{10,11... | collective-permute-start | bytes 3538952 | tf_op jit(solution)/shard_map/ppermute | solution.py:417
  125.6 1.0 weight_part.1
  126.6 6.4 %all-to-all-start.4 = ((bf16[16,32,256]{2,1,0:T(8,128)(2,1)}), bf16[16,32,256]{2,1,0:T(8,128)(2,1)S(1)}, u32[]{:S(2)}, u32[]{:S(2)}) async-start(bf16[16,32,256]{2,1,0:T(8,128)(2,1)} %weight_part.1), calls=%async_computation.4 | async-start | bytes 524288 | tf_op jit(solution)/shard_map/all_to_all | solution.py:419
  133.0 5.4 %backward_tiles.1 = bf16[16,128,256]{2,1,0:T(8,128)(2,1)} custom-call(s32[128]{0:T(128)S(1)} %get-tuple-element.26.refs_0_, s32[384]{0:T(512)S(1)} %get-tuple-element.27.refs_1_, s32[96]{0:T(128)S(1)} %get-tuple-element.28.refs_2_, s32[1]{0:T(128)} %get-tuple-element.29.refs_3_, s32[97]{0:T(128)S(1)} %get-tuple-element.32.refs_4_, ...), custom_call_target="tpu_custom_call" | custom-call | flops 1073741824 | bytes 1589248 | tf_op jit(solution)/shard_map/backward_tiles/pallas_call | solution.py:356
  138.4 4.5 %all-to-all-done.4.parts_ref = bf16[16,32,256]{2,1,0:T(8,128)(2,1)S(1)} async-done(((bf16[16,32,256]{2,1,0:T(8,128)(2,1)}), bf16[16,32,256]{2,1,0:T(8,128)(2,1)S(1)}, u32[]{:S(2)}, u32[]{:S(2)}) %all-to-all-start.4) | async-done | bytes 262176 | tf_op jit(solution)/shard_map/all_to_all | solution.py:419
  142.9 5.4 %all-to-all-start.3 = ((bf16[16,128,256]{2,1,0:T(8,128)(2,1)}), bf16[16,128,256]{2,1,0:T(8,128)(2,1)S(1)}, u32[]{:S(2)}, u32[]{:S(2)}) async-start(bf16[16,128,256]{2,1,0:T(8,128)(2,1)} %backward_tiles.1), calls=%async_computation.3 | async-start | bytes 2097152 | tf_op jit(solution)/shard_map/all_to_all | solution.py:421
  148.3 1.9 %collective-permute-start.2 = (f32[32,256]{1,0:T(8,128)S(1)}, f32[32,256]{1,0:T(8,128)S(1)}, u32[]{:S(2)}, u32[]{:S(2)}) collective-permute-start(f32[32,256]{1,0:T(8,128)S(1)} %weight_sum.1), channel_id=1, source_target_pairs={{0,1},{1,0},{2,3},{3,2},{4,5},{5,4},{6,7},{7,6},{8,9},{9,8},{10,11... | collective-permute-start | bytes 98312 | tf_op jit(solution)/shard_map/ppermute | solution.py:304
  150.3 1.2 collective-permute-done.2
  151.5 3.5 %collective-permute-start.3 = (f32[1,32,256]{2,1,0:T(8,128)S(1)}, f32[1,32,256]{2,1,0:T(8,128)S(1)}, u32[]{:S(2)}, u32[]{:S(2)}) collective-permute-start(f32[1,32,256]{2,1,0:T(8,128)S(1)} %add_bitcast_fusion), channel_id=1, source_target_pairs={{0,16},{1,17},{2,18},{3,19},{4,20},{5,21},{6,22},{7,23},{8,24},{9,... | collective-permute-start | bytes 98312 | tf_op jit(solution)/shard_map/ppermute | solution.py:307
  155.0 6.4 %collective-permute-done.3 = f32[1,32,256]{2,1,0:T(8,128)S(1)} collective-permute-done((f32[1,32,256]{2,1,0:T(8,128)S(1)}, f32[1,32,256]{2,1,0:T(8,128)S(1)}, u32[]{:S(2)}, u32[]{:S(2)}) %collective-permute-start.3) | collective-permute-done | bytes 32800 | tf_op jit(solution)/shard_map/ppermute | solution.py:307
  161.3 3.5 %collective-permute-start.4 = (f32[2,32,256]{2,1,0:T(8,128)S(1)}, f32[2,32,256]{2,1,0:T(8,128)S(1)}, u32[]{:S(2)}, u32[]{:S(2)}) collective-permute-start(f32[2,32,256]{2,1,0:T(8,128)S(1)} %maximum_select_fusion.1), channel_id=1, source_target_pairs={{0,8},{1,9},{2,10},{3,11},{4,12},{5,13},{6,14},{7,15},{8,0},{9,1},... | collective-permute-start | bytes 196616 | tf_op jit(solution)/shard_map/ppermute | solution.py:307
  164.9 3.5 %collective-permute-done.4 = f32[2,32,256]{2,1,0:T(8,128)S(1)} collective-permute-done((f32[2,32,256]{2,1,0:T(8,128)S(1)}, f32[2,32,256]{2,1,0:T(8,128)S(1)}, u32[]{:S(2)}, u32[]{:S(2)}) %collective-permute-start.4) | collective-permute-done | bytes 65568 | tf_op jit(solution)/shard_map/ppermute | solution.py:307
  168.4 3.5 %collective-permute-start.5 = (f32[4,32,256]{2,1,0:T(8,128)S(1)}, f32[4,32,256]{2,1,0:T(8,128)S(1)}, u32[]{:S(2)}, u32[]{:S(2)}) collective-permute-start(f32[4,32,256]{2,1,0:T(8,128)S(1)} %maximum_select_fusion.held_ref), channel_id=1, source_target_pairs={{0,4},{1,5},{2,6},{3,7},{4,0},{5,1},{6,2},{7,3},{8,12},{9,13},{10,... | collective-permute-start | bytes 393224 | tf_op jit(solution)/shard_map/ppermute | solution.py:307
  171.9 3.3 %collective-permute-done.5.came_ref = f32[4,32,256]{2,1,0:T(8,128)S(1)} collective-permute-done((f32[4,32,256]{2,1,0:T(8,128)S(1)}, f32[4,32,256]{2,1,0:T(8,128)S(1)}, u32[]{:S(2)}, u32[]{:S(2)}) %collective-permute-start.5) | collective-permute-done | bytes 131104 | tf_op jit(solution)/shard_map/ppermute | solution.py:307
  175.3 0.9 finish.1
  (17 shorter events, 0.1 us)
Async XLA Ops:
  0.6 14.5 %copy-start = (bf16[1,1,96,128,128]{4,3,2,1,0:T(8,128)(2,1)S(1)}, bf16[1,1,96,128,128]{4,3,2,1,0:T(8,128)(2,1)}, u32[]{:S(2)}) copy-start(bf16[1,1,96,128,128]{4,3,2,1,0:T(8,128)(2,1)} %param.9) | copy-start | bytes 9437188
  0.6 1.0 copy-start.4
  1.6 13.5 %copy-start.6 = (s32[1,1,96]{2,1,0:T(1,128)S(1)}, s32[1,1,96]{2,1,0:T(1,128)}, u32[]{:S(2)}) copy-start(s32[1,1,96]{2,1,0:T(1,128)} %param.10) | copy-start | bytes 1156
  1.6 13.6 %copy-start.7 = (s32[1,1,96]{2,1,0:T(1,128)S(1)}, s32[1,1,96]{2,1,0:T(1,128)}, u32[]{:S(2)}) copy-start(s32[1,1,96]{2,1,0:T(1,128)} %param.11) | copy-start | bytes 1156
  1.7 1.0 copy-start.1
  2.7 37.7 %all-to-all-start = ((bf16[16,128,256]{2,1,0:T(8,128)(2,1)}), bf16[16,128,256]{2,1,0:T(8,128)(2,1)}, u32[]{:S(2)}, u32[]{:S(2)}) async-start(bf16[16,128,256]{2,1,0:T(8,128)(2,1)} %copy-done.1), calls=%async_computation | async-start | bytes 2097152 | tf_op jit(solution)/shard_map/all_to_all | solution.py:405
  29.0 1.6 copy-start.2
  43.1 4.6 %collective-permute-start = (bf16[16,128,256]{2,1,0:T(8,128)(2,1)S(1)}, bf16[16,128,256]{2,1,0:T(8,128)(2,1)S(1)}, u32[]{:S(2)}, u32[]{:S(2)}) collective-permute-start(bf16[16,128,256]{2,1,0:T(8,128)(2,1)S(1)} %forward_tiles_1.1), channel_id=1, source_target_pairs={{0,1},{1,0},{2,3},{3,2},{4,5},{5,4},{6,7},{7,6},{8,9},{9,8},{10,11... | collective-permute-start | bytes 3145736 | tf_op jit(solution)/shard_map/ppermute | solution.py:410
  47.7 37.8 %copy-start.3 = (bf16[256,256]{1,0:T(8,128)(2,1)S(1)}, bf16[256,256]{1,0:T(8,128)(2,1)}, u32[]{:S(2)}) copy-start(bf16[256,256]{1,0:T(8,128)(2,1)} %weight_ref.3) | copy-start | bytes 393220
  47.7 37.8 %copy-start.5 = (bf16[128,256]{1,0:T(8,128)(2,1)S(1)}, bf16[128,256]{1,0:T(8,128)(2,1)}, u32[]{:S(2)}) copy-start(bf16[128,256]{1,0:T(8,128)(2,1)} %cotangent_ref.1) | copy-start | bytes 196612
  123.7 9.3 %collective-permute-start.1 = (bf16[16,144,256]{2,1,0:T(8,128)(2,1)S(1)}, bf16[16,144,256]{2,1,0:T(8,128)(2,1)S(1)}, u32[]{:S(2)}, u32[]{:S(2)}) collective-permute-start(bf16[16,144,256]{2,1,0:T(8,128)(2,1)S(1)} %all_to_all.26.mine_ref.refs_5_), channel_id=1, source_target_pairs={{0,1},{1,0},{2,3},{3,2},{4,5},{5,4},{6,7},{7,6},{8,9},{9,8},{10,11... | collective-permute-start | bytes 3538952 | tf_op jit(solution)/shard_map/ppermute | solution.py:417
  126.6 16.3 %all-to-all-start.4 = ((bf16[16,32,256]{2,1,0:T(8,128)(2,1)}), bf16[16,32,256]{2,1,0:T(8,128)(2,1)S(1)}, u32[]{:S(2)}, u32[]{:S(2)}) async-start(bf16[16,32,256]{2,1,0:T(8,128)(2,1)} %weight_part.1), calls=%async_computation.4 | async-start | bytes 524288 | tf_op jit(solution)/shard_map/all_to_all | solution.py:419
  142.9 32.4 %all-to-all-start.3 = ((bf16[16,128,256]{2,1,0:T(8,128)(2,1)}), bf16[16,128,256]{2,1,0:T(8,128)(2,1)S(1)}, u32[]{:S(2)}, u32[]{:S(2)}) async-start(bf16[16,128,256]{2,1,0:T(8,128)(2,1)} %backward_tiles.1), calls=%async_computation.3 | async-start | bytes 2097152 | tf_op jit(solution)/shard_map/all_to_all | solution.py:421
  148.3 3.1 %collective-permute-start.2 = (f32[32,256]{1,0:T(8,128)S(1)}, f32[32,256]{1,0:T(8,128)S(1)}, u32[]{:S(2)}, u32[]{:S(2)}) collective-permute-start(f32[32,256]{1,0:T(8,128)S(1)} %weight_sum.1), channel_id=1, source_target_pairs={{0,1},{1,0},{2,3},{3,2},{4,5},{5,4},{6,7},{7,6},{8,9},{9,8},{10,11... | collective-permute-start | bytes 98312 | tf_op jit(solution)/shard_map/ppermute | solution.py:304
  151.5 9.9 %collective-permute-start.3 = (f32[1,32,256]{2,1,0:T(8,128)S(1)}, f32[1,32,256]{2,1,0:T(8,128)S(1)}, u32[]{:S(2)}, u32[]{:S(2)}) collective-permute-start(f32[1,32,256]{2,1,0:T(8,128)S(1)} %add_bitcast_fusion), channel_id=1, source_target_pairs={{0,16},{1,17},{2,18},{3,19},{4,20},{5,21},{6,22},{7,23},{8,24},{9,... | collective-permute-start | bytes 98312 | tf_op jit(solution)/shard_map/ppermute | solution.py:307
  161.3 7.1 %collective-permute-start.4 = (f32[2,32,256]{2,1,0:T(8,128)S(1)}, f32[2,32,256]{2,1,0:T(8,128)S(1)}, u32[]{:S(2)}, u32[]{:S(2)}) collective-permute-start(f32[2,32,256]{2,1,0:T(8,128)S(1)} %maximum_select_fusion.1), channel_id=1, source_target_pairs={{0,8},{1,9},{2,10},{3,11},{4,12},{5,13},{6,14},{7,15},{8,0},{9,1},... | collective-permute-start | bytes 196616 | tf_op jit(solution)/shard_map/ppermute | solution.py:307
  168.4 6.9 %collective-permute-start.5 = (f32[4,32,256]{2,1,0:T(8,128)S(1)}, f32[4,32,256]{2,1,0:T(8,128)S(1)}, u32[]{:S(2)}, u32[]{:S(2)}) collective-permute-start(f32[4,32,256]{2,1,0:T(8,128)S(1)} %maximum_select_fusion.held_ref), channel_id=1, source_target_pairs={{0,4},{1,5},{2,6},{3,7},{4,0},{5,1},{6,2},{7,3},{8,12},{9,13},{10,... | collective-permute-start | bytes 393224 | tf_op jit(solution)/shard_map/ppermute | solution.py:307

commit v6 on v5

--- a/solution.py
+++ b/solution.py
@@ -301,7 +301,7 @@
 
 
 def gather_over_col(rows, position, size):
-    held = (rows + lax.ppermute(rows, "col", [(i, i ^ 1) for i in range(size)]))[None]
+    held = (rows + lax.ppermute(rows, "col", [(i, i ^ 1) for i in range(size)])).astype(bf16)[None]
     steps = (size // 2, size // 4, size // 8)
     for distance in steps:
         came = lax.ppermute(held, "col", [(i, i ^ distance) for i in range(size)])
@@ -376,7 +376,7 @@
         place = bits[1] * 2 + bits[2]
         held, came = held_ref[place], came_ref[place]
         low, high = (held, came) if bits[0] == 0 else (came, held)
-        weight_out_ref[k * own : (k + 1) * own, :] = jnp.where(upper, high, low)
+        weight_out_ref[k * own : (k + 1) * own, :] = jnp.where(upper, high.astype(f32), low.astype(f32))
 
 
 def finish(upper, parts, weight, held, came):

time: 177 us -> 176 us (level)
  the two profiles are of different devices: /device:TPU:2 before, /device:TPU:8 now
where the time goes in v6:
time: 176 us; the launch traced here: 175 us
  blocking collectives  75.1 us (43%)
  starting transfers between devices  35.1 us (20%)
  waiting for transfers between devices  32 us (18%)
  Pallas kernels  27.7 us (16%)
  local copies, waits for them, and re-layouts  3.65 us (2%)
    all_to_all x1, blocking collectives, local(): mine = lax.all_to_all(messages, 'col', 0, 0, axis_index_groups=groups)  37.8 us
    all_to_all x1, blocking collectives, local(): parts = lax.all_to_all(summed, 'col', 0, 0, axis_index_groups=groups)  37.3 us
    pallas_call x1, Pallas kernels, prepare(): pl.pallas_call(prepare_kernel, out_shape=(*lists, *lists, held), in_specs...  14 us
    ppermute x3, waiting for transfers between devices, gather_over_col(): came = lax.ppermute(held, 'col', [(i, i ^ distance) for i in range(size)])  13.4 us
    all_to_all x1, starting transfers between devices, local(): panel = lax.all_to_all(spread(features, row_count), 'row', 0, 0)  11.4 us
    all_to_all x1, waiting for transfers between devices, local(): panel = lax.all_to_all(spread(features, row_count), 'row', 0, 0)  10.8 us
    ppermute x3, starting transfers between devices, gather_over_col(): came = lax.ppermute(held, 'col', [(i, i ^ distance) for i in range(size)])  8.88 us
    pallas_call x1, Pallas kernels, backward_tiles(): pl.pallas_call(backward_kernel, out_shape=jax.ShapeDtypeStruct(shape, bf1...  5.37 us
  transfers between devices with their start and end apart: 9, of which 7 were waited for; matrix products, arithmetic and copies ran while one was open for 0% of the time, Pallas kernels for 13%

profile of v6, /device:TPU:8, one launch (start us, length us, event | category | flops | bytes accessed | tf_op | source)
XLA Modules:
  0.0 175.4 jit_solution(16319086866716278647)
XLA Ops:
  0.7 1.0 copy-done.4
  1.6 0.1 spread.1
  1.7 1.0 copy-done.1
  2.7 11.4 %all-to-all-start = ((bf16[16,128,256]{2,1,0:T(8,128)(2,1)}), bf16[16,128,256]{2,1,0:T(8,128)(2,1)}, u32[]{:S(2)}, u32[]{:S(2)}) async-start(bf16[16,128,256]{2,1,0:T(8,128)(2,1)} %copy-done.1), calls=%async_computation | async-start | bytes 2097152 | tf_op jit(solution)/shard_map/all_to_all | solution.py:405
  14.8 14.0 %prepare.1 = (s32[128]{0:T(128)S(1)}, s32[384]{0:T(512)S(1)}, s32[96]{0:T(128)S(1)}, s32[1]{0:T(128)}, s32[97]{0:T(128)S(1)}, /*index=5*/s32[128]{0:T(128)S(1)},...) custom-call(s32[96]{0:T(128)S(1)} %bitcast.12, ...), custom_call_target="tpu_custom_call" | custom-call | bytes 28311552 | tf_op jit(solution)/shard_map/prepare/pallas_call | solution.py:124
  28.8 1.6 copy-done.2
  30.5 10.8 %all-to-all-done.refs_5_ = bf16[16,128,256]{2,1,0:T(8,128)(2,1)} async-done(((bf16[16,128,256]{2,1,0:T(8,128)(2,1)}), bf16[16,128,256]{2,1,0:T(8,128)(2,1)}, u32[]{:S(2)}, u32[]{:S(2)}) %all-to-all-start) | async-done | bytes 1048608 | tf_op jit(solution)/shard_map/all_to_all | solution.py:405
  41.3 2.7 %forward_tiles_1.1 = bf16[16,128,256]{2,1,0:T(8,128)(2,1)S(1)} custom-call(s32[128]{0:T(128)S(1)} %get-tuple-element.20.refs_0_, s32[384]{0:T(512)S(1)} %get-tuple-element.21.refs_1_, s32[96]{0:T(128)S(1)} %get-tuple-element.22.refs_2_, s32[1]{0:T(128)} %get-tuple-element.23.refs_3_, s32[97]{0:T(128)S(1)} %get-tuple-element.24.refs_4_, ...), custom_call_target="tpu_custom_call" | custom-call | flops 536870912 | bytes 1572864 | tf_op jit(solution)/shard_map/forward_tiles_1/pallas_call | solution.py:181
  43.9 1.9 %collective-permute-start = (bf16[16,128,256]{2,1,0:T(8,128)(2,1)S(1)}, bf16[16,128,256]{2,1,0:T(8,128)(2,1)S(1)}, u32[]{:S(2)}, u32[]{:S(2)}) collective-permute-start(bf16[16,128,256]{2,1,0:T(8,128)(2,1)S(1)} %forward_tiles_1.1), channel_id=1, source_target_pairs={{0,1},{1,0},{2,3},{3,2},{4,5},{5,4},{6,7},{7,6},{8,9},{9,8},{10,11... | collective-permute-start | bytes 3145736 | tf_op jit(solution)/shard_map/ppermute | solution.py:410
  45.9 2.7 %forward_tiles_0.1 = bf16[16,128,256]{2,1,0:T(8,128)(2,1)S(1)} custom-call(s32[128]{0:T(128)S(1)} %get-tuple-element.20.refs_0_, s32[384]{0:T(512)S(1)} %get-tuple-element.21.refs_1_, s32[96]{0:T(128)S(1)} %get-tuple-element.22.refs_2_, s32[1]{0:T(128)} %get-tuple-element.23.refs_3_, s32[97]{0:T(128)S(1)} %get-tuple-element.24.refs_4_, ...), custom_call_target="tpu_custom_call" | custom-call | flops 536870912 | bytes 1572864 | tf_op jit(solution)/shard_map/forward_tiles_0/pallas_call | solution.py:181
  48.6 0.0 copy-start.3
  48.6 0.0 copy-start.5
  48.6 0.3 add_convert_fusion
  48.9 37.3 %all_to_all.25.parts_ref = bf16[16,128,256]{2,1,0:T(8,128)(2,1)S(1)} all-to-all(bf16[16,128,256]{2,1,0:T(8,128)(2,1)S(1)} %add_convert_fusion), channel_id=1, replica_groups={{0,4,8,12,16,20,24,28,2,6,10,14,18,22,26,30},{1,5,9,13,17,21,25,29,3,7,..., dimensions={0} | all-to-all | bytes 2097152 | tf_op jit(solution)/shard_map/all_to_all | solution.py:413
  86.2 0.9 dense.1
  87.2 37.8 %all_to_all.26.mine_ref.refs_5_ = bf16[16,144,256]{2,1,0:T(8,128)(2,1)S(1)} all-to-all(bf16[16,144,256]{2,1,0:T(8,128)(2,1)S(1)} %get-tuple-element.30), channel_id=1, replica_groups={{0,4,8,12,16,20,24,28,2,6,10,14,18,22,26,30},{1,5,9,13,17,21,25,29,3,7,..., dimensions={0} | all-to-all | bytes 2359296 | tf_op jit(solution)/shard_map/all_to_all | solution.py:416
  124.9 1.9 %collective-permute-start.1 = (bf16[16,144,256]{2,1,0:T(8,128)(2,1)S(1)}, bf16[16,144,256]{2,1,0:T(8,128)(2,1)S(1)}, u32[]{:S(2)}, u32[]{:S(2)}) collective-permute-start(bf16[16,144,256]{2,1,0:T(8,128)(2,1)S(1)} %all_to_all.26.mine_ref.refs_5_), channel_id=1, source_target_pairs={{0,1},{1,0},{2,3},{3,2},{4,5},{5,4},{6,7},{7,6},{8,9},{9,8},{10,11... | collective-permute-start | bytes 3538952 | tf_op jit(solution)/shard_map/ppermute | solution.py:417
  126.8 1.0 weight_part.1
  127.9 4.4 %all-to-all-start.4 = ((bf16[16,32,256]{2,1,0:T(8,128)(2,1)}), bf16[16,32,256]{2,1,0:T(8,128)(2,1)S(1)}, u32[]{:S(2)}, u32[]{:S(2)}) async-start(bf16[16,32,256]{2,1,0:T(8,128)(2,1)} %weight_part.1), calls=%async_computation.4 | async-start | bytes 524288 | tf_op jit(solution)/shard_map/all_to_all | solution.py:419
  132.3 5.4 %backward_tiles.1 = bf16[16,128,256]{2,1,0:T(8,128)(2,1)} custom-call(s32[128]{0:T(128)S(1)} %get-tuple-element.26.refs_0_, s32[384]{0:T(512)S(1)} %get-tuple-element.27.refs_1_, s32[96]{0:T(128)S(1)} %get-tuple-element.28.refs_2_, s32[1]{0:T(128)} %get-tuple-element.29.refs_3_, s32[97]{0:T(128)S(1)} %get-tuple-element.32.refs_4_, ...), custom_call_target="tpu_custom_call" | custom-call | flops 1073741824 | bytes 1589248 | tf_op jit(solution)/shard_map/backward_tiles/pallas_call | solution.py:356
  137.7 5.3 %all-to-all-done.4.parts_ref = bf16[16,32,256]{2,1,0:T(8,128)(2,1)S(1)} async-done(((bf16[16,32,256]{2,1,0:T(8,128)(2,1)}), bf16[16,32,256]{2,1,0:T(8,128)(2,1)S(1)}, u32[]{:S(2)}, u32[]{:S(2)}) %all-to-all-start.4) | async-done | bytes 262176 | tf_op jit(solution)/shard_map/all_to_all | solution.py:419
  143.0 4.6 %all-to-all-start.3 = ((bf16[16,128,256]{2,1,0:T(8,128)(2,1)}), bf16[16,128,256]{2,1,0:T(8,128)(2,1)S(1)}, u32[]{:S(2)}, u32[]{:S(2)}) async-start(bf16[16,128,256]{2,1,0:T(8,128)(2,1)} %backward_tiles.1), calls=%async_computation.3 | async-start | bytes 2097152 | tf_op jit(solution)/shard_map/all_to_all | solution.py:421
  147.6 1.9 %collective-permute-start.2 = (f32[32,256]{1,0:T(8,128)S(1)}, f32[32,256]{1,0:T(8,128)S(1)}, u32[]{:S(2)}, u32[]{:S(2)}) collective-permute-start(f32[32,256]{1,0:T(8,128)S(1)} %weight_sum.1), channel_id=1, source_target_pairs={{0,1},{1,0},{2,3},{3,2},{4,5},{5,4},{6,7},{7,6},{8,9},{9,8},{10,11... | collective-permute-start | bytes 98312 | tf_op jit(solution)/shard_map/ppermute | solution.py:304
  149.6 1.2 collective-permute-done.2
  150.7 3.7 %collective-permute-start.3 = (bf16[1,32,256]{2,1,0:T(8,128)(2,1)S(1)}, bf16[1,32,256]{2,1,0:T(8,128)(2,1)S(1)}, u32[]{:S(2)}, u32[]{:S(2)}) collective-permute-start(bf16[1,32,256]{2,1,0:T(8,128)(2,1)S(1)} %fusion), channel_id=1, source_target_pairs={{0,16},{1,17},{2,18},{3,19},{4,20},{5,21},{6,22},{7,23},{8,24},{9,... | collective-permute-start | bytes 49160 | tf_op jit(solution)/shard_map/ppermute | solution.py:307
  154.5 5.8 %collective-permute-done.3 = bf16[1,32,256]{2,1,0:T(8,128)(2,1)S(1)} collective-permute-done((bf16[1,32,256]{2,1,0:T(8,128)(2,1)S(1)}, bf16[1,32,256]{2,1,0:T(8,128)(2,1)S(1)}, u32[]{:S(2)}, u32[]{:S(2)}) %collective-permute-start.3) | collective-permute-done | bytes 16416 | tf_op jit(solution)/shard_map/ppermute | solution.py:307
  160.3 2.6 %collective-permute-start.4 = (bf16[2,32,256]{2,1,0:T(8,128)(2,1)S(1)}, bf16[2,32,256]{2,1,0:T(8,128)(2,1)S(1)}, u32[]{:S(2)}, u32[]{:S(2)}) collective-permute-start(bf16[2,32,256]{2,1,0:T(8,128)(2,1)S(1)} %maximum_select_fusion.1), channel_id=1, source_target_pairs={{0,8},{1,9},{2,10},{3,11},{4,12},{5,13},{6,14},{7,15},{8,0},{9,1},... | collective-permute-start | bytes 98312 | tf_op jit(solution)/shard_map/ppermute | solution.py:307
  163.0 4.0 %collective-permute-done.4 = bf16[2,32,256]{2,1,0:T(8,128)(2,1)S(1)} collective-permute-done((bf16[2,32,256]{2,1,0:T(8,128)(2,1)S(1)}, bf16[2,32,256]{2,1,0:T(8,128)(2,1)S(1)}, u32[]{:S(2)}, u32[]{:S(2)}) %collective-permute-start.4) | collective-permute-done | bytes 32800 | tf_op jit(solution)/shard_map/ppermute | solution.py:307
  167.0 2.5 %collective-permute-start.5 = (bf16[4,32,256]{2,1,0:T(8,128)(2,1)S(1)}, bf16[4,32,256]{2,1,0:T(8,128)(2,1)S(1)}, u32[]{:S(2)}, u32[]{:S(2)}) collective-permute-start(bf16[4,32,256]{2,1,0:T(8,128)(2,1)S(1)} %maximum_select_fusion.held_ref), channel_id=1, source_target_pairs={{0,4},{1,5},{2,6},{3,7},{4,0},{5,1},{6,2},{7,3},{8,12},{9,13},{10,... | collective-permute-start | bytes 196616 | tf_op jit(solution)/shard_map/ppermute | solution.py:307
  169.6 3.6 %collective-permute-done.5.came_ref = bf16[4,32,256]{2,1,0:T(8,128)(2,1)S(1)} collective-permute-done((bf16[4,32,256]{2,1,0:T(8,128)(2,1)S(1)}, bf16[4,32,256]{2,1,0:T(8,128)(2,1)S(1)}, u32[]{:S(2)}, u32[]{:S(2)}) %collective-permute-start.5) | collective-permute-done | bytes 65568 | tf_op jit(solution)/shard_map/ppermute | solution.py:307
  173.2 1.3 all-to-all-done.3.parts_ref
  174.5 0.9 finish.1
  (17 shorter events, 0.1 us)
Async XLA Ops:
  0.6 14.2 %copy-start = (bf16[1,1,96,128,128]{4,3,2,1,0:T(8,128)(2,1)S(1)}, bf16[1,1,96,128,128]{4,3,2,1,0:T(8,128)(2,1)}, u32[]{:S(2)}) copy-start(bf16[1,1,96,128,128]{4,3,2,1,0:T(8,128)(2,1)} %param.9) | copy-start | bytes 9437188
  0.6 1.0 copy-start.4
  1.6 13.2 %copy-start.6 = (s32[1,1,96]{2,1,0:T(1,128)S(1)}, s32[1,1,96]{2,1,0:T(1,128)}, u32[]{:S(2)}) copy-start(s32[1,1,96]{2,1,0:T(1,128)} %param.10) | copy-start | bytes 1156
  1.6 13.2 %copy-start.7 = (s32[1,1,96]{2,1,0:T(1,128)S(1)}, s32[1,1,96]{2,1,0:T(1,128)}, u32[]{:S(2)}) copy-start(s32[1,1,96]{2,1,0:T(1,128)} %param.11) | copy-start | bytes 1156
  1.7 1.0 copy-start.1
  2.7 38.5 %all-to-all-start = ((bf16[16,128,256]{2,1,0:T(8,128)(2,1)}), bf16[16,128,256]{2,1,0:T(8,128)(2,1)}, u32[]{:S(2)}, u32[]{:S(2)}) async-start(bf16[16,128,256]{2,1,0:T(8,128)(2,1)} %copy-done.1), calls=%async_computation | async-start | bytes 2097152 | tf_op jit(solution)/shard_map/all_to_all | solution.py:405
  28.8 1.6 copy-start.2
  43.9 4.6 %collective-permute-start = (bf16[16,128,256]{2,1,0:T(8,128)(2,1)S(1)}, bf16[16,128,256]{2,1,0:T(8,128)(2,1)S(1)}, u32[]{:S(2)}, u32[]{:S(2)}) collective-permute-start(bf16[16,128,256]{2,1,0:T(8,128)(2,1)S(1)} %forward_tiles_1.1), channel_id=1, source_target_pairs={{0,1},{1,0},{2,3},{3,2},{4,5},{5,4},{6,7},{7,6},{8,9},{9,8},{10,11... | collective-permute-start | bytes 3145736 | tf_op jit(solution)/shard_map/ppermute | solution.py:410
  48.6 37.7 %copy-start.3 = (bf16[256,256]{1,0:T(8,128)(2,1)S(1)}, bf16[256,256]{1,0:T(8,128)(2,1)}, u32[]{:S(2)}) copy-start(bf16[256,256]{1,0:T(8,128)(2,1)} %weight_ref.3) | copy-start | bytes 393220
  48.6 37.7 %copy-start.5 = (bf16[128,256]{1,0:T(8,128)(2,1)S(1)}, bf16[128,256]{1,0:T(8,128)(2,1)}, u32[]{:S(2)}) copy-start(bf16[128,256]{1,0:T(8,128)(2,1)} %cotangent_ref.1) | copy-start | bytes 196612
  124.9 7.4 %collective-permute-start.1 = (bf16[16,144,256]{2,1,0:T(8,128)(2,1)S(1)}, bf16[16,144,256]{2,1,0:T(8,128)(2,1)S(1)}, u32[]{:S(2)}, u32[]{:S(2)}) collective-permute-start(bf16[16,144,256]{2,1,0:T(8,128)(2,1)S(1)} %all_to_all.26.mine_ref.refs_5_), channel_id=1, source_target_pairs={{0,1},{1,0},{2,3},{3,2},{4,5},{5,4},{6,7},{7,6},{8,9},{9,8},{10,11... | collective-permute-start | bytes 3538952 | tf_op jit(solution)/shard_map/ppermute | solution.py:417
  127.9 15.1 %all-to-all-start.4 = ((bf16[16,32,256]{2,1,0:T(8,128)(2,1)}), bf16[16,32,256]{2,1,0:T(8,128)(2,1)S(1)}, u32[]{:S(2)}, u32[]{:S(2)}) async-start(bf16[16,32,256]{2,1,0:T(8,128)(2,1)} %weight_part.1), calls=%async_computation.4 | async-start | bytes 524288 | tf_op jit(solution)/shard_map/all_to_all | solution.py:419
  143.0 31.6 %all-to-all-start.3 = ((bf16[16,128,256]{2,1,0:T(8,128)(2,1)}), bf16[16,128,256]{2,1,0:T(8,128)(2,1)S(1)}, u32[]{:S(2)}, u32[]{:S(2)}) async-start(bf16[16,128,256]{2,1,0:T(8,128)(2,1)} %backward_tiles.1), calls=%async_computation.3 | async-start | bytes 2097152 | tf_op jit(solution)/shard_map/all_to_all | solution.py:421
  147.6 3.1 %collective-permute-start.2 = (f32[32,256]{1,0:T(8,128)S(1)}, f32[32,256]{1,0:T(8,128)S(1)}, u32[]{:S(2)}, u32[]{:S(2)}) collective-permute-start(f32[32,256]{1,0:T(8,128)S(1)} %weight_sum.1), channel_id=1, source_target_pairs={{0,1},{1,0},{2,3},{3,2},{4,5},{5,4},{6,7},{7,6},{8,9},{9,8},{10,11... | collective-permute-start | bytes 98312 | tf_op jit(solution)/shard_map/ppermute | solution.py:304
  150.7 9.5 %collective-permute-start.3 = (bf16[1,32,256]{2,1,0:T(8,128)(2,1)S(1)}, bf16[1,32,256]{2,1,0:T(8,128)(2,1)S(1)}, u32[]{:S(2)}, u32[]{:S(2)}) collective-permute-start(bf16[1,32,256]{2,1,0:T(8,128)(2,1)S(1)} %fusion), channel_id=1, source_target_pairs={{0,16},{1,17},{2,18},{3,19},{4,20},{5,21},{6,22},{7,23},{8,24},{9,... | collective-permute-start | bytes 49160 | tf_op jit(solution)/shard_map/ppermute | solution.py:307
  160.3 6.7 %collective-permute-start.4 = (bf16[2,32,256]{2,1,0:T(8,128)(2,1)S(1)}, bf16[2,32,256]{2,1,0:T(8,128)(2,1)S(1)}, u32[]{:S(2)}, u32[]{:S(2)}) collective-permute-start(bf16[2,32,256]{2,1,0:T(8,128)(2,1)S(1)} %maximum_select_fusion.1), channel_id=1, source_target_pairs={{0,8},{1,9},{2,10},{3,11},{4,12},{5,13},{6,14},{7,15},{8,0},{9,1},... | collective-permute-start | bytes 98312 | tf_op jit(solution)/shard_map/ppermute | solution.py:307
  167.0 6.2 %collective-permute-start.5 = (bf16[4,32,256]{2,1,0:T(8,128)(2,1)S(1)}, bf16[4,32,256]{2,1,0:T(8,128)(2,1)S(1)}, u32[]{:S(2)}, u32[]{:S(2)}) collective-permute-start(bf16[4,32,256]{2,1,0:T(8,128)(2,1)S(1)} %maximum_select_fusion.held_ref), channel_id=1, source_target_pairs={{0,4},{1,5},{2,6},{3,7},{4,0},{5,1},{6,2},{7,3},{8,12},{9,13},{10,... | collective-permute-start | bytes 196616 | tf_op jit(solution)/shard_map/ppermute | solution.py:307

commit v7 on v5

--- a/solution.py
+++ b/solution.py
@@ -302,7 +302,7 @@
 
 def gather_over_col(rows, position, size):
     held = (rows + lax.ppermute(rows, "col", [(i, i ^ 1) for i in range(size)]))[None]
-    steps = (size // 2, size // 4, size // 8)
+    steps = (size // 8, size // 4, size // 2)
     for distance in steps:
         came = lax.ppermute(held, "col", [(i, i ^ distance) for i in range(size)])
         if distance == steps[-1]:
@@ -373,9 +373,9 @@
     chunks, own, _ = held_ref.shape
     for k in range(2 * chunks):
         bits = [(k >> b) & 1 for b in range(3)]
-        place = bits[1] * 2 + bits[2]
+        place = bits[1] * 2 + bits[0]
         held, came = held_ref[place], came_ref[place]
-        low, high = (held, came) if bits[0] == 0 else (came, held)
+        low, high = (held, came) if bits[2] == 0 else (came, held)
         weight_out_ref[k * own : (k + 1) * own, :] = jnp.where(upper, high, low)
 
 
@@ -421,7 +421,7 @@
     back_parts = lax.all_to_all(back, "row", 0, 0)
     weight_rows = weight_sum(weight_parts, 1.0 / math.sqrt(node_total))
     held, came = gather_over_col(weight_rows, position, col_count)
-    upper = jnp.reshape((position // (col_count // 8)) % 2, (1,))
+    upper = jnp.reshape((position // (col_count // 2)) % 2, (1,))
     feature_grad, weight_grad = finish(upper, back_parts, weight, held, came)
     return (activations, feature_grad, weight_grad)
 

time: 177 us -> 179 us (1.011)
  waiting for transfers between devices: 28.6 us -> 31.8 us
    ppermute x3, waiting for transfers between devices: 13.2 us -> 15.4 us  [gather_over_col(): came = lax.ppermute(held, 'col', [(i, i ^ distance) for i in range(size)])]
  transfers between devices with their start and end apart: 9 -> 9, of which waited for: 6 -> 6; matrix products, arithmetic and copies ran while one was open for 0% -> 0% of each run, Pallas kernels for 13% -> 12%
where the time goes in v7:
time: 179 us; the launch traced here: 178 us
  blocking collectives  74.7 us (42%)
  starting transfers between devices  39.2 us (22%)
  waiting for transfers between devices  31.8 us (18%)
  Pallas kernels  26.5 us (15%)
  local copies, waits for them, and re-layouts  3.65 us (2%)
    all_to_all x1, blocking collectives, local(): parts = lax.all_to_all(summed, 'col', 0, 0, axis_index_groups=groups)  37.4 us
    all_to_all x1, blocking collectives, local(): mine = lax.all_to_all(messages, 'col', 0, 0, axis_index_groups=groups)  37.3 us
    ppermute x3, waiting for transfers between devices, gather_over_col(): came = lax.ppermute(held, 'col', [(i, i ^ distance) for i in range(size)])  15.4 us
    pallas_call x1, Pallas kernels, prepare(): pl.pallas_call(prepare_kernel, out_shape=(*lists, *lists, held), in_specs...  12.8 us
    all_to_all x1, starting transfers between devices, local(): panel = lax.all_to_all(spread(features, row_count), 'row', 0, 0)  11.8 us
    all_to_all x1, waiting for transfers between devices, local(): panel = lax.all_to_all(spread(features, row_count), 'row', 0, 0)  10.7 us
    ppermute x3, starting transfers between devices, gather_over_col(): came = lax.ppermute(held, 'col', [(i, i ^ distance) for i in range(size)])  10.3 us
    all_to_all x1, starting transfers between devices, local(): weight_parts = lax.all_to_all(weight_rows, 'row', 0, 0)  6 us
  transfers between devices with their start and end apart: 9, of which 6 were waited for; matrix products, arithmetic and copies ran while one was open for 0% of the time, Pallas kernels for 12%

profile of v7, /device:TPU:2, one launch (start us, length us, event | category | flops | bytes accessed | tf_op | source)
XLA Modules:
  0.0 177.8 jit_solution(14693476490583324231)
XLA Ops:
  0.7 1.0 copy-done.4
  1.6 0.1 spread.1
  1.7 1.0 copy-done.1
  2.7 11.8 %all-to-all-start = ((bf16[16,128,256]{2,1,0:T(8,128)(2,1)}), bf16[16,128,256]{2,1,0:T(8,128)(2,1)}, u32[]{:S(2)}, u32[]{:S(2)}) async-start(bf16[16,128,256]{2,1,0:T(8,128)(2,1)} %copy-done.1), calls=%async_computation | async-start | bytes 2097152 | tf_op jit(solution)/shard_map/all_to_all | solution.py:405
  15.2 12.8 %prepare.1 = (s32[128]{0:T(128)S(1)}, s32[384]{0:T(512)S(1)}, s32[96]{0:T(128)S(1)}, s32[1]{0:T(128)}, s32[97]{0:T(128)S(1)}, /*index=5*/s32[128]{0:T(128)S(1)},...) custom-call(s32[96]{0:T(128)S(1)} %bitcast.12, ...), custom_call_target="tpu_custom_call" | custom-call | bytes 28311552 | tf_op jit(solution)/shard_map/prepare/pallas_call | solution.py:124
  28.0 1.6 copy-done.2
  29.7 10.7 %all-to-all-done.refs_5_ = bf16[16,128,256]{2,1,0:T(8,128)(2,1)} async-done(((bf16[16,128,256]{2,1,0:T(8,128)(2,1)}), bf16[16,128,256]{2,1,0:T(8,128)(2,1)}, u32[]{:S(2)}, u32[]{:S(2)}) %all-to-all-start) | async-done | bytes 1048608 | tf_op jit(solution)/shard_map/all_to_all | solution.py:405
  40.4 2.7 %forward_tiles_1.1 = bf16[16,128,256]{2,1,0:T(8,128)(2,1)S(1)} custom-call(s32[128]{0:T(128)S(1)} %get-tuple-element.20.refs_0_, s32[384]{0:T(512)S(1)} %get-tuple-element.21.refs_1_, s32[96]{0:T(128)S(1)} %get-tuple-element.22.refs_2_, s32[1]{0:T(128)} %get-tuple-element.23.refs_3_, s32[97]{0:T(128)S(1)} %get-tuple-element.24.refs_4_, ...), custom_call_target="tpu_custom_call" | custom-call | flops 536870912 | bytes 1572864 | tf_op jit(solution)/shard_map/forward_tiles_1/pallas_call | solution.py:181
  43.1 1.9 %collective-permute-start = (bf16[16,128,256]{2,1,0:T(8,128)(2,1)S(1)}, bf16[16,128,256]{2,1,0:T(8,128)(2,1)S(1)}, u32[]{:S(2)}, u32[]{:S(2)}) collective-permute-start(bf16[16,128,256]{2,1,0:T(8,128)(2,1)S(1)} %forward_tiles_1.1), channel_id=1, source_target_pairs={{0,1},{1,0},{2,3},{3,2},{4,5},{5,4},{6,7},{7,6},{8,9},{9,8},{10,11... | collective-permute-start | bytes 3145736 | tf_op jit(solution)/shard_map/ppermute | solution.py:410
  45.0 2.7 %forward_tiles_0.1 = bf16[16,128,256]{2,1,0:T(8,128)(2,1)S(1)} custom-call(s32[128]{0:T(128)S(1)} %get-tuple-element.20.refs_0_, s32[384]{0:T(512)S(1)} %get-tuple-element.21.refs_1_, s32[96]{0:T(128)S(1)} %get-tuple-element.22.refs_2_, s32[1]{0:T(128)} %get-tuple-element.23.refs_3_, s32[97]{0:T(128)S(1)} %get-tuple-element.24.refs_4_, ...), custom_call_target="tpu_custom_call" | custom-call | flops 536870912 | bytes 1572864 | tf_op jit(solution)/shard_map/forward_tiles_0/pallas_call | solution.py:181
  47.7 0.0 copy-start.3
  47.7 0.0 copy-start.5
  47.7 0.0 collective-permute-done
  47.7 0.3 add_convert_fusion
  48.0 37.4 %all_to_all.25.parts_ref = bf16[16,128,256]{2,1,0:T(8,128)(2,1)S(1)} all-to-all(bf16[16,128,256]{2,1,0:T(8,128)(2,1)S(1)} %add_convert_fusion), channel_id=1, replica_groups={{0,4,8,12,16,20,24,28,2,6,10,14,18,22,26,30},{1,5,9,13,17,21,25,29,3,7,..., dimensions={0} | all-to-all | bytes 2097152 | tf_op jit(solution)/shard_map/all_to_all | solution.py:413
  85.4 0.9 dense.1
  86.4 37.3 %all_to_all.26.mine_ref.refs_5_ = bf16[16,144,256]{2,1,0:T(8,128)(2,1)S(1)} all-to-all(bf16[16,144,256]{2,1,0:T(8,128)(2,1)S(1)} %get-tuple-element.30), channel_id=1, replica_groups={{0,4,8,12,16,20,24,28,2,6,10,14,18,22,26,30},{1,5,9,13,17,21,25,29,3,7,..., dimensions={0} | all-to-all | bytes 2359296 | tf_op jit(solution)/shard_map/all_to_all | solution.py:416
  123.7 1.9 %collective-permute-start.1 = (bf16[16,144,256]{2,1,0:T(8,128)(2,1)S(1)}, bf16[16,144,256]{2,1,0:T(8,128)(2,1)S(1)}, u32[]{:S(2)}, u32[]{:S(2)}) collective-permute-start(bf16[16,144,256]{2,1,0:T(8,128)(2,1)S(1)} %all_to_all.26.mine_ref.refs_5_), channel_id=1, source_target_pairs={{0,1},{1,0},{2,3},{3,2},{4,5},{5,4},{6,7},{7,6},{8,9},{9,8},{10,11... | collective-permute-start | bytes 3538952 | tf_op jit(solution)/shard_map/ppermute | solution.py:417
  125.6 1.0 weight_part.1
  126.6 6.0 %all-to-all-start.4 = ((bf16[16,32,256]{2,1,0:T(8,128)(2,1)}), bf16[16,32,256]{2,1,0:T(8,128)(2,1)S(1)}, u32[]{:S(2)}, u32[]{:S(2)}) async-start(bf16[16,32,256]{2,1,0:T(8,128)(2,1)} %weight_part.1), calls=%async_computation.4 | async-start | bytes 524288 | tf_op jit(solution)/shard_map/all_to_all | solution.py:419
  132.6 5.4 %backward_tiles.1 = bf16[16,128,256]{2,1,0:T(8,128)(2,1)} custom-call(s32[128]{0:T(128)S(1)} %get-tuple-element.26.refs_0_, s32[384]{0:T(512)S(1)} %get-tuple-element.27.refs_1_, s32[96]{0:T(128)S(1)} %get-tuple-element.28.refs_2_, s32[1]{0:T(128)} %get-tuple-element.29.refs_3_, s32[97]{0:T(128)S(1)} %get-tuple-element.32.refs_4_, ...), custom_call_target="tpu_custom_call" | custom-call | flops 1073741824 | bytes 1589248 | tf_op jit(solution)/shard_map/backward_tiles/pallas_call | solution.py:356
  138.0 4.5 %all-to-all-done.4.parts_ref = bf16[16,32,256]{2,1,0:T(8,128)(2,1)S(1)} async-done(((bf16[16,32,256]{2,1,0:T(8,128)(2,1)}), bf16[16,32,256]{2,1,0:T(8,128)(2,1)S(1)}, u32[]{:S(2)}, u32[]{:S(2)}) %all-to-all-start.4) | async-done | bytes 262176 | tf_op jit(solution)/shard_map/all_to_all | solution.py:419
  142.5 5.4 %all-to-all-start.3 = ((bf16[16,128,256]{2,1,0:T(8,128)(2,1)}), bf16[16,128,256]{2,1,0:T(8,128)(2,1)S(1)}, u32[]{:S(2)}, u32[]{:S(2)}) async-start(bf16[16,128,256]{2,1,0:T(8,128)(2,1)} %backward_tiles.1), calls=%async_computation.3 | async-start | bytes 2097152 | tf_op jit(solution)/shard_map/all_to_all | solution.py:421
  147.9 1.9 %collective-permute-start.2 = (f32[32,256]{1,0:T(8,128)S(1)}, f32[32,256]{1,0:T(8,128)S(1)}, u32[]{:S(2)}, u32[]{:S(2)}) collective-permute-start(f32[32,256]{1,0:T(8,128)S(1)} %weight_sum.1), channel_id=1, source_target_pairs={{0,1},{1,0},{2,3},{3,2},{4,5},{5,4},{6,7},{7,6},{8,9},{9,8},{10,11... | collective-permute-start | bytes 98312 | tf_op jit(solution)/shard_map/ppermute | solution.py:304
  149.9 1.2 collective-permute-done.2
  151.0 3.3 %collective-permute-start.3 = (f32[1,32,256]{2,1,0:T(8,128)S(1)}, f32[1,32,256]{2,1,0:T(8,128)S(1)}, u32[]{:S(2)}, u32[]{:S(2)}) collective-permute-start(f32[1,32,256]{2,1,0:T(8,128)S(1)} %add_bitcast_fusion), channel_id=1, source_target_pairs={{0,4},{1,5},{2,6},{3,7},{4,0},{5,1},{6,2},{7,3},{8,12},{9,13},{10,... | collective-permute-start | bytes 98312 | tf_op jit(solution)/shard_map/ppermute | solution.py:307
  154.3 2.5 %collective-permute-done.3 = f32[1,32,256]{2,1,0:T(8,128)S(1)} collective-permute-done((f32[1,32,256]{2,1,0:T(8,128)S(1)}, f32[1,32,256]{2,1,0:T(8,128)S(1)}, u32[]{:S(2)}, u32[]{:S(2)}) %collective-permute-start.3) | collective-permute-done | bytes 32800 | tf_op jit(solution)/shard_map/ppermute | solution.py:307
  156.8 3.4 %collective-permute-start.4 = (f32[2,32,256]{2,1,0:T(8,128)S(1)}, f32[2,32,256]{2,1,0:T(8,128)S(1)}, u32[]{:S(2)}, u32[]{:S(2)}) collective-permute-start(f32[2,32,256]{2,1,0:T(8,128)S(1)} %maximum_select_fusion.1), channel_id=1, source_target_pairs={{0,8},{1,9},{2,10},{3,11},{4,12},{5,13},{6,14},{7,15},{8,0},{9,1},... | collective-permute-start | bytes 196616 | tf_op jit(solution)/shard_map/ppermute | solution.py:307
  160.3 3.6 %collective-permute-done.4 = f32[2,32,256]{2,1,0:T(8,128)S(1)} collective-permute-done((f32[2,32,256]{2,1,0:T(8,128)S(1)}, f32[2,32,256]{2,1,0:T(8,128)S(1)}, u32[]{:S(2)}, u32[]{:S(2)}) %collective-permute-start.4) | collective-permute-done | bytes 65568 | tf_op jit(solution)/shard_map/ppermute | solution.py:307
  163.9 3.6 %collective-permute-start.5 = (f32[4,32,256]{2,1,0:T(8,128)S(1)}, f32[4,32,256]{2,1,0:T(8,128)S(1)}, u32[]{:S(2)}, u32[]{:S(2)}) collective-permute-start(f32[4,32,256]{2,1,0:T(8,128)S(1)} %maximum_select_fusion.held_ref), channel_id=1, source_target_pairs={{0,16},{1,17},{2,18},{3,19},{4,20},{5,21},{6,22},{7,23},{8,24},{9,... | collective-permute-start | bytes 393224 | tf_op jit(solution)/shard_map/ppermute | solution.py:307
  167.6 9.3 %collective-permute-done.5.came_ref = f32[4,32,256]{2,1,0:T(8,128)S(1)} collective-permute-done((f32[4,32,256]{2,1,0:T(8,128)S(1)}, f32[4,32,256]{2,1,0:T(8,128)S(1)}, u32[]{:S(2)}, u32[]{:S(2)}) %collective-permute-start.5) | collective-permute-done | bytes 131104 | tf_op jit(solution)/shard_map/ppermute | solution.py:307
  176.9 0.9 finish.1
  (17 shorter events, 0.1 us)
Async XLA Ops:
  0.6 14.5 %copy-start = (bf16[1,1,96,128,128]{4,3,2,1,0:T(8,128)(2,1)S(1)}, bf16[1,1,96,128,128]{4,3,2,1,0:T(8,128)(2,1)}, u32[]{:S(2)}) copy-start(bf16[1,1,96,128,128]{4,3,2,1,0:T(8,128)(2,1)} %param.9) | copy-start | bytes 9437188
  0.6 1.0 copy-start.4
  1.6 13.5 %copy-start.6 = (s32[1,1,96]{2,1,0:T(1,128)S(1)}, s32[1,1,96]{2,1,0:T(1,128)}, u32[]{:S(2)}) copy-start(s32[1,1,96]{2,1,0:T(1,128)} %param.10) | copy-start | bytes 1156
  1.6 13.6 %copy-start.7 = (s32[1,1,96]{2,1,0:T(1,128)S(1)}, s32[1,1,96]{2,1,0:T(1,128)}, u32[]{:S(2)}) copy-start(s32[1,1,96]{2,1,0:T(1,128)} %param.11) | copy-start | bytes 1156
  1.7 1.0 copy-start.1
  2.7 37.7 %all-to-all-start = ((bf16[16,128,256]{2,1,0:T(8,128)(2,1)}), bf16[16,128,256]{2,1,0:T(8,128)(2,1)}, u32[]{:S(2)}, u32[]{:S(2)}) async-start(bf16[16,128,256]{2,1,0:T(8,128)(2,1)} %copy-done.1), calls=%async_computation | async-start | bytes 2097152 | tf_op jit(solution)/shard_map/all_to_all | solution.py:405
  28.0 1.6 copy-start.2
  43.1 4.6 %collective-permute-start = (bf16[16,128,256]{2,1,0:T(8,128)(2,1)S(1)}, bf16[16,128,256]{2,1,0:T(8,128)(2,1)S(1)}, u32[]{:S(2)}, u32[]{:S(2)}) collective-permute-start(bf16[16,128,256]{2,1,0:T(8,128)(2,1)S(1)} %forward_tiles_1.1), channel_id=1, source_target_pairs={{0,1},{1,0},{2,3},{3,2},{4,5},{5,4},{6,7},{7,6},{8,9},{9,8},{10,11... | collective-permute-start | bytes 3145736 | tf_op jit(solution)/shard_map/ppermute | solution.py:410
  47.7 37.8 %copy-start.3 = (bf16[256,256]{1,0:T(8,128)(2,1)S(1)}, bf16[256,256]{1,0:T(8,128)(2,1)}, u32[]{:S(2)}) copy-start(bf16[256,256]{1,0:T(8,128)(2,1)} %weight_ref.3) | copy-start | bytes 393220
  47.7 37.8 %copy-start.5 = (bf16[128,256]{1,0:T(8,128)(2,1)S(1)}, bf16[128,256]{1,0:T(8,128)(2,1)}, u32[]{:S(2)}) copy-start(bf16[128,256]{1,0:T(8,128)(2,1)} %cotangent_ref.1) | copy-start | bytes 196612
  123.7 8.9 %collective-permute-start.1 = (bf16[16,144,256]{2,1,0:T(8,128)(2,1)S(1)}, bf16[16,144,256]{2,1,0:T(8,128)(2,1)S(1)}, u32[]{:S(2)}, u32[]{:S(2)}) collective-permute-start(bf16[16,144,256]{2,1,0:T(8,128)(2,1)S(1)} %all_to_all.26.mine_ref.refs_5_), channel_id=1, source_target_pairs={{0,1},{1,0},{2,3},{3,2},{4,5},{5,4},{6,7},{7,6},{8,9},{9,8},{10,11... | collective-permute-start | bytes 3538952 | tf_op jit(solution)/shard_map/ppermute | solution.py:417
  126.6 15.9 %all-to-all-start.4 = ((bf16[16,32,256]{2,1,0:T(8,128)(2,1)}), bf16[16,32,256]{2,1,0:T(8,128)(2,1)S(1)}, u32[]{:S(2)}, u32[]{:S(2)}) async-start(bf16[16,32,256]{2,1,0:T(8,128)(2,1)} %weight_part.1), calls=%async_computation.4 | async-start | bytes 524288 | tf_op jit(solution)/shard_map/all_to_all | solution.py:419
  142.5 34.4 %all-to-all-start.3 = ((bf16[16,128,256]{2,1,0:T(8,128)(2,1)}), bf16[16,128,256]{2,1,0:T(8,128)(2,1)S(1)}, u32[]{:S(2)}, u32[]{:S(2)}) async-start(bf16[16,128,256]{2,1,0:T(8,128)(2,1)} %backward_tiles.1), calls=%async_computation.3 | async-start | bytes 2097152 | tf_op jit(solution)/shard_map/all_to_all | solution.py:421
  147.9 3.1 %collective-permute-start.2 = (f32[32,256]{1,0:T(8,128)S(1)}, f32[32,256]{1,0:T(8,128)S(1)}, u32[]{:S(2)}, u32[]{:S(2)}) collective-permute-start(f32[32,256]{1,0:T(8,128)S(1)} %weight_sum.1), channel_id=1, source_target_pairs={{0,1},{1,0},{2,3},{3,2},{4,5},{5,4},{6,7},{7,6},{8,9},{9,8},{10,11... | collective-permute-start | bytes 98312 | tf_op jit(solution)/shard_map/ppermute | solution.py:304
  151.0 5.8 %collective-permute-start.3 = (f32[1,32,256]{2,1,0:T(8,128)S(1)}, f32[1,32,256]{2,1,0:T(8,128)S(1)}, u32[]{:S(2)}, u32[]{:S(2)}) collective-permute-start(f32[1,32,256]{2,1,0:T(8,128)S(1)} %add_bitcast_fusion), channel_id=1, source_target_pairs={{0,4},{1,5},{2,6},{3,7},{4,0},{5,1},{6,2},{7,3},{8,12},{9,13},{10,... | collective-permute-start | bytes 98312 | tf_op jit(solution)/shard_map/ppermute | solution.py:307
  156.8 7.1 %collective-permute-start.4 = (f32[2,32,256]{2,1,0:T(8,128)S(1)}, f32[2,32,256]{2,1,0:T(8,128)S(1)}, u32[]{:S(2)}, u32[]{:S(2)}) collective-permute-start(f32[2,32,256]{2,1,0:T(8,128)S(1)} %maximum_select_fusion.1), channel_id=1, source_target_pairs={{0,8},{1,9},{2,10},{3,11},{4,12},{5,13},{6,14},{7,15},{8,0},{9,1},... | collective-permute-start | bytes 196616 | tf_op jit(solution)/shard_map/ppermute | solution.py:307
  163.9 13.0 %collective-permute-start.5 = (f32[4,32,256]{2,1,0:T(8,128)S(1)}, f32[4,32,256]{2,1,0:T(8,128)S(1)}, u32[]{:S(2)}, u32[]{:S(2)}) collective-permute-start(f32[4,32,256]{2,1,0:T(8,128)S(1)} %maximum_select_fusion.held_ref), channel_id=1, source_target_pairs={{0,16},{1,17},{2,18},{3,19},{4,20},{5,21},{6,22},{7,23},{8,24},{9,... | collective-permute-start | bytes 393224 | tf_op jit(solution)/shard_map/ppermute | solution.py:307
